TPU v7x, 32 devices: a whole 2x2x4 slice. The times are simulated.
32 devices in a mesh: dp: 8 (over y, x, core), mp: 4 (over z).
Axes of the slice: x: 2, y: 2, z: 4, core: 2. Of those that a mesh axis runs over, the one named last changes fastest.
Arguments:
- token_ids: int32 [256, 128], P('dp'), may hold values from 0 to 30591
- replacements: int32 [256, 128], P('dp'), may hold values from 0 to 30591
- replaced: int32 [256, 128], P('dp'), may hold values 0 or 1
- lengths: int32 [256], P('dp'), may hold values from 32 to 128, as said below
- widths: int32 [256], P('dp'), may hold values from 1 to 4
- teacher_embed: bfloat16 [256, 128, 768], P(('dp', 'mp')), may hold values from -6 to 6
- teacher_hidden: bfloat16 [256, 128, 768], P(('dp', 'mp')), may hold values from -6 to 6
- teacher_logits: float32 [256, 3], P(('dp', 'mp')), may hold values from -6 to 6
- embed_table: float32 [30592, 768], P(('dp', 'mp')), may hold values from -0.3125 to 0.3125
- embed_moment: float32 [30592, 768], P(('dp', 'mp')), may hold values from -0.00061035156 to 0.00061035156
- embed_square: float32 [30592, 768], P(('dp', 'mp')), may hold values from 1e-09 to 4e-09
- dense_weights: float32 [3840, 768], P(('dp', 'mp'))
- dense_moment: float32 [3840, 768], P(('dp', 'mp')), may hold values from -0.00030517578 to 0.00030517578
- dense_square: float32 [3840, 768], P(('dp', 'mp')), may hold values from 2.6e-10 to 1.04e-09
- feedforward: float32 [3072, 1536], P(('dp', 'mp')), may hold values from -0.15625 to 0.15625
- feedforward_moment: float32 [3072, 1536], P(('dp', 'mp')), may hold values from -0.00012207031 to 0.00012207031
- feedforward_square: float32 [3072, 1536], P(('dp', 'mp')), may hold values from 3.2e-11 to 1.3e-10
- classifier: float32 [768, 3], replicated, may hold values from -0.21875 to 0.21875
- classifier_moment: float32 [768, 3], replicated, may hold values from -0.00012207031 to 0.00012207031
- classifier_square: float32 [768, 3], replicated, may hold values from 3.2e-11 to 1.3e-10
- norm_gains: float32 [6, 768], replicated
- norm_moment: float32 [6, 768], replicated, may hold values from -0.0068359375 to 0.0068359375
- norm_square: float32 [6, 768], replicated, may hold values from 1.2e-07 to 4.8e-07
Outputs:
- loss_sum: float32 [], replicated
- token_count: float32 [], replicated
- grad_norm: float32 [], replicated
- new_embed_table: float32 [30592, 768], P(('dp', 'mp'))
- new_embed_moment: float32 [30592, 768], P(('dp', 'mp'))
- new_embed_square: float32 [30592, 768], P(('dp', 'mp'))
- embed_copy: bfloat16 [30592, 768], P(('dp', 'mp'))
- new_dense_weights: float32 [3840, 768], P(('dp', 'mp'))
- new_dense_moment: float32 [3840, 768], P(('dp', 'mp'))
- new_dense_square: float32 [3840, 768], P(('dp', 'mp'))
- dense_copy: bfloat16 [3840, 768], P(('dp', 'mp'))
- new_feedforward: float32 [3072, 1536], P(('dp', 'mp'))
- new_feedforward_moment: float32 [3072, 1536], P(('dp', 'mp'))
- new_feedforward_square: float32 [3072, 1536], P(('dp', 'mp'))
- feedforward_copy: bfloat16 [3072, 1536], P(('dp', 'mp'))
- new_classifier: float32 [768, 3], replicated
- new_classifier_moment: float32 [768, 3], replicated
- new_classifier_square: float32 [768, 3], replicated
- classifier_copy: bfloat16 [768, 3], replicated
- new_norm_gains: float32 [6, 768], replicated
- new_norm_moment: float32 [6, 768], replicated
- new_norm_square: float32 [6, 768], replicated
Inputs may be any that keep to these rules, and one draw needn't show every extreme that they name: `lengths`: in every draw some sequence has length 128.
All inputs are finite; a program needn't handle non-finite values. No bound on the sum of `replaced` on one device may be relied on, other than what follows from the above.
Results may differ from a plain program's by a relative error of at most 0.017.
Values may be sent and summed in bfloat16 or wider, within the bound.
No kernel may reach another device: no remote copies, remote signals or barrier semaphores. Data moves between devices by JAX's collectives and lax.ppermute only.
A program may use at most 256 MiB of HBM per device.

v0:
```python
import jax
import jax.numpy as jnp
from jax import lax
from jax.sharding import PartitionSpec as P

MODEL_WIDTH = 768
HEADS = 12
FF = 3072
L = 128
LEVELS = 4
STEP = 10


highest_precision = lax.Precision.HIGHEST
norm_epsilon = 1e-05
learn_rate = 0.05
gain_rate = 0.5
beta_one = 0.9
beta_two = 0.999
adam_epsilon = 1e-08
weight_decay = 0.01
clip_bound = 1.0


def layer_norm(values, gain_row, shift_row):
    center = values - jnp.mean(values, axis=-1, keepdims=True)
    spread = jnp.mean(center * center, axis=-1, keepdims=True)
    return center * lax.rsqrt(spread + norm_epsilon) * gain_row + shift_row


def adam_update(weight, gradient, first_moment, second, decay_rate, rate):
    first_new = beta_one * first_moment + (1.0 - beta_one) * gradient
    second_new = beta_two * second + (1.0 - beta_two) * gradient * gradient
    direction = (
        first_new
        / (1.0 - beta_one**STEP)
        / (jnp.sqrt(second_new / (1.0 - beta_two**STEP)) + adam_epsilon)
    )
    return (weight - rate * (direction + decay_rate * weight), first_new, second_new)


def contract_last(left, right):
    return lax.dot_general(
        left, right, (((1,), (1,)), ((), ())), preferred_element_type=jnp.float32
    )


def contract_first(left, right):
    return lax.dot_general(
        left, right, (((0,), (0,)), ((), ())), preferred_element_type=jnp.float32
    )


def split_heads(output_projection):
    sequences = output_projection.shape[0] // L
    pieces = output_projection.reshape(sequences, L, 3, HEADS, MODEL_WIDTH // HEADS)
    return (pieces[:, :, 0], pieces[:, :, 1], pieces[:, :, 2])


def attention_forward(output_projection, usable, head_on):
    queries, keying, values = split_heads(output_projection)
    scores = jnp.einsum("sqhc,skhc->shqk", queries, keying, preferred_element_type=jnp.float32) * (
        MODEL_WIDTH // HEADS
    ) ** (-0.5)
    scores = scores + jnp.where(usable[:, None, None, :] > 0, 0.0, -1000000000.0)
    attend = jax.nn.softmax(scores, axis=-1)
    head_mixture = jnp.einsum(
        "shqk,skhc->sqhc", attend.astype(jnp.bfloat16), values, preferred_element_type=jnp.float32
    )
    head_mixture = (head_mixture * head_on[:, None, :, None]).astype(jnp.bfloat16)
    return (attend, head_mixture.reshape(output_projection.shape[0], MODEL_WIDTH))


def attention_backward(output_projection, attend, grad_mixture):
    queries, keying, values = split_heads(output_projection)
    attend_low = attend.astype(jnp.bfloat16)
    grad_values = jnp.einsum(
        "shqk,sqhc->skhc", attend_low, grad_mixture, preferred_element_type=jnp.float32
    )
    grad_attend = jnp.einsum(
        "sqhc,skhc->shqk", grad_mixture, values, preferred_element_type=jnp.float32
    )
    grad_scores = attend * (grad_attend - jnp.sum(grad_attend * attend, axis=-1, keepdims=True))
    grad_scores = grad_scores.astype(jnp.bfloat16)
    scaling = (MODEL_WIDTH // HEADS) ** (-0.5)
    grad_queries = (
        jnp.einsum("shqk,skhc->sqhc", grad_scores, keying, preferred_element_type=jnp.float32)
        * scaling
    )
    grad_keying = (
        jnp.einsum("shqk,sqhc->skhc", grad_scores, queries, preferred_element_type=jnp.float32)
        * scaling
    )
    stacked = jnp.stack([grad_queries, grad_keying, grad_values], axis=2)
    return stacked.reshape(output_projection.shape[0], 3 * MODEL_WIDTH).astype(jnp.bfloat16)


def per_device(
    token_ids,
    replacements,
    replaced,
    lengths,
    widths,
    teacher_embed,
    teacher_hidden,
    teacher_logits,
    embed_table,
    embed_moment,
    embed_square,
    dense_weights,
    dense_moment,
    dense_square,
    feedforward,
    feedforward_moment,
    feedforward_square,
    classifier,
    classifier_moment,
    classifier_square,
    norm_gains,
    norm_moment,
    norm_square,
):
    mp_count = lax.axis_size("mp")
    mp_index = lax.axis_index("mp")
    own_seqs = teacher_logits.shape[0]
    own_rows = own_seqs * L
    table_low = embed_table.astype(jnp.bfloat16)
    dense_narrow_part = dense_weights.astype(jnp.bfloat16)
    feedforward_narrow = feedforward.astype(jnp.bfloat16)
    table_block, ffn_local = (
        lax.all_gather(table_low, "dp", axis=0, tiled=True),
        lax.all_gather(feedforward_narrow, "dp", axis=0, tiled=True),
    )
    dense_full = lax.all_gather(dense_narrow_part, ("dp", "mp"), axis=0, tiled=True)
    neuron_piece = feedforward.shape[0]
    neuron_slot = jnp.arange(ffn_local.shape[0])
    neuron_index = (
        neuron_slot // neuron_piece * mp_count + mp_index
    ) * neuron_piece + neuron_slot % neuron_piece
    block_rows = table_block.shape[0]
    piece_rows = embed_table.shape[0]
    chosen = jnp.where(replaced == 1, replacements, token_ids).reshape(-1)
    block_number = chosen // piece_rows
    inside = block_number % mp_count == mp_index
    clipped = block_number // mp_count * piece_rows + chosen % piece_rows
    picked = jnp.where(inside[:, None], table_block[clipped], jnp.zeros((), jnp.bfloat16))
    embedded = lax.psum_scatter(picked, "mp", scatter_dimension=0, tiled=True).astype(jnp.float32)
    own_start = mp_index * own_seqs
    own_lengths = lax.dynamic_slice_in_dim(lengths, own_start, own_seqs)
    own_levels = lax.dynamic_slice_in_dim(widths, own_start, own_seqs)
    usable_grid = (jnp.arange(L)[None, :] < own_lengths[:, None]).astype(jnp.float32)
    usable = usable_grid.reshape(own_rows, 1)
    head_on = (jnp.arange(HEADS)[None, :] < own_levels[:, None] * HEADS // LEVELS).astype(
        jnp.float32
    )
    normalized_rows, normed_pull = jax.vjp(layer_norm, embedded, norm_gains[0], norm_gains[1])
    normed_low = normalized_rows.astype(jnp.bfloat16)
    qkv_rows = dense_full[: 3 * MODEL_WIDTH]
    output_projection = contract_last(normed_low, qkv_rows).astype(jnp.bfloat16)
    attend, head_mixture = attention_forward(output_projection, usable_grid, head_on)
    out_rows = dense_full[3 * MODEL_WIDTH : 4 * MODEL_WIDTH]
    attention_result = jnp.dot(head_mixture, out_rows, preferred_element_type=jnp.float32)
    middle_activation, middle_pull = jax.vjp(
        layer_norm, normalized_rows + attention_result, norm_gains[2], norm_gains[3]
    )
    middle_low = middle_activation.astype(jnp.bfloat16)
    up_rows = ffn_local[:, :MODEL_WIDTH]
    down_rows = ffn_local[:, MODEL_WIDTH:]
    ffn_rows_in = lax.all_gather(middle_low, "mp", axis=0, tiled=True)
    row_levels = jnp.repeat(widths, L, total_repeat_length=own_rows * mp_count)
    residual_before = contract_last(ffn_rows_in, up_rows)
    neuron_on = (neuron_index[None, :] < row_levels[:, None] * FF // LEVELS).astype(jnp.float32)
    activated, gelu_pull = jax.vjp(jax.nn.gelu, residual_before)
    hidden_low = (activated * neuron_on).astype(jnp.bfloat16)
    rows_in = lax.slice_in_dim(hidden_low, 0, lax.axis_size("mp") * own_rows, axis=0)
    feedforward_result = lax.psum_scatter(
        jnp.dot(rows_in, down_rows, preferred_element_type=jnp.float32).astype(jnp.bfloat16),
        "mp",
        scatter_dimension=0,
        tiled=True,
    ).astype(jnp.float32)
    output, output_pull = jax.vjp(
        layer_norm, middle_activation + feedforward_result, norm_gains[4], norm_gains[5]
    )
    embed_diff = normalized_rows - teacher_embed.reshape(own_rows, MODEL_WIDTH).astype(jnp.float32)
    hidden_diff = output - teacher_hidden.reshape(own_rows, MODEL_WIDTH).astype(jnp.float32)
    first_low = output.reshape(own_seqs, L, MODEL_WIDTH)[:, 0].astype(jnp.bfloat16)
    pool_rows = dense_full[4 * MODEL_WIDTH :]
    pooled = jnp.tanh(jnp.dot(first_low, pool_rows, preferred_element_type=jnp.float32))
    pooled_low = pooled.astype(jnp.bfloat16)
    class_low = classifier.astype(jnp.bfloat16)
    logits = jnp.dot(pooled_low, class_low, preferred_element_type=jnp.float32)
    logit_diff = logits - teacher_logits
    loss_own = jnp.sum(usable * embed_diff * embed_diff) + jnp.sum(
        usable * hidden_diff * hidden_diff
    )
    loss_own = loss_own + L * jnp.sum(logit_diff * logit_diff)
    grad_logits = 2.0 * L * logit_diff
    pooled_wide = pooled_low.astype(jnp.float32)
    first_wide = first_low.astype(jnp.float32)
    grad_class = jnp.dot(pooled_wide.T, grad_logits, precision=highest_precision)
    grad_pooled = jnp.dot(grad_logits, class_low.astype(jnp.float32).T, precision=highest_precision)
    grad_inner = grad_pooled * (1.0 - pooled * pooled)
    grad_pool_rows = jnp.dot(first_wide.T, grad_inner, precision=highest_precision)
    grad_first = jnp.dot(grad_inner, pool_rows.astype(jnp.float32).T, precision=highest_precision)
    grad_output = (2.0 * usable * hidden_diff).reshape(own_seqs, L, MODEL_WIDTH)
    grad_output = grad_output.at[:, 0].add(grad_first).reshape(own_rows, MODEL_WIDTH)
    grad_second, gain_two, shift_two = output_pull(grad_output)
    grad_feed_low = grad_second.astype(jnp.bfloat16)
    grad_feed_rows = lax.all_gather(grad_feed_low, "mp", axis=0, tiled=True)
    grad_down = contract_first(hidden_low, grad_feed_rows)
    grad_hidden = contract_last(grad_feed_rows, down_rows)
    grad_before = gelu_pull(grad_hidden * neuron_on)[0].astype(jnp.bfloat16)
    grad_up = contract_first(grad_before, ffn_rows_in)
    rows_in = grad_before
    grad_middle_ffn = lax.psum_scatter(
        jnp.dot(rows_in, up_rows, preferred_element_type=jnp.float32),
        "mp",
        scatter_dimension=0,
        tiled=True,
    )
    grad_first_sum, gain_one, shift_one = middle_pull(grad_second + grad_middle_ffn)
    grad_att_low = grad_first_sum.astype(jnp.bfloat16)
    grad_out_rows = contract_first(head_mixture, grad_att_low)
    grad_mixture = contract_last(grad_att_low, out_rows).astype(jnp.bfloat16)
    grad_mixture = grad_mixture.reshape(own_seqs, L, HEADS, MODEL_WIDTH // HEADS) * head_on[
        :, None, :, None
    ].astype(jnp.bfloat16)
    grad_project = attention_backward(output_projection, attend, grad_mixture)
    grad_qkv_rows = contract_first(grad_project, normed_low)
    grad_normed = (
        grad_first_sum
        + 2.0 * usable * embed_diff
        + jnp.dot(grad_project, qkv_rows, preferred_element_type=jnp.float32)
    )
    grad_embedded, gain_base, shift_base = normed_pull(grad_normed)
    grad_embed_rows = lax.all_gather(grad_embedded.astype(jnp.bfloat16), "mp", axis=0, tiled=True)
    grad_table = jax.ops.segment_sum(
        jnp.where(inside[:, None], grad_embed_rows.astype(jnp.float32), 0.0),
        clipped,
        num_segments=block_rows,
    )
    grad_dense = jnp.concatenate([grad_qkv_rows, grad_out_rows, grad_pool_rows], axis=0)
    grad_ffn = jnp.concatenate([grad_up, grad_down], axis=1)
    dense_grad = lax.psum_scatter(grad_dense, ("dp", "mp"), scatter_dimension=0, tiled=True)
    table_grad, ffn_grad = (
        lax.psum_scatter(
            grad_table.astype(jnp.bfloat16), "dp", scatter_dimension=0, tiled=True
        ).astype(jnp.float32),
        lax.psum_scatter(
            grad_ffn.astype(jnp.bfloat16), "dp", scatter_dimension=0, tiled=True
        ).astype(jnp.float32),
    )
    grad_gains = jnp.stack(
        [gain_base, shift_base, gain_one, shift_one, gain_two, shift_two], axis=0
    )
    gains_grad, class_grad = lax.psum((grad_gains, grad_class), ("dp", "mp"))
    square_sum = (
        jnp.sum(table_grad * table_grad)
        + jnp.sum(dense_grad * dense_grad)
        + jnp.sum(ffn_grad * ffn_grad)
    )
    own_count = jnp.sum(own_lengths).astype(jnp.float32)
    total_square, token_count, loss_sum = lax.psum((square_sum, own_count, loss_own), ("dp", "mp"))
    small_square = jnp.sum(gains_grad * gains_grad) + jnp.sum(class_grad * class_grad)
    inverse = 1.0 / token_count
    grad_norm = jnp.sqrt(total_square + small_square) * inverse
    scaling = inverse * (clip_bound / jnp.maximum(grad_norm, clip_bound))
    table_new = adam_update(
        embed_table, table_grad * scaling, embed_moment, embed_square, weight_decay, learn_rate
    )
    dense_new = adam_update(
        dense_weights, dense_grad * scaling, dense_moment, dense_square, weight_decay, learn_rate
    )
    ffn_new = adam_update(
        feedforward,
        ffn_grad * scaling,
        feedforward_moment,
        feedforward_square,
        weight_decay,
        learn_rate,
    )
    class_new = adam_update(
        classifier,
        class_grad * scaling,
        classifier_moment,
        classifier_square,
        weight_decay,
        learn_rate,
    )
    gains_new = adam_update(
        norm_gains, gains_grad * scaling, norm_moment, norm_square, 0.0, gain_rate
    )
    return (
        loss_sum,
        token_count,
        grad_norm,
        table_new[0],
        table_new[1],
        table_new[2],
        table_new[0].astype(jnp.bfloat16),
        dense_new[0],
        dense_new[1],
        dense_new[2],
        dense_new[0].astype(jnp.bfloat16),
        ffn_new[0],
        ffn_new[1],
        ffn_new[2],
        ffn_new[0].astype(jnp.bfloat16),
        class_new[0],
        class_new[1],
        class_new[2],
        class_new[0].astype(jnp.bfloat16),
        gains_new[0],
        gains_new[1],
        gains_new[2],
    )


def solution(mesh):
    placed = (
        P("dp", None),
        P("dp", None),
        P("dp", None),
        P("dp"),
        P("dp"),
        P(("dp", "mp"), None, None),
        P(("dp", "mp"), None, None),
        P(("dp", "mp"), None),
        P(("dp", "mp"), None),
        P(("dp", "mp"), None),
        P(("dp", "mp"), None),
        P(("dp", "mp"), None),
        P(("dp", "mp"), None),
        P(("dp", "mp"), None),
        P(("dp", "mp"), None),
        P(("dp", "mp"), None),
        P(("dp", "mp"), None),
        P(),
        P(),
        P(),
        P(),
        P(),
        P(),
    )
    return jax.shard_map(
        per_device,
        mesh=mesh,
        in_specs=placed,
        out_specs=(
            P(),
            P(),
            P(),
            P(("dp", "mp"), None),
            P(("dp", "mp"), None),
            P(("dp", "mp"), None),
            P(("dp", "mp"), None),
            P(("dp", "mp"), None),
            P(("dp", "mp"), None),
            P(("dp", "mp"), None),
            P(("dp", "mp"), None),
            P(("dp", "mp"), None),
            P(("dp", "mp"), None),
            P(("dp", "mp"), None),
            P(("dp", "mp"), None),
            P(),
            P(),
            P(),
            P(),
            P(),
            P(),
            P(),
        ),
        check_vma=False,
    )
```

profile of v0, /device:TPU:0, one launch (start us, length us, event | category | flops | bytes accessed | tf_op | source)
XLA Modules:
  0.0 1376.7 jit_solution(11154116893890545619)
XLA Ops:
  12.1 70.7 %all-gather.18.cloned.1.call-done = bf16[8,956,768]{2,1,0:T(8,128)(2,1)} async-done(((bf16[1,956,768]{2,1,0:T(8,128)(2,1)}), bf16[8,956,768]{2,1,0:T(8,128)(2,1)}) %all-gather.18.cloned.1.call-update) | async-done | bytes 11747344 | tf_op jit(solution)/shard_map/all_gather | solution.py:131
  82.9 9.5 reshape.769
  92.4 24.9 %gather_fusion = bf16[4096,768]{1,0:T(8,128)(2,1)} fusion(bf16[7648,768]{1,0:T(8,128)(2,1)} %reshape.769, s32[4096]{0:T(1024)S(1)} %broadcast_clamp_fusion), kind=kCustom, calls=%fused_computation | custom fusion | bytes 12599296 | tf_op jit(solution)/shard_map/gather | solution.py:146
  117.3 7.4 broadcast_select_fusion
  128.5 110.2 %reduce-scatter.10.cloned.1.call-done = bf16[1024,768]{1,0:T(8,128)(2,1)} async-done(((bf16[4096,768]{1,0:T(8,128)(2,1)}), bf16[1024,768]{1,0:T(8,128)(2,1)}) %reduce-scatter.10.cloned.1.call-update) | async-done | bytes 1572880 | tf_op jit(solution)/shard_map/reduce_scatter | solution.py:147
  242.5 44.3 %all-gather.8.cloned.1.call-done = bf16[3840,768]{1,0:T(8,128)(2,1)} async-done(((bf16[120,768]{1,0:T(8,128)(2,1)}), bf16[3840,768]{1,0:T(8,128)(2,1)}) %all-gather.8.cloned.1.call-update) | async-done | bytes 5898256 | tf_op jit(solution)/shard_map/all_gather | solution.py:134
  286.8 7.8 convolution_convert_fusion.1
  294.7 6.7 copy.88
  322.2 4.6 compare_select_fusion.4
  328.1 15.6 %add_select_fusion = s32[4096]{0:T(1024)S(1)} fusion(pred[4096]{0:T(1024)(128)(4,1)S(1)} %get-tuple-element.152, pred[4096]{0:T(1024)(128)(4,1)S(1)} %get-tuple-element.151, pred[4096]{0:T(1024)(128)(4,1)S(1)} %get-tuple-element.150, pred[4096]{0:T(1024)(128)(4,1)S(1)} %get-tuple-element.149, pred[4096]{0:T(1024)(128)(4,1)S(1)} %get-tuple-element.148, ...), kind=kLoop, calls=%fused_computation.194 | loop fusion | flops 204800 | bytes 135268 | tf_op jit(solution)/shard_map/jit(floor_divide)/jit(_where)/select_n | solution.py:172
  343.7 90.7 %all-gather.10.cloned.1.call-done = bf16[4096,768]{1,0:T(8,128)(2,1)} async-done(((bf16[1024,768]{1,0:T(8,128)(2,1)}), bf16[4096,768]{1,0:T(8,128)(2,1)}) %all-gather.10.cloned.1.call-update) | async-done | bytes 6291472 | tf_op jit(solution)/shard_map/all_gather | solution.py:169
  434.4 12.8 fusion.2
  449.9 7.0 convolution_convert_fusion
  457.4 108.5 %reduce-scatter.12.cloned.1.call-done = bf16[1024,768]{1,0:T(8,128)(2,1)} async-done(((bf16[4096,768]{1,0:T(8,128)(2,1)}), bf16[1024,768]{1,0:T(8,128)(2,1)}) %reduce-scatter.12.cloned.1.call-update) | async-done | bytes 1572880 | tf_op jit(solution)/shard_map/reduce_scatter | solution.py:176
  579.7 4.7 fusion.39
  589.1 116.0 %all-gather.14.cloned.1.call-done = bf16[4096,768]{1,0:T(8,128)(2,1)} async-done(((bf16[1024,768]{1,0:T(8,128)(2,1)}), bf16[4096,768]{1,0:T(8,128)(2,1)}) %all-gather.14.cloned.1.call-update) | async-done | bytes 6291472 | tf_op jit(solution)/shard_map/all_gather | solution.py:210
  705.0 14.4 %fusion.9 = bf16[4096,768]{1,0:T(8,128)(2,1)S(1)} fusion(f32[4096,768]{1,0:T(8,128)} %get-tuple-element.243, s32[768]{0:T(1024)S(1)} %fusion.112, s32[4096]{0:T(1024)S(1)} %add_select_fusion, bf16[4096,768]{1,0:T(8,128)(2,1)} %all-gather.14.cloned.1.call-done, bf16[768,1536]{1,0:T(8,128)(2,1)S(1)} %copy-done.63), kind=kOutput, calls=%fused_computation.14 | convolution fusion | flops 4901044224 | bytes 26365952 | tf_op jit(solution)/shard_map/dot_general | solution.py:43
  722.1 8.0 fusion.77
  730.4 9.2 convolution_convert_fusion.4
  739.7 5.4 convolution_convert_fusion.5
  751.4 188.8 %reduce-scatter.14.cloned.1.call-done = f32[1024,768]{1,0:T(8,128)} async-done(((f32[4096,768]{1,0:T(8,128)}), f32[1024,768]{1,0:T(8,128)}) %reduce-scatter.14.cloned.1.call-update) | async-done | bytes 3145744 | tf_op jit(solution)/shard_map/reduce_scatter | solution.py:216
  951.3 7.0 fusion.60
  966.5 9.3 copy.104
  976.0 6.7 fusion.34
  995.0 5.0 pad_maximum_fusion
  1009.0 104.1 %all-gather.16.cloned.1.call-done = bf16[4096,768]{1,0:T(8,128)(2,1)} async-done(((bf16[1024,768]{1,0:T(8,128)(2,1)}), bf16[4096,768]{1,0:T(8,128)(2,1)}) %all-gather.16.cloned.1.call-update) | async-done | bytes 6291472 | tf_op jit(solution)/shard_map/all_gather | solution.py:237
  1113.1 39.6 %scatter_custom_fusion = f32[7648,768]{1,0:T(8,128)} fusion(s32[4096]{0:T(1024)} %bitcast.203, bf16[4096,768]{1,0:T(8,128)(2,1)} %all-gather.16.cloned.1.call-done, f32[]{:T(128)} %constant.281.clone.1, pred[4096]{0:T(1024)(128)(4,1)S(1)} %copy-done.40), kind=kCustom, calls=%fused_computation.15 | custom fusion | flops 9437184 | bytes 29791232 | tf_op jit(solution)/shard_map/scatter-add | solution.py:238
  1152.7 12.5 convert_element_type.187
  1165.2 122.2 %fusion = bf16[960,768]{1,0:T(8,128)(2,1)S(1)} fusion(bf16[7648,768]{1,0:T(8,128)(2,1)} %convert_element_type.187), kind=kCustom, calls=%all-reduce-scatter | all-reduce-scatter fusion | flops 5898241 | bytes 13222400
  1290.9 7.0 concatenate.15
  1305.2 39.8 %all-reduce.2 = (f32[]{:T(128)}, f32[]{:T(128)}, f32[]{:T(128)}, f32[6,768]{1,0:T(8,128)S(1)}, f32[768,3]{0,1:T(4,128)S(1)}) all-reduce(f32[]{:T(128)S(6)} %add.424, f32[]{:T(128)S(6)} %convert_element_type.177, f32[]{:T(128)S(6)} %add.430, f32[6,768]{1,0:T(8,128)S(1)} %stack.29, ...), channel_id=1, replica_groups=mesh['dp'=8,'mp'=4] {'dp','mp'}, use_global_device_ids=true, to_apply=%region_13.14 | all-reduce | flops 6915 | bytes 55320 | tf_op jit(solution)/shard_map/psum | solution.py:264
  1359.8 7.1 fusion.139
  (284 shorter events, 123.2 us)
Async XLA Ops:
  8.1 74.8 %all-gather.18.cloned.1.call-start = ((), (), s32[]{:S(2)}) async-start(), calls=%async_computation.14 | async-start | bytes 13271040 | tf_op jit(solution)/shard_map/all_gather | solution.py:131
  11.2 227.4 %reduce-scatter.10.cloned.1.call-start = ((), (), s32[]{:S(2)}) async-start(), calls=%async_computation.5 | async-start | bytes 7864320 | tf_op jit(solution)/shard_map/reduce_scatter | solution.py:147
  11.3 106.0 %copy-start.39 = (pred[4096]{0:T(1024)(128)(4,1)}, pred[4096]{0:T(1024)(128)(4,1)S(1)}, u32[]{:S(2)}) copy-start(pred[4096]{0:T(1024)(128)(4,1)S(1)} %get-tuple-element.190) | copy-start | bytes 12292
  124.8 162.0 %all-gather.8.cloned.1.call-start = ((), (), s32[]{:S(2)}) async-start(), calls=%async_computation.6 | async-start | bytes 6082560 | tf_op jit(solution)/shard_map/all_gather | solution.py:134
  126.5 217.2 %all-gather.12.cloned.1.call-start = ((), (), s32[]{:S(2)}) async-start(), calls=%async_computation.8 | async-start | bytes 2654208 | tf_op jit(solution)/shard_map/all_gather | solution.py:132
  127.3 307.1 %all-gather.10.cloned.1.call-start = ((), (), s32[]{:S(2)}) async-start(), calls=%async_computation.7 | async-start | bytes 7864320 | tf_op jit(solution)/shard_map/all_gather | solution.py:169
  128.5 184.9 %copy-start.49 = (f32[768]{0:T(1024)}, f32[768]{0:T(1024)S(1)}, u32[]{:S(2)}) copy-start(f32[768]{0:T(1024)S(1)} %get-tuple-element.126) | copy-start | bytes 9220
  128.5 184.9 %copy-start.57 = (f32[768]{0:T(1024)}, f32[768]{0:T(1024)S(1)}, u32[]{:S(2)}) copy-start(f32[768]{0:T(1024)S(1)} %get-tuple-element.125) | copy-start | bytes 9220
  238.7 48.2 %copy-start.7 = (bf16[1024,768]{1,0:T(8,128)(2,1)S(1)}, bf16[1024,768]{1,0:T(8,128)(2,1)}, u32[]{:S(2)}) copy-start(bf16[1024,768]{1,0:T(8,128)(2,1)} %reduce-scatter.10.cloned.1.call-done) | copy-start | bytes 4718596
  240.5 73.0 %copy-start.37 = (f32[1024]{0:T(1024)}, f32[1024]{0:T(1024)S(1)}, u32[]{:S(2)}) copy-start(f32[1024]{0:T(1024)S(1)} %broadcast_multiply_fusion.4) | copy-start | bytes 12292
  242.5 52.2 %copy-start.41 = (f32[1024]{0:T(1024)}, f32[1024]{0:T(1024)S(1)}, u32[]{:S(2)}) copy-start(f32[1024]{0:T(1024)S(1)} %fusion.35) | copy-start | bytes 12292
  242.5 70.9 %copy-start.47 = (f32[1024]{0:T(1024)}, f32[1024]{0:T(1024)S(1)}, u32[]{:S(2)}) copy-start(f32[1024]{0:T(1024)S(1)} %fusion.116) | copy-start | bytes 12292
  320.5 245.3 %reduce-scatter.12.cloned.1.call-start = ((), (), s32[]{:S(2)}) async-start(), calls=%async_computation.9 | async-start | bytes 7864320 | tf_op jit(solution)/shard_map/reduce_scatter | solution.py:176
  434.4 15.5 %copy-start.62 = (bf16[768,1536]{1,0:T(8,128)(2,1)S(1)}, bf16[768,1536]{1,0:T(8,128)(2,1)}, u32[]{:S(2)}) copy-start(bf16[768,1536]{1,0:T(8,128)(2,1)} %all-gather.12.cloned.1.call-done) | copy-start | bytes 7077892
  456.9 248.2 %all-gather.14.cloned.1.call-start = ((), (), s32[]{:S(2)}) async-start(), calls=%async_computation.10 | async-start | bytes 7864320 | tf_op jit(solution)/shard_map/all_gather | solution.py:210
  587.6 117.4 %copy-start.63 = (bf16[768,1536]{1,0:T(8,128)(2,1)S(1)}, bf16[768,1536]{1,0:T(8,128)(2,1)}, u32[]{:S(2)}) copy-start(bf16[768,1536]{1,0:T(8,128)(2,1)} %all-gather.12.cloned.1.call-done) | copy-start | bytes 7077892
  589.0 351.2 %reduce-scatter.14.cloned.1.call-start = ((), (), s32[]{:S(2)}) async-start(), calls=%async_computation.11 | async-start | bytes 15728640 | tf_op jit(solution)/shard_map/reduce_scatter | solution.py:216
  730.1 9.6 slice-start.6
  730.1 277.6 %reduce-scatter.18.cloned.1.call-start = ((), (), s32[]{:S(2)}) async-start(), calls=%async_computation.15 | async-start | bytes 2654208
  746.7 193.6 %copy-start.1 = (f32[1024,768]{1,0:T(8,128)S(1)}, f32[1024,768]{1,0:T(8,128)}, u32[]{:S(2)}) copy-start(f32[1024,768]{1,0:T(8,128)} %copy-done) | copy-start | bytes 9437188
  751.1 361.9 %all-gather.16.cloned.1.call-start = ((), (), s32[]{:S(2)}) async-start(), calls=%async_computation.12 | async-start | bytes 7864320 | tf_op jit(solution)/shard_map/all_gather | solution.py:237
  964.1 11.8 slice-start.4
  965.5 10.4 slice-start.5
  966.5 9.5 copy-start.8
  966.5 9.5 copy-start.16
  966.5 9.5 copy-start.38
  966.5 9.5 copy-start.48
  966.5 9.5 copy-start.50
  985.6 313.7 %reduce-scatter.16.cloned.1.call-start = ((), (), s32[]{:S(2)}) async-start(), calls=%async_computation.13 | async-start | bytes 12165120 | tf_op jit(solution)/shard_map/reduce_scatter | solution.py:245
  1000.1 113.0 %copy-start.40 = (pred[4096]{0:T(1024)(128)(4,1)S(1)}, pred[4096]{0:T(1024)(128)(4,1)}, u32[]{:S(2)}) copy-start(pred[4096]{0:T(1024)(128)(4,1)} %copy-done.39) | copy-start | bytes 12292
  1287.4 3.5 collective-permute-start
  1297.9 50.9 %copy-start.17 = (f32[96,1536]{0,1:T(8,128)S(1)}, f32[96,1536]{0,1:T(8,128)}, u32[]{:S(2)}) copy-start(f32[96,1536]{0,1:T(8,128)} %copy.108) | copy-start | bytes 1769476
  (56 other events, 260.3 us)
Sparse Core Ops, SparseCore 0:
  11.4 71.4 all-gather.17
  124.9 113.6 reduce-scatter.9
  589.1 115.8 all-gather.13
  985.8 127.2 all-gather.15
Sparse Core Ops, SparseCore 1:
  128.7 158.1 all-gather.7
  289.1 27.3 all-gather.11
  320.6 113.7 all-gather.9
  457.0 108.8 reduce-scatter.11
  730.2 210.0 reduce-scatter.13
  944.2 43.4 reduce-scatter.17
  1000.2 194.9 reduce-scatter.15
where the time goes:
time: 1380 us
  waiting for transfers between devices  834 us (60%)
  blocking collectives  162 us (12%)
  other arithmetic  144 us (10%)
  matrix products  106 us (8%)
  local copies, waits for them, and re-layouts  102 us (7%)
  between operations  25.9 us (2%)
    reduce_scatter x1, waiting for transfers between devices, per_device(): lax.psum_scatter(jnp.dot(rows_in, up_rows, preferred_element_type=jnp.flo...  189 us
    unnamed x1, blocking collectives  122 us
    all_gather x1, waiting for transfers between devices, per_device(): grad_feed_rows = lax.all_gather(grad_feed_low, 'mp', axis=0, tiled=True)  116 us
    reduce_scatter x1, waiting for transfers between devices, per_device(): lax.psum_scatter(picked, 'mp', scatter_dimension=0, tiled=True)  110 us
    reduce_scatter x1, waiting for transfers between devices, per_device(): lax.psum_scatter(jnp.dot(rows_in, down_rows, preferred_element_type=jnp.f...  108 us
    all_gather x1, waiting for transfers between devices, per_device(): lax.all_gather(grad_embedded.astype(jnp.bfloat16), 'mp', axis=0, tiled=True)  104 us
    all_gather x1, waiting for transfers between devices, per_device(): ffn_rows_in = lax.all_gather(middle_low, 'mp', axis=0, tiled=True)  90.7 us
    all_gather x1, waiting for transfers between devices, per_device(): lax.all_gather(table_low, 'dp', axis=0, tiled=True)  70.7 us
  transfers between devices with their start and end apart: 12, of which 8 were waited for; matrix products, arithmetic and copies ran while one was open for 24% of the time, Pallas kernels for 0%

commit v1 on v0

--- a/solution.py
+++ b/solution.py
@@ -22,10 +22,35 @@
 clip_bound = 1.0
 
 
-def layer_norm(values, gain_row, shift_row):
+def norm_forward(values, gain_row, shift_row):
     center = values - jnp.mean(values, axis=-1, keepdims=True)
     spread = jnp.mean(center * center, axis=-1, keepdims=True)
-    return center * lax.rsqrt(spread + norm_epsilon) * gain_row + shift_row
+    inverse = lax.rsqrt(spread + norm_epsilon)
+    unit = center * inverse
+    return (unit * gain_row + shift_row, unit, inverse)
+
+
+def norm_backward(grad, unit, inverse, gain_row):
+    scaled = grad * gain_row
+    level = jnp.mean(scaled, axis=-1, keepdims=True)
+    along = jnp.mean(scaled * unit, axis=-1, keepdims=True)
+    grad_values = inverse * (scaled - level - unit * along)
+    return (grad_values, jnp.sum(grad * unit, axis=0), jnp.sum(grad, axis=0))
+
+
+gelu_rate = 0.7978845608028654
+gelu_cube = 0.044715
+
+
+def gelu_forward(before):
+    bend = jnp.tanh(gelu_rate * (before + gelu_cube * before * before * before))
+    return 0.5 * before * (1.0 + bend)
+
+
+def gelu_slope(before):
+    bend = jnp.tanh(gelu_rate * (before + gelu_cube * before * before * before))
+    inner = gelu_rate * (1.0 + 3.0 * gelu_cube * before * before)
+    return 0.5 * (1.0 + bend) + 0.5 * before * (1.0 - bend * bend) * inner
 
 
 def adam_update(weight, gradient, first_moment, second, decay_rate, rate):
@@ -120,75 +145,111 @@
     norm_moment,
     norm_square,
 ):
+    both = ("dp", "mp")
     mp_count = lax.axis_size("mp")
     mp_index = lax.axis_index("mp")
+    n_dev = lax.axis_size("dp") * mp_count
     own_seqs = teacher_logits.shape[0]
     own_rows = own_seqs * L
-    table_low = embed_table.astype(jnp.bfloat16)
-    dense_narrow_part = dense_weights.astype(jnp.bfloat16)
-    feedforward_narrow = feedforward.astype(jnp.bfloat16)
-    table_block, ffn_local = (
-        lax.all_gather(table_low, "dp", axis=0, tiled=True),
-        lax.all_gather(feedforward_narrow, "dp", axis=0, tiled=True),
-    )
-    dense_full = lax.all_gather(dense_narrow_part, ("dp", "mp"), axis=0, tiled=True)
-    neuron_piece = feedforward.shape[0]
-    neuron_slot = jnp.arange(ffn_local.shape[0])
-    neuron_index = (
-        neuron_slot // neuron_piece * mp_count + mp_index
-    ) * neuron_piece + neuron_slot % neuron_piece
-    block_rows = table_block.shape[0]
-    piece_rows = embed_table.shape[0]
-    chosen = jnp.where(replaced == 1, replacements, token_ids).reshape(-1)
-    block_number = chosen // piece_rows
-    inside = block_number % mp_count == mp_index
-    clipped = block_number // mp_count * piece_rows + chosen % piece_rows
-    picked = jnp.where(inside[:, None], table_block[clipped], jnp.zeros((), jnp.bfloat16))
-    embedded = lax.psum_scatter(picked, "mp", scatter_dimension=0, tiled=True).astype(jnp.float32)
+    table_rows = embed_table.shape[0]
+    low = jnp.bfloat16
+    dense_full = lax.all_gather(dense_weights.astype(low), both, axis=0, tiled=True)
+    ffn_full = lax.all_gather(feedforward.astype(low), both, axis=0, tiled=True)
+    table_low = embed_table.astype(low)
+
+    depth = -(-(own_rows * 3 // 2) // (n_dev * 16)) * 16
+    capacity = depth - 1
     own_start = mp_index * own_seqs
+    own_ids = lax.dynamic_slice_in_dim(
+        jnp.where(replaced == 1, replacements, token_ids), own_start, own_seqs
+    ).reshape(own_rows)
+    owner = own_ids // table_rows
+    local = own_ids - owner * table_rows
+    place = jnp.arange(own_rows)
+    first = jnp.min(
+        jnp.where(own_ids[:, None] == own_ids[None, :], place[None, :], own_rows), axis=1
+    )
+    leads = first == place
+    slot = jnp.sum(
+        (leads[None, :] & (owner[:, None] == owner[None, :]) & (place[None, :] < first[:, None])).astype(
+            jnp.int32
+        ),
+        axis=1,
+    )
+    deepest = jnp.max(slot)
+
+    def positions(turn):
+        rank = slot - turn * capacity
+        return jnp.where((rank >= 0) & (rank < capacity), owner * depth + rank, -1)
+
+    def wanted(turn):
+        spot = jnp.where(leads, positions(turn), -1)
+        hits = spot[:, None] == jnp.arange(n_dev * depth)[None, :]
+        rows = jnp.max(jnp.where(hits, local[:, None], -1), axis=0).reshape(n_dev, depth)
+        return jnp.where(jnp.arange(depth)[None, :] == capacity, deepest, rows)
+
+    def exchange(blocks):
+        return lax.all_to_all(blocks, both, split_axis=0, concat_axis=0)
+
+    def asked_hot(asked):
+        flat = jnp.where(jnp.arange(depth)[None, :] < capacity, asked, -1).reshape(-1)
+        return (flat[:, None] == jnp.arange(table_rows)[None, :]).astype(low)
+
+    def own_hot(turn):
+        return (positions(turn)[:, None] == jnp.arange(n_dev * depth)[None, :]).astype(low)
+
+    def fetch(turn, asked):
+        rows = jnp.dot(asked_hot(asked), table_low, preferred_element_type=low)
+        rows = exchange(rows.reshape(n_dev, depth, MODEL_WIDTH)).reshape(-1, MODEL_WIDTH)
+        return jnp.dot(own_hot(turn), rows, preferred_element_type=jnp.float32)
+
+    asked_first = exchange(wanted(0))
+    turns = jnp.max(asked_first[:, capacity]) // capacity + 1
+    embedded = fetch(0, asked_first)
+    embedded = lax.while_loop(
+        lambda state: state[0] < turns,
+        lambda state: (state[0] + 1, state[1] + fetch(state[0], exchange(wanted(state[0])))),
+        (jnp.int32(1), embedded),
+    )[1]
+
     own_lengths = lax.dynamic_slice_in_dim(lengths, own_start, own_seqs)
     own_levels = lax.dynamic_slice_in_dim(widths, own_start, own_seqs)
     usable_grid = (jnp.arange(L)[None, :] < own_lengths[:, None]).astype(jnp.float32)
     usable = usable_grid.reshape(own_rows, 1)
-    head_on = (jnp.arange(HEADS)[None, :] < own_levels[:, None] * HEADS // LEVELS).astype(
+    head_on = (jnp.arange(HEADS)[None, :] < own_levels[:, None] * (HEADS // LEVELS)).astype(
         jnp.float32
     )
-    normalized_rows, normed_pull = jax.vjp(layer_norm, embedded, norm_gains[0], norm_gains[1])
-    normed_low = normalized_rows.astype(jnp.bfloat16)
+    row_limit = jnp.broadcast_to(own_levels[:, None] * (FF // LEVELS), (own_seqs, L)).reshape(
+        own_rows, 1
+    )
+    neuron_on = jnp.arange(FF)[None, :] < row_limit
+
+    normalized_rows, unit_base, inverse_base = norm_forward(embedded, norm_gains[0], norm_gains[1])
+    normed_low = normalized_rows.astype(low)
     qkv_rows = dense_full[: 3 * MODEL_WIDTH]
-    output_projection = contract_last(normed_low, qkv_rows).astype(jnp.bfloat16)
+    output_projection = contract_last(normed_low, qkv_rows).astype(low)
     attend, head_mixture = attention_forward(output_projection, usable_grid, head_on)
     out_rows = dense_full[3 * MODEL_WIDTH : 4 * MODEL_WIDTH]
     attention_result = jnp.dot(head_mixture, out_rows, preferred_element_type=jnp.float32)
-    middle_activation, middle_pull = jax.vjp(
-        layer_norm, normalized_rows + attention_result, norm_gains[2], norm_gains[3]
-    )
-    middle_low = middle_activation.astype(jnp.bfloat16)
-    up_rows = ffn_local[:, :MODEL_WIDTH]
-    down_rows = ffn_local[:, MODEL_WIDTH:]
-    ffn_rows_in = lax.all_gather(middle_low, "mp", axis=0, tiled=True)
-    row_levels = jnp.repeat(widths, L, total_repeat_length=own_rows * mp_count)
-    residual_before = contract_last(ffn_rows_in, up_rows)
-    neuron_on = (neuron_index[None, :] < row_levels[:, None] * FF // LEVELS).astype(jnp.float32)
-    activated, gelu_pull = jax.vjp(jax.nn.gelu, residual_before)
-    hidden_low = (activated * neuron_on).astype(jnp.bfloat16)
-    rows_in = lax.slice_in_dim(hidden_low, 0, lax.axis_size("mp") * own_rows, axis=0)
-    feedforward_result = lax.psum_scatter(
-        jnp.dot(rows_in, down_rows, preferred_element_type=jnp.float32).astype(jnp.bfloat16),
-        "mp",
-        scatter_dimension=0,
-        tiled=True,
-    ).astype(jnp.float32)
-    output, output_pull = jax.vjp(
-        layer_norm, middle_activation + feedforward_result, norm_gains[4], norm_gains[5]
+    middle_activation, unit_one, inverse_one = norm_forward(
+        normalized_rows + attention_result, norm_gains[2], norm_gains[3]
+    )
+    middle_low = middle_activation.astype(low)
+    up_rows = ffn_full[:, :MODEL_WIDTH]
+    down_rows = ffn_full[:, MODEL_WIDTH:]
+    residual_before = contract_last(middle_low, up_rows)
+    hidden_low = jnp.where(neuron_on, gelu_forward(residual_before), 0.0).astype(low)
+    feedforward_result = jnp.dot(hidden_low, down_rows, preferred_element_type=jnp.float32)
+    output, unit_two, inverse_two = norm_forward(
+        middle_activation + feedforward_result, norm_gains[4], norm_gains[5]
     )
     embed_diff = normalized_rows - teacher_embed.reshape(own_rows, MODEL_WIDTH).astype(jnp.float32)
     hidden_diff = output - teacher_hidden.reshape(own_rows, MODEL_WIDTH).astype(jnp.float32)
-    first_low = output.reshape(own_seqs, L, MODEL_WIDTH)[:, 0].astype(jnp.bfloat16)
+    first_low = output.reshape(own_seqs, L, MODEL_WIDTH)[:, 0].astype(low)
     pool_rows = dense_full[4 * MODEL_WIDTH :]
     pooled = jnp.tanh(jnp.dot(first_low, pool_rows, preferred_element_type=jnp.float32))
-    pooled_low = pooled.astype(jnp.bfloat16)
-    class_low = classifier.astype(jnp.bfloat16)
+    pooled_low = pooled.astype(low)
+    class_low = classifier.astype(low)
     logits = jnp.dot(pooled_low, class_low, preferred_element_type=jnp.float32)
     logit_diff = logits - teacher_logits
     loss_own = jnp.sum(usable * embed_diff * embed_diff) + jnp.sum(
@@ -205,66 +266,101 @@
     grad_first = jnp.dot(grad_inner, pool_rows.astype(jnp.float32).T, precision=highest_precision)
     grad_output = (2.0 * usable * hidden_diff).reshape(own_seqs, L, MODEL_WIDTH)
     grad_output = grad_output.at[:, 0].add(grad_first).reshape(own_rows, MODEL_WIDTH)
-    grad_second, gain_two, shift_two = output_pull(grad_output)
-    grad_feed_low = grad_second.astype(jnp.bfloat16)
-    grad_feed_rows = lax.all_gather(grad_feed_low, "mp", axis=0, tiled=True)
-    grad_down = contract_first(hidden_low, grad_feed_rows)
-    grad_hidden = contract_last(grad_feed_rows, down_rows)
-    grad_before = gelu_pull(grad_hidden * neuron_on)[0].astype(jnp.bfloat16)
-    grad_up = contract_first(grad_before, ffn_rows_in)
-    rows_in = grad_before
-    grad_middle_ffn = lax.psum_scatter(
-        jnp.dot(rows_in, up_rows, preferred_element_type=jnp.float32),
-        "mp",
-        scatter_dimension=0,
-        tiled=True,
-    )
-    grad_first_sum, gain_one, shift_one = middle_pull(grad_second + grad_middle_ffn)
-    grad_att_low = grad_first_sum.astype(jnp.bfloat16)
+    grad_second, gain_two, shift_two = norm_backward(grad_output, unit_two, inverse_two, norm_gains[4])
+    grad_feed_low = grad_second.astype(low)
+
+    def scatter_sum(rows):
+        over_dp = lax.psum_scatter(rows, "dp", scatter_dimension=0, tiled=True)
+        return lax.psum_scatter(over_dp, "mp", scatter_dimension=0, tiled=True)
+
+    grad_down = scatter_sum(contract_first(hidden_low, grad_feed_low).astype(low))
+    grad_hidden = contract_last(grad_feed_low, down_rows)
+    grad_before = jnp.where(neuron_on, grad_hidden * gelu_slope(residual_before), 0.0).astype(low)
+    grad_up = scatter_sum(contract_first(grad_before, middle_low).astype(low))
+    grad_middle_ffn = jnp.dot(grad_before, up_rows, preferred_element_type=jnp.float32)
+    grad_first_sum, gain_one, shift_one = norm_backward(
+        grad_second + grad_middle_ffn, unit_one, inverse_one, norm_gains[2]
+    )
+    grad_att_low = grad_first_sum.astype(low)
     grad_out_rows = contract_first(head_mixture, grad_att_low)
-    grad_mixture = contract_last(grad_att_low, out_rows).astype(jnp.bfloat16)
+    grad_mixture = contract_last(grad_att_low, out_rows).astype(low)
     grad_mixture = grad_mixture.reshape(own_seqs, L, HEADS, MODEL_WIDTH // HEADS) * head_on[
         :, None, :, None
-    ].astype(jnp.bfloat16)
+    ].astype(low)
     grad_project = attention_backward(output_projection, attend, grad_mixture)
     grad_qkv_rows = contract_first(grad_project, normed_low)
+    grad_dense = jnp.concatenate([grad_qkv_rows, grad_out_rows, grad_pool_rows], axis=0)
+    dense_grad = scatter_sum(grad_dense.astype(low)).astype(jnp.float32)
     grad_normed = (
         grad_first_sum
         + 2.0 * usable * embed_diff
         + jnp.dot(grad_project, qkv_rows, preferred_element_type=jnp.float32)
     )
-    grad_embedded, gain_base, shift_base = normed_pull(grad_normed)
-    grad_embed_rows = lax.all_gather(grad_embedded.astype(jnp.bfloat16), "mp", axis=0, tiled=True)
-    grad_table = jax.ops.segment_sum(
-        jnp.where(inside[:, None], grad_embed_rows.astype(jnp.float32), 0.0),
-        clipped,
-        num_segments=block_rows,
-    )
-    grad_dense = jnp.concatenate([grad_qkv_rows, grad_out_rows, grad_pool_rows], axis=0)
-    grad_ffn = jnp.concatenate([grad_up, grad_down], axis=1)
-    dense_grad = lax.psum_scatter(grad_dense, ("dp", "mp"), scatter_dimension=0, tiled=True)
-    table_grad, ffn_grad = (
-        lax.psum_scatter(
-            grad_table.astype(jnp.bfloat16), "dp", scatter_dimension=0, tiled=True
-        ).astype(jnp.float32),
-        lax.psum_scatter(
-            grad_ffn.astype(jnp.bfloat16), "dp", scatter_dimension=0, tiled=True
-        ).astype(jnp.float32),
-    )
-    grad_gains = jnp.stack(
-        [gain_base, shift_base, gain_one, shift_one, gain_two, shift_two], axis=0
-    )
-    gains_grad, class_grad = lax.psum((grad_gains, grad_class), ("dp", "mp"))
+    grad_embedded, gain_base, shift_base = norm_backward(
+        grad_normed, unit_base, inverse_base, norm_gains[0]
+    )
+    grad_embed_low = grad_embedded.astype(low)
+
+    small = jnp.concatenate(
+        [
+            jnp.stack([gain_base, shift_base, gain_one, shift_one, gain_two, shift_two]).reshape(-1),
+            grad_class.reshape(-1),
+        ]
+    )
+    share = -(-small.shape[0] // n_dev)
+    small_parts = jnp.pad(small, (0, share * n_dev - small.shape[0])).reshape(n_dev, share)
+    upper = lax.reduce_precision(small_parts, 8, 7)
+    rider = jnp.concatenate([upper, small_parts - upper], axis=1).astype(low)
+    rider = jnp.pad(rider, ((0, 0), (0, MODEL_WIDTH - 2 * share)))
+
+    def give_back(turn):
+        sums = lax.dot_general(
+            own_hot(turn), grad_embed_low, (((0,), (0,)), ((), ())), preferred_element_type=jnp.float32
+        )
+        return sums.reshape(n_dev, depth, MODEL_WIDTH)
+
+    def collect(asked, returned):
+        return lax.dot_general(
+            asked_hot(asked),
+            returned.reshape(-1, MODEL_WIDTH),
+            (((0,), (0,)), ((), ())),
+            preferred_element_type=jnp.float32,
+        )
+
+    sums = give_back(0)
+    sums = jnp.where(jnp.arange(depth)[None, :, None] == capacity, rider.astype(jnp.float32)[:, None, :], sums)
+    returned = exchange(sums.astype(low))
+    table_grad = collect(asked_first, returned)
+    table_grad = lax.while_loop(
+        lambda state: state[0] < turns,
+        lambda state: (
+            state[0] + 1,
+            state[1]
+            + collect(exchange(wanted(state[0])), exchange(give_back(state[0]).astype(low))),
+        ),
+        (jnp.int32(1), table_grad),
+    )[1]
+    riders = jnp.sum(returned[:, capacity, : 2 * share].astype(jnp.float32), axis=0)
+    small_share = riders[:share] + riders[share:]
+    ffn_grad = jnp.concatenate([grad_up, grad_down], axis=1).astype(jnp.float32)
     square_sum = (
         jnp.sum(table_grad * table_grad)
         + jnp.sum(dense_grad * dense_grad)
         + jnp.sum(ffn_grad * ffn_grad)
+        + jnp.sum(small_share * small_share)
     )
     own_count = jnp.sum(own_lengths).astype(jnp.float32)
-    total_square, token_count, loss_sum = lax.psum((square_sum, own_count, loss_own), ("dp", "mp"))
-    small_square = jnp.sum(gains_grad * gains_grad) + jnp.sum(class_grad * class_grad)
+    message = jnp.concatenate([small_share, jnp.stack([square_sum, own_count, loss_own])])
+    message = jnp.pad(message, (0, -message.shape[0] % 128))
+    told = exchange(jnp.broadcast_to(message[None], (n_dev, message.shape[0])))
+    scalars = jnp.sum(told[:, share : share + 3], axis=0)
+    total_square, token_count, loss_sum = scalars[0], scalars[1], scalars[2]
+    small_all = told[:, :share].reshape(-1)
+    gains_size = norm_gains.size
+    gains_grad = small_all[:gains_size].reshape(norm_gains.shape)
+    class_grad = small_all[gains_size : gains_size + classifier.size].reshape(classifier.shape)
     inverse = 1.0 / token_count
-    grad_norm = jnp.sqrt(total_square + small_square) * inverse
+    grad_norm = jnp.sqrt(total_square) * inverse
     scaling = inverse * (clip_bound / jnp.maximum(grad_norm, clip_bound))
     table_new = adam_update(
         embed_table, table_grad * scaling, embed_moment, embed_square, weight_decay, learn_rate

time: 1380 us -> 565 us (0.41)
  waiting for transfers between devices: 834 us -> 263 us
  blocking collectives: 162 us -> 11.2 us
  other arithmetic: 144 us -> 64.6 us
  local copies, waits for them, and re-layouts: 102 us -> 43.9 us
  matrix products: 106 us -> 135 us
    all_gather x6 -> x2, waiting for transfers between devices: 426 us -> 37.4 us  [the longest x1 37.4 us: per_device(): ffn_full = lax.all_gather(feedforward.astype(low), both, axis=0, tiled=True)]
    reduce_scatter x4 -> x6, waiting for transfers between devices: 407 us -> 130 us  [the longest x3 65.5 us: scatter_sum(): over_dp = lax.psum_scatter(rows, 'dp', scatter_dimension=0, tiled=True)]
    unnamed x1 -> x0, blocking collectives: 122 us -> none
    all_to_all x0 -> x3, waiting for transfers between devices: none -> 94.5 us  [exchange(): return lax.all_to_all(blocks, both, split_axis=0, concat_axis=0)]
    psum x1 -> x0, blocking collectives: 39.8 us -> none  [per_device(): lax.psum((square_sum, own_count, loss_own), ('dp', 'mp'))]
    scatter-add x1 -> x0, other arithmetic: 39.6 us -> none  [per_device(): jax.ops.segment_sum(jnp.where(inside[:, None], grad_embed_rows.astype(jnp...]
    unnamed x167 -> x140, local copies, waits for them, and re-layouts: 55 us -> 20.2 us
    gather x3 -> x0, local copies, waits for them, and re-layouts: 26.3 us -> none  [the longest x1 24.9 us: per_device(): table_block[clipped]]
  transfers between devices with their start and end apart: 12 -> 11, of which waited for: 8 -> 9; matrix products, arithmetic and copies ran while one was open for 24% -> 28% of each run, Pallas kernels for 0% -> 0%
where the time goes in v1:
time: 565 us; the launch traced here: 558 us
  waiting for transfers between devices  263 us (47%)
  matrix products  135 us (24%)
  other arithmetic  64.6 us (11%)
  local copies, waits for them, and re-layouts  43.9 us (8%)
  between operations  25.3 us (4%)
  starting transfers between devices  14.9 us (3%)
  blocking collectives  11.2 us (2%)
    all_to_all x3, waiting for transfers between devices, exchange(): return lax.all_to_all(blocks, both, split_axis=0, concat_axis=0)  94.5 us
    reduce_scatter x3, waiting for transfers between devices, scatter_sum(): over_dp = lax.psum_scatter(rows, 'dp', scatter_dimension=0, tiled=True)  65.5 us
    reduce_scatter x3, waiting for transfers between devices, scatter_sum(): return lax.psum_scatter(over_dp, 'mp', scatter_dimension=0, tiled=True)  64.5 us
    dot_general x4, matrix products, contract_last(): lax.dot_general(left, right, (((1,), (1,)), ((), ())), preferred_element_...  40.4 us
    all_gather x1, waiting for transfers between devices, per_device(): ffn_full = lax.all_gather(feedforward.astype(low), both, axis=0, tiled=True)  37.4 us
    dot_general x4, matrix products, contract_first(): lax.dot_general(left, right, (((0,), (0,)), ((), ())), preferred_element_...  23.9 us
    unnamed x140, local copies, waits for them, and re-layouts  20.2 us
    all_to_all x3, starting transfers between devices, exchange(): return lax.all_to_all(blocks, both, split_axis=0, concat_axis=0)  14.4 us
  transfers between devices with their start and end apart: 11, of which 9 were waited for; matrix products, arithmetic and copies ran while one was open for 28% of the time, Pallas kernels for 0%

profile of v1, /device:TPU:0, one launch (start us, length us, event | category | flops | bytes accessed | tf_op | source)
XLA Modules:
  0.0 557.7 jit_solution(11036392182914962764)
XLA Ops:
  18.5 7.3 %all-to-all-start.4 = ((s32[32,1,48]{2,1,0:T(1,128)}), s32[32,1,48]{2,1,0:T(1,128)S(1)}, u32[]{:S(2)}, u32[]{:S(2)}) async-start(s32[32,1,48]{2,1,0:T(1,128)} %bitcast.5), calls=%async_computation.4 | async-start | bytes 32768 | tf_op jit(solution)/shard_map/all_to_all | solution.py:192
  27.9 5.1 all-to-all-done.4
  34.3 4.2 fusion.22
  46.7 68.9 %all-to-all-done.5 = bf16[32,48,768]{2,1,0:T(8,128)(2,1)S(1)} async-done(((bf16[32,48,768]{2,1,0:T(8,128)(2,1)}), bf16[32,48,768]{2,1,0:T(8,128)(2,1)S(1)}, u32[]{:S(2)}, u32[]{:S(2)}) %all-to-all-start.5) | async-done | bytes 2359328 | tf_op jit(solution)/shard_map/all_to_all | solution.py:192
  115.5 4.5 fusion.24
  124.2 7.8 %convolution_convert_fusion = bf16[1024,2304]{1,0:T(8,128)(2,1)} fusion(bf16[3840,768]{1,0:T(8,128)(2,1)} %all-gather.3.cloned.1.call-done, f32[768]{0:T(1024)S(1)} %get-tuple-element.259, f32[768]{0:T(1024)S(1)} %get-tuple-element.260, f32[1024,768]{1,0:T(8,128)S(1)} %copy-done.2, f32[1024]{0:T(1024)S(1)} %add_rsqrt_fusion.2, ...), kind=kOutput, calls=%fused_computation.58 | convolution fusion | flops 3630170112 | bytes 11417600 | tf_op jit(solution)/shard_map/dot_general | solution.py:68
  132.0 6.7 %copy.220 = bf16[1024,2304]{0,1:T(8,128)(2,1)} copy(bf16[1024,2304]{1,0:T(8,128)(2,1)} %convolution_convert_fusion) | data formatting | bytes 9437184 | tf_op jit(solution)/shard_map/convert_element_type | solution.py:230
  138.7 3.6 copy.252
  150.9 3.8 fusion.151
  156.9 37.4 %all-gather.5.cloned.1.call-done = bf16[3072,1536]{1,0:T(8,128)(2,1)} async-done(((bf16[96,1536]{1,0:T(8,128)(2,1)}), bf16[3072,1536]{1,0:T(8,128)(2,1)}) %all-gather.5.cloned.1.call-update) | async-done | bytes 9437200 | tf_op jit(solution)/shard_map/all_gather | solution.py:157
  194.3 14.6 %select_convert_fusion = (bf16[1024,3072]{1,0:T(8,128)(2,1)S(1)}, f32[1024,3072]{1,0:T(8,128)}) fusion(s32[1024]{0:T(1024)S(1)} %broadcast_bitcast_fusion, bf16[3072,1536]{1,0:T(8,128)(2,1)} %all-gather.5.cloned.1.call-done, f32[1024,768]{1,0:T(8,128)} %copy-done.9, f32[768]{0:T(1024)S(1)} %get-tuple-element.258, f32[768]{0:T(1024)S(1)} %get-tuple-element.256, ...), kind=kOutput, calls=%fused_computation.43 | convolution fusion | flops 4870373376 | bytes 26757120 | tf_op jit(solution)/shard_map/dot_general | solution.py:68
  208.9 5.4 fusion.152
  225.1 4.4 fusion.41
  230.8 15.2 %fusion.20 = bf16[1024,3072]{1,0:T(8,128)(2,1)S(1)} fusion(f32[1024,3072]{1,0:T(8,128)} %get-tuple-element.352, s32[1024]{0:T(1024)S(1)} %broadcast_bitcast_fusion, bf16[3072,1536]{1,0:T(8,128)(2,1)S(1)} %bitcast.179, f32[1024,768]{1,0:T(8,128)S(1)} %subtract_multiply_fusion.1), kind=kOutput, calls=%fused_computation.42 | convolution fusion | flops 4898684928 | bytes 26742784 | tf_op jit(solution)/shard_map/dot_general | solution.py:68
  248.7 7.8 %convolution_convert_fusion.2 = bf16[3072,768]{1,0:T(8,128)(2,1)} fusion(bf16[1024,3072]{1,0:T(8,128)(2,1)S(1)} %fusion.20, f32[1024,768]{1,0:T(8,128)S(1)} %copy-done.11, f32[768]{0:T(1024)S(1)} %get-tuple-element.258, f32[768]{0:T(1024)S(1)} %get-tuple-element.256, f32[1024]{0:T(1024)S(1)} %add_rsqrt_fusion.1, f32[1024]{0:T(1024)S(1)} %broadcast_multiply_fusion.7), kind=kOutput, calls=%fused_computation.60 | convolution fusion | flops 4838129664 | bytes 14170112 | tf_op jit(solution)/shard_map/dot_general | solution.py:74
  257.3 11.3 %multiply_reduce_fusion.2 = (f32[768]{0:T(1024)S(1)}, f32[1024]{0:T(1024)S(1)}, f32[1024]{0:T(1024)S(1)}, f32[768]{0:T(1024)S(1)}, f32[1024,768]{1,0:T(8,128)}) fusion(f32[1024,768]{1,0:T(8,128)S(1)} %copy-done.11, f32[1024]{0:T(1024)S(1)} %add_rsqrt_fusion.1, f32[1024]{0:T(1024)S(1)} %broadcast_multiply_fusion.7, f32[768]{0:T(1024)S(1)} %get-tuple-element.256, ...), kind=kOutput, calls=%fused_computation.93 | convolution fusion | flops 4839698432 | bytes 20472832 | tf_op jit(solution)/shard_map/dot_general | solution.py:280
  268.7 10.0 %convolution_convert_fusion.1 = bf16[3072,768]{1,0:T(8,128)(2,1)} fusion(bf16[1024,3072]{1,0:T(8,128)(2,1)} %copy-done.62, f32[1024,768]{1,0:T(8,128)S(1)} %copy-done.18), kind=kOutput, calls=%fused_computation.59 | convolution fusion | flops 4834983936 | bytes 14155776 | tf_op jit(solution)/shard_map/dot_general | solution.py:74
  288.0 5.4 multiply_reduce_fusion
  302.5 9.3 %copy.236 = bf16[8,128,3,12,64]{1,0,4,3,2:T(8,128)(2,1)S(1)} copy(bf16[8,128,3,12,64]{1,4,3,0,2:T(8,128)(2,1)S(1)} %pad_maximum_fusion.1) | data formatting | bytes 9437184 | tf_op jit(solution)/shard_map/stack | solution.py:119
  315.3 4.7 convolution_convert_fusion.3
  323.1 13.3 %multiply_reduce_fusion.3 = (f32[768]{0:T(1024)S(1)}, f32[1024]{0:T(1024)}, f32[]{:T(128)}, f32[1024]{0:T(1024)}, f32[768]{0:T(1024)S(1)}, /*index=5*/f32[1024,768]{1,0:T(8,128)}) fusion(f32[1024]{0:T(1024)S(1)} %add_rsqrt_fusion.2, f32[1024,768]{1,0:T(8,128)S(1)} %copy-done.3, f32[1024]{0:T(1024)S(1)} %broadcast_multiply_fusion.8, ...), kind=kOutput, calls=%fused_computation.94 | convolution fusion | flops 3638817280 | bytes 19304452 | tf_op jit(solution)/shard_map/dot_general | solution.py:297
  343.5 3.8 fusion.23
  349.0 4.2 all-to-all-start.6
  353.8 28.7 %reduce-scatter.15.cloned.1.call-done = bf16[384,768]{1,0:T(8,128)(2,1)} async-done(((bf16[3072,768]{1,0:T(8,128)(2,1)}), bf16[384,768]{1,0:T(8,128)(2,1)}) %reduce-scatter.15.cloned.1.call-update) | async-done | bytes 589840 | tf_op jit(solution)/shard_map/reduce_scatter | solution.py:273
  385.4 20.6 %all-to-all-done.6 = bf16[32,48,768]{2,1,0:T(8,128)(2,1)S(1)} async-done(((bf16[32,48,768]{2,1,0:T(8,128)(2,1)}), bf16[32,48,768]{2,1,0:T(8,128)(2,1)S(1)}, u32[]{:S(2)}, u32[]{:S(2)}) %all-to-all-start.6) | async-done | bytes 2359328 | tf_op jit(solution)/shard_map/all_to_all | solution.py:192
  406.1 4.6 fusion.21
  410.7 36.7 %reduce-scatter.7.cloned.1.call-done = bf16[480,768]{1,0:T(8,128)(2,1)} async-done(((bf16[3840,768]{1,0:T(8,128)(2,1)}), bf16[480,768]{1,0:T(8,128)(2,1)}) %reduce-scatter.7.cloned.1.call-update) | async-done | bytes 737296 | tf_op jit(solution)/shard_map/reduce_scatter | solution.py:273
  451.5 20.0 %reduce-scatter.13.cloned.1.call-done = bf16[96,768]{1,0:T(8,128)(2,1)} async-done(((bf16[384,768]{1,0:T(8,128)(2,1)}), bf16[96,768]{1,0:T(8,128)(2,1)}) %reduce-scatter.13.cloned.1.call-update) | async-done | bytes 147472 | tf_op jit(solution)/shard_map/reduce_scatter | solution.py:274
  471.5 22.8 %reduce-scatter.17.cloned.1.call-done = bf16[96,768]{1,0:T(8,128)(2,1)} async-done(((bf16[384,768]{1,0:T(8,128)(2,1)}), bf16[96,768]{1,0:T(8,128)(2,1)}) %reduce-scatter.17.cloned.1.call-update) | async-done | bytes 147472 | tf_op jit(solution)/shard_map/reduce_scatter | solution.py:274
  496.0 21.8 %reduce-scatter.9.cloned.1.call-done = bf16[120,768]{1,0:T(8,128)(2,1)} async-done(((bf16[480,768]{1,0:T(8,128)(2,1)}), bf16[120,768]{1,0:T(8,128)(2,1)}) %reduce-scatter.9.cloned.1.call-update) | async-done | bytes 184336 | tf_op jit(solution)/shard_map/reduce_scatter | solution.py:274
  522.1 11.2 %all_to_all.65 = f32[32,1,256]{2,1,0:T(1,128)S(1)} all-to-all(f32[32,1,256]{2,1,0:T(1,128)S(1)} %broadcast_in_dim.249), channel_id=1, replica_groups=mesh['dp'=8,'mp'=4] {'dp','mp'}, dimensions={0} | all-to-all | bytes 65536 | tf_op jit(solution)/shard_map/all_to_all | solution.py:192
  538.2 7.0 %fusion.144 = (bf16[956,768]{1,0:T(8,128)(2,1)}, f32[956,768]{1,0:T(8,128)}, f32[956,768]{1,0:T(8,128)}, f32[956,768]{1,0:T(8,128)}) fusion(f32[956,768]{1,0:T(8,128)S(1)} %copy-done.12, f32[956,768]{1,0:T(8,128)} %get-tuple-element.131, f32[]{:T(128)S(6)} %mul.686, f32[956,768]{1,0:T(8,128)} %param.38, f32[956,768]{1,0:T(8,128)} %param.39), kind=kLoop, calls=%fused_computation.278 | loop fusion | flops 12481536 | bytes 22026244 | tf_op jit(solution)/shard_map/convert_element_type | solution.py:397
  (265 shorter events, 100.3 us)
Async XLA Ops:
  7.2 117.0 %all-gather.3.cloned.1.call-start = ((), (), s32[]{:S(2)}) async-start(), calls=%async_computation.14 | async-start | bytes 6082560 | tf_op jit(solution)/shard_map/all_gather | solution.py:156
  16.0 99.5 %copy-start.53 = (s32[1024]{0:T(1024)}, s32[1024]{0:T(1024)S(1)}, u32[]{:S(2)}) copy-start(s32[1024]{0:T(1024)S(1)} %get-tuple-element.326) | copy-start | bytes 12292
  17.2 8.6 %copy-start.55 = (pred[48]{0:T(512)(128)(4,1)}, pred[48]{0:T(512)(128)(4,1)S(1)}, u32[]{:S(2)}) copy-start(pred[48]{0:T(512)(128)(4,1)S(1)} %iota_compare_fusion.34) | copy-start | bytes 148
  18.5 14.5 %all-to-all-start.4 = ((s32[32,1,48]{2,1,0:T(1,128)}), s32[32,1,48]{2,1,0:T(1,128)S(1)}, u32[]{:S(2)}, u32[]{:S(2)}) async-start(s32[32,1,48]{2,1,0:T(1,128)} %bitcast.5), calls=%async_computation.4 | async-start | bytes 32768 | tf_op jit(solution)/shard_map/all_to_all | solution.py:192
  38.5 77.0 %all-to-all-start.5 = ((bf16[32,48,768]{2,1,0:T(8,128)(2,1)}), bf16[32,48,768]{2,1,0:T(8,128)(2,1)S(1)}, u32[]{:S(2)}, u32[]{:S(2)}) async-start(bf16[32,48,768]{2,1,0:T(8,128)(2,1)} %bitcast.170), calls=%async_computation.5 | async-start | bytes 4718592 | tf_op jit(solution)/shard_map/all_to_all | solution.py:192
  41.5 152.9 %all-gather.5.cloned.1.call-start = ((), (), s32[]{:S(2)}) async-start(), calls=%async_computation.15 | async-start | bytes 9732096 | tf_op jit(solution)/shard_map/all_gather | solution.py:157
  42.3 310.9 %reduce-scatter.11.cloned.1.call-start = ((), (), s32[]{:S(2)}) async-start(), calls=%async_computation.18 | async-start | bytes 5308416 | tf_op jit(solution)/shard_map/reduce_scatter | solution.py:273
  43.1 280.0 %copy-start.45 = (f32[768]{0:T(1024)}, f32[768]{0:T(1024)S(1)}, u32[]{:S(2)}) copy-start(f32[768]{0:T(1024)S(1)} %get-tuple-element.260) | copy-start | bytes 9220
  124.2 198.9 %copy-start.44 = (f32[1024]{0:T(1024)}, f32[1024]{0:T(1024)S(1)}, u32[]{:S(2)}) copy-start(f32[1024]{0:T(1024)S(1)} %add_rsqrt_fusion.2) | copy-start | bytes 12292
  194.3 14.6 %copy-start.10 = (f32[1024,768]{1,0:T(8,128)S(1)}, f32[1024,768]{1,0:T(8,128)}, u32[]{:S(2)}) copy-start(f32[1024,768]{1,0:T(8,128)} %copy-done.9) | copy-start | bytes 9437188
  194.3 14.6 %copy-start.60 = (bf16[3072,1536]{1,0:T(8,128)(2,1)S(1)}, bf16[3072,1536]{1,0:T(8,128)(2,1)}, u32[]{:S(2)}) copy-start(bf16[3072,1536]{1,0:T(8,128)(2,1)} %all-gather.5.cloned.1.call-done) | copy-start | bytes 28311556
  230.8 15.3 %copy-start.17 = (f32[1024,768]{1,0:T(8,128)}, f32[1024,768]{1,0:T(8,128)S(1)}, u32[]{:S(2)}) copy-start(f32[1024,768]{1,0:T(8,128)S(1)} %subtract_multiply_fusion.1) | copy-start | bytes 9437188
  230.8 17.9 %copy-start.11 = (f32[1024,768]{1,0:T(8,128)S(1)}, f32[1024,768]{1,0:T(8,128)}, u32[]{:S(2)}) copy-start(f32[1024,768]{1,0:T(8,128)} %copy-done.9) | copy-start | bytes 9437188
  256.6 125.9 %reduce-scatter.15.cloned.1.call-start = ((), (), s32[]{:S(2)}) async-start(), calls=%async_computation.20 | async-start | bytes 5308416 | tf_op jit(solution)/shard_map/reduce_scatter | solution.py:273
  257.3 11.3 %copy-start.18 = (f32[1024,768]{1,0:T(8,128)S(1)}, f32[1024,768]{1,0:T(8,128)}, u32[]{:S(2)}) copy-start(f32[1024,768]{1,0:T(8,128)} %copy-done.17) | copy-start | bytes 9437188
  278.7 168.8 %reduce-scatter.7.cloned.1.call-start = ((), (), s32[]{:S(2)}) async-start(), calls=%async_computation.16 | async-start | bytes 6635520 | tf_op jit(solution)/shard_map/reduce_scatter | solution.py:273
  302.5 10.5 %copy-start.16 = (f32[1024,768]{1,0:T(8,128)S(1)}, f32[1024,768]{1,0:T(8,128)}, u32[]{:S(2)}) copy-start(f32[1024,768]{1,0:T(8,128)} %copy-done.15) | copy-start | bytes 9437188
  302.5 10.5 %copy-start.25 = (bf16[8,128,12,64]{1,0,3,2:T(8,128)(2,1)S(1)}, bf16[8,128,12,64]{1,0,3,2:T(8,128)(2,1)}, u32[]{:S(2)}) copy-start(bf16[8,128,12,64]{1,0,3,2:T(8,128)(2,1)} %copy-done.24) | copy-start | bytes 4718596
  349.0 57.1 %copy-start.50 = (s32[1536]{0:T(1024)S(1)}, s32[1536]{0:T(1024)}, u32[]{:S(2)}) copy-start(s32[1536]{0:T(1024)} %copy-done.49) | copy-start | bytes 18436
  349.0 56.9 %all-to-all-start.6 = ((bf16[32,48,768]{2,1,0:T(8,128)(2,1)}), bf16[32,48,768]{2,1,0:T(8,128)(2,1)S(1)}, u32[]{:S(2)}, u32[]{:S(2)}) async-start(bf16[32,48,768]{2,1,0:T(8,128)(2,1)} %select_convert_fusion.1), calls=%async_computation.6 | async-start | bytes 4718592 | tf_op jit(solution)/shard_map/all_to_all | solution.py:192
  353.2 118.3 %reduce-scatter.13.cloned.1.call-start = ((), (), s32[]{:S(2)}) async-start(), calls=%async_computation.19 | async-start | bytes 737280 | tf_op jit(solution)/shard_map/reduce_scatter | solution.py:274
  353.7 140.5 %reduce-scatter.17.cloned.1.call-start = ((), (), s32[]{:S(2)}) async-start(), calls=%async_computation.21 | async-start | bytes 737280 | tf_op jit(solution)/shard_map/reduce_scatter | solution.py:274
  382.5 135.3 %reduce-scatter.9.cloned.1.call-start = ((), (), s32[]{:S(2)}) async-start(), calls=%async_computation.17 | async-start | bytes 921600 | tf_op jit(solution)/shard_map/reduce_scatter | solution.py:274
  406.0 41.4 %copy-start.52 = (s32[1024]{0:T(1024)S(1)}, s32[1024]{0:T(1024)}, u32[]{:S(2)}) copy-start(s32[1024]{0:T(1024)} %copy-done.51) | copy-start | bytes 12292
  447.5 90.6 %copy-start.12 = (f32[956,768]{1,0:T(8,128)S(1)}, f32[956,768]{1,0:T(8,128)}, u32[]{:S(2)}) copy-start(f32[956,768]{1,0:T(8,128)} %param.37) | copy-start | bytes 8810500
  538.1 7.8 %copy-start.39 = (f32[768,3]{0,1:T(4,128)S(1)}, f32[768,3]{0,1:T(4,128)}, u32[]{:S(2)}) copy-start(f32[768,3]{0,1:T(4,128)} %param.46) | copy-start | bytes 27652
  538.1 7.8 %copy-start.46 = (f32[768,3]{0,1:T(4,128)S(1)}, f32[768,3]{0,1:T(4,128)}, u32[]{:S(2)}) copy-start(f32[768,3]{0,1:T(4,128)} %param.47) | copy-start | bytes 27652
  538.1 8.4 %copy-start.20 = (f32[96,1536]{1,0:T(8,128)S(1)}, f32[96,1536]{1,0:T(8,128)}, u32[]{:S(2)}) copy-start(f32[96,1536]{1,0:T(8,128)} %param.43) | copy-start | bytes 1769476
  538.1 8.4 %copy-start.31 = (f32[96,1536]{1,0:T(8,128)S(1)}, f32[96,1536]{1,0:T(8,128)}, u32[]{:S(2)}) copy-start(f32[96,1536]{1,0:T(8,128)} %param.44) | copy-start | bytes 1769476
  538.1 8.4 %copy-start.32 = (f32[96,1536]{1,0:T(8,128)S(1)}, f32[96,1536]{1,0:T(8,128)}, u32[]{:S(2)}) copy-start(f32[96,1536]{1,0:T(8,128)} %param.45) | copy-start | bytes 1769476
  538.2 8.4 %copy-start.33 = (bf16[96,768]{1,0:T(8,128)(2,1)S(1)}, bf16[96,768]{1,0:T(8,128)(2,1)}, u32[]{:S(2)}) copy-start(bf16[96,768]{1,0:T(8,128)(2,1)} %reduce-scatter.13.cloned.1.call-done) | copy-start | bytes 442372
  538.2 8.4 %copy-start.34 = (bf16[96,768]{1,0:T(8,128)(2,1)S(1)}, bf16[96,768]{1,0:T(8,128)(2,1)}, u32[]{:S(2)}) copy-start(bf16[96,768]{1,0:T(8,128)(2,1)} %reduce-scatter.17.cloned.1.call-done) | copy-start | bytes 442372
  (47 other events, 163.4 us)
Sparse Core Ops, SparseCore 0:
  11.4 96.2 all-gather.2
  111.1 83.2 all-gather.4
  256.7 52.4 reduce-scatter.10
  312.9 69.5 reduce-scatter.14
  385.8 61.5 reduce-scatter.6
  449.6 21.8 reduce-scatter.12
  473.8 20.4 reduce-scatter.16
  496.6 21.1 reduce-scatter.8

commit v2 on v1

v2 whole, which is shorter than its diff:
```python
import jax
import jax.numpy as jnp
from jax import lax
from jax.experimental import pallas as pl
from jax.experimental.pallas import tpu as pltpu
from jax.sharding import PartitionSpec as P

MODEL_WIDTH = 768
HEADS = 12
FF = 3072
L = 128
LEVELS = 4
STEP = 10


highest_precision = lax.Precision.HIGHEST
norm_epsilon = 1e-05
learn_rate = 0.05
gain_rate = 0.5
beta_one = 0.9
beta_two = 0.999
adam_epsilon = 1e-08
weight_decay = 0.01
clip_bound = 1.0


def norm_forward(values, gain_row, shift_row):
    center = values - jnp.mean(values, axis=-1, keepdims=True)
    spread = jnp.mean(center * center, axis=-1, keepdims=True)
    inverse = lax.rsqrt(spread + norm_epsilon)
    unit = center * inverse
    return (unit * gain_row + shift_row, unit, inverse)


def norm_backward(grad, unit, inverse, gain_row):
    scaled = grad * gain_row
    level = jnp.mean(scaled, axis=-1, keepdims=True)
    along = jnp.mean(scaled * unit, axis=-1, keepdims=True)
    grad_values = inverse * (scaled - level - unit * along)
    return (grad_values, jnp.sum(grad * unit, axis=0), jnp.sum(grad, axis=0))


gelu_rate = 0.7978845608028654
gelu_cube = 0.044715


def gelu_forward(before):
    bend = jnp.tanh(gelu_rate * (before + gelu_cube * before * before * before))
    return 0.5 * before * (1.0 + bend)


def gelu_slope(before):
    bend = jnp.tanh(gelu_rate * (before + gelu_cube * before * before * before))
    inner = gelu_rate * (1.0 + 3.0 * gelu_cube * before * before)
    return 0.5 * (1.0 + bend) + 0.5 * before * (1.0 - bend * bend) * inner


def adam_update(weight, gradient, first_moment, second, decay_rate, rate):
    first_new = beta_one * first_moment + (1.0 - beta_one) * gradient
    second_new = beta_two * second + (1.0 - beta_two) * gradient * gradient
    direction = (
        first_new
        / (1.0 - beta_one**STEP)
        / (jnp.sqrt(second_new / (1.0 - beta_two**STEP)) + adam_epsilon)
    )
    return (weight - rate * (direction + decay_rate * weight), first_new, second_new)


def contract_last(left, right):
    return lax.dot_general(
        left, right, (((1,), (1,)), ((), ())), preferred_element_type=jnp.float32
    )


def contract_first(left, right):
    return lax.dot_general(
        left, right, (((0,), (0,)), ((), ())), preferred_element_type=jnp.float32
    )


def flip(block, bit):
    size = lax.axis_size("dp")
    return lax.ppermute(block, "dp", [(i, i ^ bit) for i in range(size)])


def add_low(*terms):
    return sum(term.astype(jnp.float32) for term in terms).astype(jnp.bfloat16)


piece_codes = (0, 2, 6, 4, 1, 3, 7, 5)


def gather_near(own):
    return own, flip(own, 2), flip(own, 4)


def gather_far(own, along_x, along_y):
    half = own.shape[0] // 2
    far_top, far_low = flip(along_x[:half], 4), flip(along_y[half:], 2)
    mine = [own, along_x, far_top, far_low, along_y]
    return mine + [flip(block, 1) for block in mine]


def assemble_kernel(place_ref, *refs):
    pieces, full_ref, arrivals = refs[:10], refs[10], refs[11]
    chunk = pieces[0].shape[0]
    copies = []
    for block, piece in enumerate(pieces):
        code = (0, 2, 6, 6, 4)[block % 5] + block // 5
        at = (place_ref[0] ^ code) * chunk
        if block % 5 == 3:
            at = at + chunk // 2
        at = pl.multiple_of(at, 16)
        copies.append(
            pltpu.make_async_copy(piece, full_ref.at[pl.ds(at, piece.shape[0])], arrivals.at[block])
        )
    for copy in copies:
        copy.start()
    for copy in copies:
        copy.wait()


def assemble(place, pieces):
    chunk, width = pieces[0].shape
    return pl.pallas_call(
        assemble_kernel,
        in_specs=[pl.BlockSpec(memory_space=pltpu.SMEM)] + [pl.BlockSpec(memory_space=pl.ANY)] * len(pieces),
        out_specs=pl.BlockSpec(memory_space=pltpu.VMEM),
        out_shape=jax.ShapeDtypeStruct((8 * chunk, width), pieces[0].dtype),
        compiler_params=pltpu.CompilerParams(vmem_limit_bytes=VMEM_BYTES),
        scratch_shapes=[pltpu.SemaphoreType.DMA((len(pieces),))],
        cost_estimate=pl.CostEstimate(flops=0, bytes_accessed=32 * chunk * width, transcendentals=0),
        name="assemble",
    )(place.reshape(1), *pieces)


def partner(index, step):
    size = lax.axis_size("mp")
    return index ^ step if size & (size - 1) == 0 else (index + step) % size


def pass_mp(block, step):
    return lax.ppermute(block, "mp", [(i, partner(i, step)) for i in range(lax.axis_size("mp"))])


def gather_mp(rows):
    return [rows] + [pass_mp(rows, step) for step in range(1, lax.axis_size("mp"))]


def sum_mp(blocks):
    total = blocks[0].astype(jnp.float32)
    for step in range(1, lax.axis_size("mp")):
        total = total + pass_mp(blocks[step], step).astype(jnp.float32)
    return total


def send_first(top, low):
    size = top.shape[0] // 4
    from_x = flip(top[size : 3 * size], 2)
    from_y = flip(low[2 * size :], 4)
    late_y = add_low(top[3 * size :], from_x[size:])
    late_x = add_low(low[size : 2 * size], from_y[:size])
    return top[:size], low[:size], from_x[:size], from_y[size:], late_y, late_x


def send_last(top, low, from_x, from_y, late_y, late_x):
    late_y, late_x = flip(late_y, 4), flip(late_x, 2)
    return add_low(top, from_x, late_y), add_low(low, from_y, late_x)


def together(*values):
    return lax.optimization_barrier(values)


PAIR = 2 * (MODEL_WIDTH // HEADS)
PAIRS = HEADS // 2
BLOCK = 2 * L
VMEM_BYTES = 56 * 1024 * 1024


def dot_nt(left, right):
    return lax.dot_general(
        left, right, (((1,), (1,)), ((), ())), preferred_element_type=jnp.float32
    )


def dot_tn(left, right):
    return lax.dot_general(
        left, right, (((0,), (0,)), ((), ())), preferred_element_type=jnp.float32
    )


def dot_nn(left, right):
    return jnp.dot(left, right, preferred_element_type=jnp.float32)


def both_heads(pair, left_half):
    zero = jnp.zeros_like(pair)
    return jnp.concatenate([jnp.where(left_half, pair, zero), jnp.where(left_half, zero, pair)], axis=0)


def pair_attend(queries, keys, key_bias):
    scores = dot_nt(queries, keys) * (MODEL_WIDTH // HEADS) ** (-0.5) + key_bias
    raised = jnp.exp(scores - jnp.max(scores, axis=-1, keepdims=True))
    return raised * (1.0 / jnp.sum(raised, axis=-1, keepdims=True))


def attention_kernel(
    length_ref, level_ref, embed_ref, qkv_ref, out_ref, gains_ref, project_ref, mixture_ref, first_ref, normed_ref
):
    step = pl.program_id(0)
    normed, _, _ = norm_forward(embed_ref[...].astype(jnp.float32), gains_ref[0:1], gains_ref[1:2])
    normed_low = normed.astype(jnp.bfloat16)
    normed_ref[...] = normed_low
    for part in range(3):
        columns = slice(part * MODEL_WIDTH, (part + 1) * MODEL_WIDTH)
        project_ref[:, columns] = dot_nt(normed_low, qkv_ref[columns]).astype(jnp.bfloat16)
    lane = lax.broadcasted_iota(jnp.int32, (L, PAIR), 1)
    left_half = lane < PAIR // 2
    for seq in range(BLOCK // L):
        rows = slice(seq * L, (seq + 1) * L)
        length = length_ref[step * (BLOCK // L) + seq]
        heads = level_ref[step * (BLOCK // L) + seq] * (HEADS // LEVELS)
        key_bias = jnp.where(lax.broadcasted_iota(jnp.int32, (1, L), 1) < length, 0.0, -1000000000.0)
        for pair in range(PAIRS):
            at = pair * PAIR
            queries = both_heads(project_ref[rows, at : at + PAIR], left_half)
            keys = project_ref[rows, MODEL_WIDTH + at : MODEL_WIDTH + at + PAIR]
            values = project_ref[rows, 2 * MODEL_WIDTH + at : 2 * MODEL_WIDTH + at + PAIR]
            attend = pair_attend(queries, keys, key_bias).astype(jnp.bfloat16)
            mixed = dot_nn(attend, values)
            mixed = jnp.where(left_half, mixed[:L], mixed[L:])
            head = 2 * pair + (lane >= PAIR // 2).astype(jnp.int32)
            mixture_ref[rows, at : at + PAIR] = jnp.where(head < heads, mixed, 0.0).astype(jnp.bfloat16)
    first_ref[...] = normed + dot_nn(mixture_ref[...], out_ref[...])


def whole(shape):
    return pl.BlockSpec(shape, lambda step: (0,) * len(shape))


def by_rows(width):
    return pl.BlockSpec((BLOCK, width), lambda step: (step, 0))


def attention_layer(own_lengths, own_levels, embedded, dense_full, norm_gains):
    rows = embedded.shape[0]
    low = jnp.bfloat16
    return pl.pallas_call(
        attention_kernel,
        grid=(rows // BLOCK,),
        in_specs=[
            pl.BlockSpec(memory_space=pltpu.SMEM),
            pl.BlockSpec(memory_space=pltpu.SMEM),
            by_rows(MODEL_WIDTH),
            whole((3 * MODEL_WIDTH, MODEL_WIDTH)),
            pl.BlockSpec((MODEL_WIDTH, MODEL_WIDTH), lambda step: (3, 0)),
            whole((6, MODEL_WIDTH)),
        ],
        out_specs=[by_rows(3 * MODEL_WIDTH), by_rows(MODEL_WIDTH), by_rows(MODEL_WIDTH), by_rows(MODEL_WIDTH)],
        out_shape=[
            jax.ShapeDtypeStruct((rows, 3 * MODEL_WIDTH), low),
            jax.ShapeDtypeStruct((rows, MODEL_WIDTH), low),
            jax.ShapeDtypeStruct((rows, MODEL_WIDTH), jnp.float32),
            jax.ShapeDtypeStruct((rows, MODEL_WIDTH), low),
        ],
        compiler_params=pltpu.CompilerParams(vmem_limit_bytes=VMEM_BYTES),
        cost_estimate=pl.CostEstimate(
            flops=rows * MODEL_WIDTH * MODEL_WIDTH * 10, bytes_accessed=rows * MODEL_WIDTH * 16, transcendentals=0
        ),
        name="attention_layer",
    )(own_lengths, own_levels, embedded, dense_full, dense_full, norm_gains)


def attention_back_kernel(
    start,
    length_ref,
    level_ref,
    grad_ref,
    first_ref,
    project_ref,
    embed_ref,
    teacher_ref,
    qkv_ref,
    out_ref,
    gains_ref,
    grad_project_ref,
    grad_att_ref,
    grad_embed_ref,
    sums_ref,
    grad_mixture_ref,
):
    turn = pl.program_id(0)
    step = turn + start
    low = jnp.bfloat16
    _, unit_one, inverse_one = norm_forward(first_ref[...], gains_ref[2:3], gains_ref[3:4])
    grad_first, gain_one, shift_one = norm_backward(grad_ref[...], unit_one, inverse_one, gains_ref[2:3])
    grad_att = grad_first.astype(low)
    grad_att_ref[...] = grad_att
    grad_mixture_ref[...] = dot_nt(grad_att, out_ref[...]).astype(low)
    lane = lax.broadcasted_iota(jnp.int32, (L, PAIR), 1)
    left_half = lane < PAIR // 2
    scaling = (MODEL_WIDTH // HEADS) ** (-0.5)
    usable = []
    for seq in range(BLOCK // L):
        rows = slice(seq * L, (seq + 1) * L)
        length = length_ref[step * (BLOCK // L) + seq]
        heads = level_ref[step * (BLOCK // L) + seq] * (HEADS // LEVELS)
        usable.append((lax.broadcasted_iota(jnp.int32, (L, 1), 0) < length).astype(jnp.float32))
        key_bias = jnp.where(lax.broadcasted_iota(jnp.int32, (1, L), 1) < length, 0.0, -1000000000.0)
        for pair in range(PAIRS):
            at = pair * PAIR
            queries = both_heads(project_ref[rows, at : at + PAIR], left_half)
            keys = project_ref[rows, MODEL_WIDTH + at : MODEL_WIDTH + at + PAIR]
            values = project_ref[rows, 2 * MODEL_WIDTH + at : 2 * MODEL_WIDTH + at + PAIR]
            attend = pair_attend(queries, keys, key_bias)
            head = 2 * pair + (lane >= PAIR // 2).astype(jnp.int32)
            mixture = grad_mixture_ref[rows, at : at + PAIR]
            mixture = both_heads(jnp.where(head < heads, mixture, jnp.zeros_like(mixture)), left_half)
            grad_values = dot_tn(attend.astype(low), mixture)
            grad_attend = dot_nt(mixture, values)
            level = jnp.sum(grad_attend * attend, axis=-1, keepdims=True)
            grad_scores = (attend * (grad_attend - level)).astype(low)
            grad_queries = dot_nn(grad_scores, keys) * scaling
            grad_queries = jnp.where(left_half, grad_queries[:L], grad_queries[L:])
            grad_keys = dot_tn(grad_scores, queries) * scaling
            grad_project_ref[rows, at : at + PAIR] = grad_queries.astype(low)
            grad_project_ref[rows, MODEL_WIDTH + at : MODEL_WIDTH + at + PAIR] = grad_keys.astype(low)
            grad_project_ref[rows, 2 * MODEL_WIDTH + at : 2 * MODEL_WIDTH + at + PAIR] = grad_values.astype(low)
    normed, unit_base, inverse_base = norm_forward(
        embed_ref[...].astype(jnp.float32), gains_ref[0:1], gains_ref[1:2]
    )
    usable = jnp.concatenate(usable, axis=0)
    gap = usable * (normed - teacher_ref[...].astype(jnp.float32))
    grad_normed = grad_first + 2.0 * gap + dot_nn(grad_project_ref[...], qkv_ref[...])
    grad_embed, gain_base, shift_base = norm_backward(grad_normed, unit_base, inverse_base, gains_ref[0:1])
    grad_embed_ref[...] = grad_embed.astype(low)

    @pl.when(turn == 0)
    def _():
        sums_ref[...] = jnp.zeros_like(sums_ref)

    for row, value in enumerate((gain_base, shift_base, gain_one, shift_one, jnp.sum(gap * gap, axis=0))):
        sums_ref[row : row + 1] += value[None]


def attention_backward(start, steps, scalars, arrays, weights, before):
    rows = arrays[0].shape[0]
    low = jnp.bfloat16

    def at_rows(width):
        return pl.BlockSpec((BLOCK, width), lambda step: (step + start, 0))

    widths = (MODEL_WIDTH, MODEL_WIDTH, 3 * MODEL_WIDTH, MODEL_WIDTH, MODEL_WIDTH)
    count = len(before)

    def body(length_ref, level_ref, *refs):
        attention_back_kernel(start, length_ref, level_ref, *refs[:8], *refs[8 + count :])

    return pl.pallas_call(
        body,
        grid=(steps,),
        in_specs=[pl.BlockSpec(memory_space=pltpu.SMEM)] * 2
        + [at_rows(width) for width in widths]
        + [
            whole((3 * MODEL_WIDTH, MODEL_WIDTH)),
            pl.BlockSpec((MODEL_WIDTH, MODEL_WIDTH), lambda step: (3, 0)),
            whole((6, MODEL_WIDTH)),
        ]
        + [pl.BlockSpec(memory_space=pl.ANY)] * count,
        out_specs=[at_rows(3 * MODEL_WIDTH), at_rows(MODEL_WIDTH), at_rows(MODEL_WIDTH), whole((8, MODEL_WIDTH))],
        out_shape=[
            jax.ShapeDtypeStruct((rows, 3 * MODEL_WIDTH), low),
            jax.ShapeDtypeStruct((rows, MODEL_WIDTH), low),
            jax.ShapeDtypeStruct((rows, MODEL_WIDTH), low),
            jax.ShapeDtypeStruct((8, MODEL_WIDTH), jnp.float32),
        ],
        input_output_aliases={10 + place: place for place in range(count)},
        scratch_shapes=[pltpu.VMEM((BLOCK, MODEL_WIDTH), low)],
        compiler_params=pltpu.CompilerParams(vmem_limit_bytes=VMEM_BYTES),
        cost_estimate=pl.CostEstimate(
            flops=steps * BLOCK * MODEL_WIDTH * MODEL_WIDTH * 40,
            bytes_accessed=steps * BLOCK * MODEL_WIDTH * 24,
            transcendentals=0,
        ),
        name="attention_backward",
    )(*scalars, *arrays, *weights, *before)


FFN_CHUNK = 768


def split_low(value):
    upper = value.astype(jnp.bfloat16)
    return jnp.concatenate([upper, (value - upper.astype(jnp.float32)).astype(jnp.bfloat16)], axis=0)


def ffn_kernel(sizes, length_ref, level_ref, first_ref, teacher_ref, pool_ref, class_ref, logits_ref, gains_ref, index_ref, *refs):
    pieces = refs[: len(sizes)]
    (hidden_ref, grad_before_ref, grad_feed_ref, middle_ref, grad_middle_ref, grad_pool_ref, grad_class_ref, sums_ref) = refs[
        len(sizes) : len(sizes) + 8
    ]
    weights_ref, slope_ref, unit_ref, inverse_ref, pooled_rows_ref, grad_rows_ref, arrivals = refs[len(sizes) + 8 :]
    step = pl.program_id(0)
    blocks = slope_ref.shape[0]
    seqs = BLOCK // L
    low = jnp.bfloat16
    row = lax.broadcasted_iota(jnp.int32, (BLOCK, 1), 0)

    def copies():
        at = 0
        for place, size in enumerate(sizes):
            yield pltpu.make_async_copy(pieces[place], weights_ref.at[pl.ds(at, size)], arrivals.at[place])
            at += size

    @pl.when(step == 0)
    def _():
        for copy in copies():
            copy.start()
        for copy in copies():
            copy.wait()
        sums_ref[...] = jnp.zeros_like(sums_ref)

    @pl.when(step < blocks)
    def _():
        middle, _, _ = norm_forward(first_ref[...], gains_ref[2:3], gains_ref[3:4])
        middle_low = middle.astype(low)
        middle_ref[...] = middle_low
        limit = jnp.full((BLOCK, 1), level_ref[step * seqs])
        for seq in range(1, seqs):
            limit = jnp.where(row >= seq * L, level_ref[step * seqs + seq], limit)
        limit = limit * (FF // LEVELS)
        for at in range(0, FF, FFN_CHUNK):
            columns = slice(at, at + FFN_CHUNK)
            before = dot_nt(middle_low, weights_ref[columns, :MODEL_WIDTH])
            square = before * before
            bend = jnp.tanh(before * (gelu_rate + gelu_rate * gelu_cube * square))
            rise = 0.5 + 0.5 * bend
            value = before * rise
            slope = rise + (0.5 * before) * (1.0 - bend * bend) * (gelu_rate + 3.0 * gelu_rate * gelu_cube * square)
            on = index_ref[:, columns] < limit
            hidden_ref[:, columns] = jnp.where(on, value, 0.0).astype(low)
            slope_ref[step, :, columns] = jnp.where(on, slope, 0.0).astype(low)
        feed = dot_nn(hidden_ref[...], weights_ref[:, MODEL_WIDTH:])
        output, unit, inverse = norm_forward(middle + feed, gains_ref[4:5], gains_ref[5:6])
        unit_ref[step] = unit
        inverse_ref[step] = inverse
        for seq in range(seqs):
            pooled_rows_ref[pl.ds(step * seqs + seq, 1), :] = output[seq * L : seq * L + 1]

    @pl.when(step == blocks)
    def _():
        first_low = pooled_rows_ref[...].astype(low)
        pooled = jnp.tanh(dot_nn(first_low, pool_ref[...]))
        pooled_low = pooled.astype(low)
        gap = dot_nn(pooled_low, class_ref[...]) - logits_ref[...]
        grad_logits = split_low(2.0 * L * gap)
        rows = gap.shape[0]
        grad_class_ref[...] = dot_tn(jnp.concatenate([pooled_low, pooled_low], axis=0), grad_logits)
        grad_pooled = dot_nt(grad_logits, class_ref[...])
        grad_inner = split_low((grad_pooled[:rows] + grad_pooled[rows:]) * (1.0 - pooled * pooled))
        grad_pool_ref[...] = dot_tn(jnp.concatenate([first_low, first_low], axis=0), grad_inner).astype(low)
        grad_rows = dot_nt(grad_inner, pool_ref[...])
        grad_rows_ref[...] = grad_rows[:rows] + grad_rows[rows:]
        sums_ref[3:4, : gap.shape[1]] += L * jnp.sum(gap * gap, axis=0, keepdims=True)

    @pl.when(step > blocks)
    def _():
        block = step - blocks - 1
        unit = unit_ref[block]
        reach = jnp.full((BLOCK, 1), length_ref[block * seqs])
        pooled_grad = jnp.where(row == 0, grad_rows_ref[pl.ds(block * seqs, 1), :], 0.0)
        for seq in range(1, seqs):
            reach = jnp.where(row >= seq * L, length_ref[block * seqs + seq] + seq * L, reach)
            pooled_grad = jnp.where(row == seq * L, grad_rows_ref[pl.ds(block * seqs + seq, 1), :], pooled_grad)
        output = unit * gains_ref[4:5] + gains_ref[5:6]
        gap = jnp.where(row < reach, output - teacher_ref[...].astype(jnp.float32), 0.0)
        grad_second, gain, shift = norm_backward(2.0 * gap + pooled_grad, unit, inverse_ref[block], gains_ref[4:5])
        grad_feed = grad_second.astype(low)
        grad_feed_ref[...] = grad_feed
        for at in range(0, FF, FFN_CHUNK):
            columns = slice(at, at + FFN_CHUNK)
            grad_hidden = dot_nt(grad_feed, weights_ref[columns, MODEL_WIDTH:])
            grad_before_ref[:, columns] = (grad_hidden * slope_ref[block, :, columns].astype(jnp.float32)).astype(low)
        grad_middle_ref[...] = grad_second + dot_nn(grad_before_ref[...], weights_ref[:, :MODEL_WIDTH])
        for place, value in enumerate((gain, shift, jnp.sum(gap * gap, axis=0))):
            sums_ref[place : place + 1] += value[None]


def ffn_layer(scalars, first, teacher, dense_full, class_wide, logits_wide, norm_gains, neuron_index, pieces):
    rows = first.shape[0]
    seqs = rows // L
    blocks = rows // BLOCK
    low = jnp.bfloat16
    sizes = tuple(piece.shape[0] for piece in pieces)

    def going(width):
        return pl.BlockSpec((BLOCK, width), lambda step: (jnp.minimum(step, blocks - 1), 0))

    def coming(width):
        return pl.BlockSpec((BLOCK, width), lambda step: (jnp.maximum(step - blocks - 1, 0), 0))

    return pl.pallas_call(
        lambda *refs: ffn_kernel(sizes, *refs),
        grid=(2 * blocks + 1,),
        in_specs=[
            pl.BlockSpec(memory_space=pltpu.SMEM),
            pl.BlockSpec(memory_space=pltpu.SMEM),
            going(MODEL_WIDTH),
            coming(MODEL_WIDTH),
            pl.BlockSpec((MODEL_WIDTH, MODEL_WIDTH), lambda step: (4, 0)),
            whole(class_wide.shape),
            whole(logits_wide.shape),
            whole((6, MODEL_WIDTH)),
            whole((1, FF)),
        ]
        + [pl.BlockSpec(memory_space=pl.ANY)] * len(sizes),
        out_specs=[
            going(FF),
            coming(FF),
            coming(MODEL_WIDTH),
            going(MODEL_WIDTH),
            coming(MODEL_WIDTH),
            whole((MODEL_WIDTH, MODEL_WIDTH)),
            whole(class_wide.shape),
            whole((8, MODEL_WIDTH)),
        ],
        out_shape=[
            jax.ShapeDtypeStruct((rows, FF), low),
            jax.ShapeDtypeStruct((rows, FF), low),
            jax.ShapeDtypeStruct((rows, MODEL_WIDTH), low),
            jax.ShapeDtypeStruct((rows, MODEL_WIDTH), low),
            jax.ShapeDtypeStruct((rows, MODEL_WIDTH), jnp.float32),
            jax.ShapeDtypeStruct((MODEL_WIDTH, MODEL_WIDTH), low),
            jax.ShapeDtypeStruct(class_wide.shape, jnp.float32),
            jax.ShapeDtypeStruct((8, MODEL_WIDTH), jnp.float32),
        ],
        scratch_shapes=[
            pltpu.VMEM((FF, 2 * MODEL_WIDTH), low),
            pltpu.VMEM((blocks, BLOCK, FF), low),
            pltpu.VMEM((blocks, BLOCK, MODEL_WIDTH), jnp.float32),
            pltpu.VMEM((blocks, BLOCK, 1), jnp.float32),
            pltpu.VMEM((seqs, MODEL_WIDTH), jnp.float32),
            pltpu.VMEM((seqs, MODEL_WIDTH), jnp.float32),
            pltpu.SemaphoreType.DMA((len(sizes),)),
        ],
        compiler_params=pltpu.CompilerParams(vmem_limit_bytes=VMEM_BYTES),
        cost_estimate=pl.CostEstimate(
            flops=rows * MODEL_WIDTH * FF * 16, bytes_accessed=rows * FF * 8, transcendentals=rows * FF
        ),
        name="ffn_layer",
    )(*scalars, first, teacher, dense_full, class_wide, logits_wide, norm_gains, neuron_index, *pieces)


def per_device(
    token_ids,
    replacements,
    replaced,
    lengths,
    widths,
    teacher_embed,
    teacher_hidden,
    teacher_logits,
    embed_table,
    embed_moment,
    embed_square,
    dense_weights,
    dense_moment,
    dense_square,
    feedforward,
    feedforward_moment,
    feedforward_square,
    classifier,
    classifier_moment,
    classifier_square,
    norm_gains,
    norm_moment,
    norm_square,
):
    both = ("dp", "mp")
    mp_count = lax.axis_size("mp")
    mp_index = lax.axis_index("mp")
    n_dev = lax.axis_size("dp") * mp_count
    own_seqs = teacher_logits.shape[0]
    own_rows = own_seqs * L
    table_rows = embed_table.shape[0]
    low = jnp.bfloat16
    by_bits = lax.axis_size("dp") == 8 and mp_count & (mp_count - 1) == 0
    if by_bits:
        dense_steps = gather_mp(dense_weights.astype(low))
        dense_column = jnp.concatenate(
            [lax.select_n(mp_index, *[dense_steps[k ^ z] for z in range(mp_count)]) for k in range(mp_count)],
            axis=0,
        )
    else:
        dense_column = lax.all_gather(dense_weights.astype(low), "mp", axis=0, tiled=True)
    dp_index = lax.axis_index("dp")
    neuron_piece = feedforward.shape[0]
    neuron_slot = jnp.arange(FF)
    if by_bits:
        chunk = neuron_piece * mp_count
        codes = jnp.repeat(jnp.array(piece_codes), chunk, total_repeat_length=FF)
        steps = neuron_slot % chunk // neuron_piece
        neuron_index = (dp_index ^ codes) * chunk + (mp_index ^ steps) * neuron_piece + neuron_slot % neuron_piece
    else:
        neuron_index = neuron_slot
    table_low = embed_table.astype(low)

    depth = -(-(own_rows * 3 // 2) // (n_dev * 16)) * 16
    capacity = depth - 1
    own_start = mp_index * own_seqs
    own_ids = lax.dynamic_slice_in_dim(
        jnp.where(replaced == 1, replacements, token_ids), own_start, own_seqs
    ).reshape(own_rows)
    owner = own_ids // table_rows
    local = own_ids - owner * table_rows
    place = jnp.arange(own_rows)
    first = jnp.min(
        jnp.where(own_ids[:, None] == own_ids[None, :], place[None, :], own_rows), axis=1
    )
    leads = first == place
    slot = jnp.sum(
        (leads[None, :] & (owner[:, None] == owner[None, :]) & (place[None, :] < first[:, None])).astype(
            jnp.int32
        ),
        axis=1,
    )
    deepest = jnp.max(slot)

    def positions(turn):
        rank = slot - turn * capacity
        return jnp.where((rank >= 0) & (rank < capacity), owner * depth + rank, -1)

    def wanted(turn):
        spot = jnp.where(leads, positions(turn), -1)
        hits = spot[:, None] == jnp.arange(n_dev * depth)[None, :]
        rows = jnp.max(jnp.where(hits, local[:, None], -1), axis=0).reshape(n_dev, depth)
        return jnp.where(jnp.arange(depth)[None, :] == capacity, deepest, rows)

    def exchange(blocks):
        return lax.all_to_all(blocks, both, split_axis=0, concat_axis=0)

    def asked_hot(asked):
        flat = jnp.where(jnp.arange(depth)[None, :] < capacity, asked, -1).reshape(-1)
        return (flat[:, None] == jnp.arange(table_rows)[None, :]).astype(low)

    def own_hot(turn):
        return (positions(turn)[:, None] == jnp.arange(n_dev * depth)[None, :]).astype(low)

    def answer(asked, *others):
        rows = jnp.dot(asked_hot(asked), table_low, preferred_element_type=low)
        rows, *others = together(rows.reshape(n_dev, depth, MODEL_WIDTH), *others)
        return exchange(rows).reshape(-1, MODEL_WIDTH), *others

    def place_rows(turn, rows):
        return jnp.dot(own_hot(turn), rows, preferred_element_type=low)

    dense_column, ffn_low = together(dense_column, feedforward.astype(low))
    asked_first = exchange(wanted(0))
    turns = jnp.max(asked_first[:, capacity]) // capacity + 1
    if by_bits:
        ffn_column = jnp.concatenate(gather_mp(ffn_low), axis=0)
        rows_first, ffn_column, *dense_near = answer(asked_first, ffn_column, *gather_near(dense_column))
        ffn_near = gather_near(ffn_column)
        dense_full = assemble(dp_index, gather_far(*dense_near))
        rows_first, dense_full, *ffn_near = together(rows_first, dense_full, *ffn_near)
        ffn_pieces = gather_far(*ffn_near)
    else:
        dense_full = lax.all_gather(dense_column, "dp", axis=0, tiled=True)
        ffn_column = lax.all_gather(ffn_low, "mp", axis=0, tiled=True)
        ffn_pieces = [lax.all_gather(ffn_column, "dp", axis=0, tiled=True)]
        rows_first, = answer(asked_first)
    embedded_low = lax.while_loop(
        lambda state: state[0] < turns,
        lambda state: (
            state[0] + 1,
            state[1] + place_rows(state[0], answer(exchange(wanted(state[0])))[0]),
        ),
        (jnp.int32(1), place_rows(0, rows_first)),
    )[1]

    own_lengths = lax.dynamic_slice_in_dim(lengths, own_start, own_seqs)
    own_levels = lax.dynamic_slice_in_dim(widths, own_start, own_seqs)
    scalars = (own_lengths, own_levels)
    project, head_mixture, first_sum, normed_low = attention_layer(
        own_lengths, own_levels, embedded_low, dense_full, norm_gains
    )
    class_pad = -classifier.shape[1] % 128
    hidden_low, grad_before, grad_feed_low, middle_low, grad_middle, grad_pool_rows, grad_class, ffn_sums = ffn_layer(
        scalars,
        first_sum,
        teacher_hidden.reshape(own_rows, MODEL_WIDTH),
        dense_full,
        jnp.pad(classifier, ((0, 0), (0, class_pad))).astype(low),
        jnp.pad(teacher_logits, ((0, 0), (0, class_pad))),
        norm_gains,
        neuron_index[None, :],
        ffn_pieces,
    )
    grad_class = grad_class[:, : classifier.shape[1]]

    def over_both(rows):
        rows = lax.psum_scatter(rows, "dp", scatter_dimension=0, tiled=True)
        return lax.psum_scatter(rows, "mp", scatter_dimension=0, tiled=True).astype(jnp.float32)

    def weight_sums(left, right):
        half = left.shape[1] // 2
        given = flip(contract_first(left[:, half:], right).astype(low), 1)
        return contract_first(left[:, :half], right).astype(low), given

    def dense_scatter(rows):
        if not by_bits:
            return over_both(rows)
        chunks = rows.reshape(4, 2, rows.shape[0] // 8, rows.shape[1])
        core = dp_index % 2
        place = dp_index // 2
        parts = add_low(
            lax.dynamic_index_in_dim(chunks, core, 1, keepdims=False),
            flip(lax.dynamic_index_in_dim(chunks, 1 - core, 1, keepdims=False), 1),
        )
        half = parts.shape[1] // 2
        parts = [lax.dynamic_index_in_dim(parts, place ^ code, 0, keepdims=False) for code in (0, 1, 3, 2)]
        top = jnp.concatenate([part[:half] for part in parts], axis=0)
        rest = jnp.concatenate([part[half:] for part in parts], axis=0)
        parts = jnp.concatenate(send_last(*send_first(top, rest)), axis=0).reshape(mp_count, -1, rows.shape[1])
        return sum_mp([lax.dynamic_index_in_dim(parts, mp_index ^ step, 0, keepdims=False) for step in range(mp_count)])

    arrays = [
        grad_middle,
        first_sum,
        project,
        embedded_low,
        teacher_embed.reshape(own_rows, MODEL_WIDTH),
    ]
    weights = (dense_full, dense_full, norm_gains)
    blocks = own_rows // BLOCK
    if by_bits:
        down_own, down_given = weight_sums(hidden_low, grad_feed_low)
        up_own, up_given = weight_sums(grad_before, middle_low)
        parts = (add_low(up_own, up_given), add_low(down_own, down_given))
        arrays[0], *parts = together(arrays[0], *parts)
        parts = send_first(*parts)
        before = attention_backward(0, blocks - 2, scalars, arrays, weights, ())
        arrays[0], *flow = together(arrays[0], *before, *parts)
        *before, sums_one = flow[:4]
        parts = send_last(*flow[4:])
        before = attention_backward(blocks - 2, 1, scalars, arrays, weights, before)
        arrays[0], *flow = together(arrays[0], *before, *parts)
        *before, sums_two = flow[:4]
        parts = [part.reshape(mp_count, neuron_piece, MODEL_WIDTH) for part in flow[4:]]
        ffn_grad = sum_mp([jnp.concatenate([part[step] for part in parts], axis=1) for step in range(mp_count)])
        *before, sums_last = attention_backward(blocks - 1, 1, scalars, arrays, weights, before)
        sums = sums_one + sums_two + sums_last
    else:
        ffn_grad = jnp.concatenate(
            [contract_first(grad_before, middle_low), contract_first(hidden_low, grad_feed_low)], axis=1
        ).astype(low)
        ffn_grad = over_both(ffn_grad)
        *before, sums = attention_backward(0, blocks, scalars, arrays, weights, ())
    grad_project, grad_att_low, grad_embed_low = before
    grad_dense = jnp.concatenate(
        [
            contract_first(grad_project, normed_low).astype(low),
            contract_first(head_mixture, grad_att_low).astype(low),
            grad_pool_rows,
        ],
        axis=0,
    )
    grad_embed_low, grad_dense, ffn_grad = together(grad_embed_low, grad_dense, ffn_grad)
    loss_own = jnp.sum(sums[4]) + jnp.sum(ffn_sums[2:4])

    small = jnp.concatenate(
        [
            sums[:4].reshape(-1),
            ffn_sums[:2].reshape(-1),
            grad_class.reshape(-1),
        ]
    )
    share = -(-small.shape[0] // n_dev)
    small_parts = jnp.pad(small, (0, share * n_dev - small.shape[0])).reshape(n_dev, share)
    upper = lax.reduce_precision(small_parts, 8, 7)
    rider = jnp.concatenate([upper, small_parts - upper], axis=1).astype(low)
    rider = jnp.pad(rider, ((0, 0), (0, MODEL_WIDTH - 2 * share)))

    def give_back(turn):
        sums = lax.dot_general(
            own_hot(turn), grad_embed_low, (((0,), (0,)), ((), ())), preferred_element_type=jnp.float32
        )
        return sums.reshape(n_dev, depth, MODEL_WIDTH)

    def collect(asked, returned):
        return lax.dot_general(
            asked_hot(asked),
            returned.reshape(-1, MODEL_WIDTH),
            (((0,), (0,)), ((), ())),
            preferred_element_type=jnp.float32,
        )

    given = give_back(0)
    given = jnp.where(jnp.arange(depth)[None, :, None] == capacity, rider.astype(jnp.float32)[:, None, :], given)
    given = given.astype(low)
    returned = exchange(given)
    dense_grad = dense_scatter(grad_dense)
    table_grad = collect(asked_first, returned)
    table_grad = lax.while_loop(
        lambda state: state[0] < turns,
        lambda state: (
            state[0] + 1,
            state[1]
            + collect(exchange(wanted(state[0])), exchange(give_back(state[0]).astype(low))),
        ),
        (jnp.int32(1), table_grad),
    )[1]
    riders = jnp.sum(returned[:, capacity, : 2 * share].astype(jnp.float32), axis=0)
    small_share = riders[:share] + riders[share:]
    square_sum = (
        jnp.sum(table_grad * table_grad)
        + jnp.sum(dense_grad * dense_grad)
        + jnp.sum(ffn_grad * ffn_grad)
        + jnp.sum(small_share * small_share)
    )
    own_count = jnp.sum(own_lengths).astype(jnp.float32)
    message = jnp.concatenate([small_share, jnp.stack([square_sum, own_count, loss_own])])
    message = jnp.pad(message, (0, -message.shape[0] % 128))
    told = exchange(jnp.broadcast_to(message[None], (n_dev, message.shape[0])))
    scalars = jnp.sum(told[:, share : share + 3], axis=0)
    total_square, token_count, loss_sum = scalars[0], scalars[1], scalars[2]
    small_all = told[:, :share].reshape(-1)
    gains_size = norm_gains.size
    gains_grad = small_all[:gains_size].reshape(norm_gains.shape)
    class_grad = small_all[gains_size : gains_size + classifier.size].reshape(classifier.shape)
    inverse = 1.0 / token_count
    grad_norm = jnp.sqrt(total_square) * inverse
    scaling = inverse * (clip_bound / jnp.maximum(grad_norm, clip_bound))
    table_new = adam_update(
        embed_table, table_grad * scaling, embed_moment, embed_square, weight_decay, learn_rate
    )
    dense_new = adam_update(
        dense_weights, dense_grad * scaling, dense_moment, dense_square, weight_decay, learn_rate
    )
    ffn_new = adam_update(
        feedforward,
        ffn_grad * scaling,
        feedforward_moment,
        feedforward_square,
        weight_decay,
        learn_rate,
    )
    class_new = adam_update(
        classifier,
        class_grad * scaling,
        classifier_moment,
        classifier_square,
        weight_decay,
        learn_rate,
    )
    gains_new = adam_update(
        norm_gains, gains_grad * scaling, norm_moment, norm_square, 0.0, gain_rate
    )
    return (
        loss_sum,
        token_count,
        grad_norm,
        table_new[0],
        table_new[1],
        table_new[2],
        table_new[0].astype(jnp.bfloat16),
        dense_new[0],
        dense_new[1],
        dense_new[2],
        dense_new[0].astype(jnp.bfloat16),
        ffn_new[0],
        ffn_new[1],
        ffn_new[2],
        ffn_new[0].astype(jnp.bfloat16),
        class_new[0],
        class_new[1],
        class_new[2],
        class_new[0].astype(jnp.bfloat16),
        gains_new[0],
        gains_new[1],
        gains_new[2],
    )


def solution(mesh):
    placed = (
        P("dp", None),
        P("dp", None),
        P("dp", None),
        P("dp"),
        P("dp"),
        P(("dp", "mp"), None, None),
        P(("dp", "mp"), None, None),
        P(("dp", "mp"), None),
        P(("dp", "mp"), None),
        P(("dp", "mp"), None),
        P(("dp", "mp"), None),
        P(("dp", "mp"), None),
        P(("dp", "mp"), None),
        P(("dp", "mp"), None),
        P(("dp", "mp"), None),
        P(("dp", "mp"), None),
        P(("dp", "mp"), None),
        P(),
        P(),
        P(),
        P(),
        P(),
        P(),
    )
    return jax.shard_map(
        per_device,
        mesh=mesh,
        in_specs=placed,
        out_specs=(
            P(),
            P(),
            P(),
            P(("dp", "mp"), None),
            P(("dp", "mp"), None),
            P(("dp", "mp"), None),
            P(("dp", "mp"), None),
            P(("dp", "mp"), None),
            P(("dp", "mp"), None),
            P(("dp", "mp"), None),
            P(("dp", "mp"), None),
            P(("dp", "mp"), None),
            P(("dp", "mp"), None),
            P(("dp", "mp"), None),
            P(("dp", "mp"), None),
            P(),
            P(),
            P(),
            P(),
            P(),
            P(),
            P(),
        ),
        check_vma=False,
    )
```

time: 565 us -> 458 us (0.81)
  waiting for transfers between devices: 263 us -> 125 us
  Pallas kernels: 0 us -> 119 us
  matrix products: 135 us -> 42 us
  starting transfers between devices: 14.9 us -> 57.1 us
  between operations: 25.3 us -> 10.9 us
  local copies, waits for them, and re-layouts: 43.9 us -> 32 us
  other arithmetic: 64.6 us -> 57.3 us
    reduce_scatter x6 -> x0, waiting for transfers between devices: 130 us -> none  [the longest x3 65.5 us: scatter_sum(): over_dp = lax.psum_scatter(rows, 'dp', scatter_dimension=0, tiled=True)]
    ppermute x0 -> x41, waiting for transfers between devices: none -> 121 us  [the longest x29 105 us: flip(): return lax.ppermute(block, 'dp', [(i, i ^ bit) for i in range(size)])]
    pallas_call x0 -> x6, Pallas kernels: none -> 119 us  [the longest x1 50.8 us: ffn_layer(): pl.pallas_call(lambda *refs: ffn_kernel(sizes, *refs), grid=(2 * blocks +...]
    dot_general x22 -> x2, matrix products: 103 us -> 8.2 us  [the longest x1 4.2 us: answer(): rows = jnp.dot(asked_hot(asked), table_low, preferred_element_type=low)]
    all_to_all x3, waiting for transfers between devices: 94.5 us -> 3.86 us  [exchange(): return lax.all_to_all(blocks, both, split_axis=0, concat_axis=0)]
    ppermute x0 -> x41, starting transfers between devices: none -> 39.6 us  [the longest x12 20.6 us: pass_mp(): lax.ppermute(block, 'mp', [(i, partner(i, step)) for i in range(lax.axis_...]
    all_gather x2 -> x0, waiting for transfers between devices: 37.4 us -> none  [the longest x1 37.4 us: per_device(): ffn_full = lax.all_gather(feedforward.astype(low), both, axis=0, tiled=True)]
    another operation x9 -> x1, local copies, waits for them, and re-layouts: 9.39 us -> 0.18 us  [the longest x1 9.31 us: attention_backward(): stacked = jnp.stack([grad_queries, grad_keying, grad_values], axis=2)]
  transfers between devices with their start and end apart: 11 -> 44, of which waited for: 9 -> 16; matrix products, arithmetic and copies ran while one was open for 28% -> 19% of each run, Pallas kernels for 0% -> 15%
where the time goes in v2:
time: 458 us; the launch traced here: 455 us
  waiting for transfers between devices  125 us (27%)
  Pallas kernels  119 us (26%)
  other arithmetic  57.3 us (13%)
  starting transfers between devices  57.1 us (12%)
  matrix products  42 us (9%)
  local copies, waits for them, and re-layouts  32 us (7%)
  blocking collectives  11 us (2%)
  between operations  10.9 us (2%)
    ppermute x29, waiting for transfers between devices, flip(): return lax.ppermute(block, 'dp', [(i, i ^ bit) for i in range(size)])  105 us
    pallas_call x1, Pallas kernels, ffn_layer(): pl.pallas_call(lambda *refs: ffn_kernel(sizes, *refs), grid=(2 * blocks +...  50.8 us
    pallas_call x3, Pallas kernels, attention_backward(): pl.pallas_call(body, grid=(steps,), in_specs=[pl.BlockSpec(memory_space=p...  46.8 us
    dot_general x6, matrix products, contract_first(): lax.dot_general(left, right, (((0,), (0,)), ((), ())), preferred_element_...  22.4 us
    ppermute x12, starting transfers between devices, pass_mp(): lax.ppermute(block, 'mp', [(i, partner(i, step)) for i in range(lax.axis_...  20.6 us
    ppermute x29, starting transfers between devices, flip(): return lax.ppermute(block, 'dp', [(i, i ^ bit) for i in range(size)])  19 us
    all_to_all x3, starting transfers between devices, exchange(): return lax.all_to_all(blocks, both, split_axis=0, concat_axis=0)  17.5 us
    pallas_call x1, Pallas kernels, attention_layer(): pl.pallas_call(attention_kernel, grid=(rows // BLOCK,), in_specs=[pl.Bloc...  16.1 us
  transfers between devices with their start and end apart: 44, of which 16 were waited for; matrix products, arithmetic and copies ran while one was open for 19% of the time, Pallas kernels for 15%

profile of v2, /device:TPU:0, one launch (start us, length us, event | category | flops | bytes accessed | tf_op | source)
XLA Modules:
  0.0 454.7 jit_solution(3654929231755723427)
XLA Ops:
  1.7 3.1 collective-permute-start
  13.6 6.1 %all-to-all-start.4 = ((s32[32,1,48]{2,1,0:T(1,128)}), s32[32,1,48]{2,1,0:T(1,128)S(1)}, u32[]{:S(2)}, u32[]{:S(2)}) async-start(s32[32,1,48]{2,1,0:T(1,128)} %bitcast.5), calls=%async_computation.4 | async-start | bytes 32768 | tf_op jit(solution)/shard_map/all_to_all | solution.py:641
  22.9 3.9 all-to-all-done.4
  33.9 4.2 fusion.12
  38.1 4.1 collective-permute-done.3
  42.2 10.2 %collective-permute-done.4 = bf16[96,1536]{1,0:T(8,128)(2,1)S(1)} collective-permute-done((bf16[96,1536]{1,0:T(8,128)(2,1)S(1)}, bf16[96,1536]{1,0:T(8,128)(2,1)S(1)}, u32[]{:S(2)}, u32[]{:S(2)}) %collective-permute-start.4) | collective-permute-done | bytes 294944 | tf_op jit(solution)/shard_map/ppermute | solution.py:143
  55.2 6.4 %all-to-all-start.5 = ((bf16[32,48,768]{2,1,0:T(8,128)(2,1)}), bf16[32,48,768]{2,1,0:T(8,128)(2,1)S(1)}, u32[]{:S(2)}, u32[]{:S(2)}) async-start(bf16[32,48,768]{2,1,0:T(8,128)(2,1)} %bitcast.117), calls=%async_computation.5 | async-start | bytes 4718592 | tf_op jit(solution)/shard_map/all_to_all | solution.py:641
  67.8 24.1 %collective-permute-done.8.refs_2_ = bf16[240,768]{1,0:T(8,128)(2,1)} collective-permute-done((bf16[240,768]{1,0:T(8,128)(2,1)S(1)}, bf16[240,768]{1,0:T(8,128)(2,1)}, u32[]{:S(2)}, u32[]{:S(2)}) %collective-permute-start.8) | collective-permute-done | bytes 368672 | tf_op jit(solution)/shard_map/ppermute | solution.py:83
  100.3 5.2 %assemble.1.qkv_ref.out_ref.refs_4_.refs_5_.refs_6_ = bf16[3840,768]{1,0:T(8,128)(2,1)} custom-call(s32[1]{0:T(128)} %bitcast.8.place_ref, bf16[480,768]{1,0:T(8,128)(2,1)} %copy-done.11, bf16[480,768]{1,0:T(8,128)(2,1)} %copy-done.13, bf16[240,768]{1,0:T(8,128)(2,1)} %collective-permute-done.8.refs_2_, bf16[240,768]{1,0:T(8,128)(2,1)} %collective-permute-done.9.refs_3_, ...), custom_call_target="tpu_custom_call" | custom-call | bytes 11796480 | tf_op jit(solution)/shard_map/assemble/pallas_call | solution.py:125
  105.5 17.8 %collective-permute-done.15.refs_10_ = bf16[384,1536]{1,0:T(8,128)(2,1)} collective-permute-done((bf16[384,1536]{1,0:T(8,128)(2,1)}, bf16[384,1536]{1,0:T(8,128)(2,1)}, u32[]{:S(2)}, u32[]{:S(2)}) %collective-permute-start.15) | collective-permute-done | bytes 1179680 | tf_op jit(solution)/shard_map/ppermute | solution.py:83
  131.5 4.0 fusion.14
  135.5 4.9 %collective-permute-done.17.refs_11_ = bf16[192,1536]{1,0:T(8,128)(2,1)} collective-permute-done((bf16[192,1536]{1,0:T(8,128)(2,1)}, bf16[192,1536]{1,0:T(8,128)(2,1)}, u32[]{:S(2)}, u32[]{:S(2)}) %collective-permute-start.17) | collective-permute-done | bytes 589856 | tf_op jit(solution)/shard_map/ppermute | solution.py:83
  142.8 16.1 %attention_layer.1 = (bf16[1024,2304]{1,0:T(8,128)(2,1)}, bf16[1024,768]{1,0:T(8,128)(2,1)}, f32[1024,768]{1,0:T(8,128)}, bf16[1024,768]{1,0:T(8,128)(2,1)}) custom-call(s32[8]{0:T(128)} %get-tuple-element.426.length_ref.refs_0_, s32[8]{0:T(128)} %dynamic_slice.43.level_ref.refs_1_, bf16[1024,768]{1,0:T(8,128)(2,1)} %get-tuple-element.198.embed_ref.refs_3_, ...), custom_call_target="tpu_custom_call" | custom-call | flops 6039797760 | bytes 12582912 | tf_op jit(solution)/shard_map/attention_layer/pallas_call | solution.py:249
  159.7 50.8 %ffn_layer.1 = (bf16[1024,3072]{1,0:T(8,128)(2,1)}, bf16[1024,3072]{1,0:T(8,128)(2,1)}, bf16[1024,768]{1,0:T(8,128)(2,1)}, bf16[1024,768]{1,0:T(8,128)(2,1)}, f3...) custom-call(s32[8]{0:T(128)} %get-tuple-element.426.length_ref.refs_0_, ...), custom_call_target="tpu_custom_call" | custom-call | flops 38654705664 | bytes 25165824 | tf_op jit(solution)/shard_map/ffn_layer/pallas_call | solution.py:503
  210.6 5.2 %convolution_convert_fusion.1 = bf16[1536,768]{1,0:T(8,128)(2,1)S(1)} fusion(bf16[1024,768]{1,0:T(8,128)(2,1)} %get-tuple-element.208, bf16[1024,3072]{1,0:T(8,128)(2,1)} %get-tuple-element.207), kind=kOutput, calls=%fused_computation.51 | convolution fusion | flops 2417098752 | bytes 7077888 | tf_op jit(solution)/shard_map/dot_general | solution.py:76
  232.7 21.7 %attention_backward.3 = (bf16[1024,2304]{1,0:T(8,128)(2,1)}, bf16[1024,768]{1,0:T(8,128)(2,1)}, bf16[1024,768]{1,0:T(8,128)(2,1)}, f32[8,768]{1,0:T(8,128)}) custom-call(s32[8]{0:T(128)} %get-tuple-element.426.length_ref.refs_0_, s32[8]{0:T(128)} %dynamic_slice.43.level_ref.refs_1_, f32[1024,768]{1,0:T(8,128)} %get-tuple-element.233.refs_0_, ...), custom_call_target="tpu_custom_call" | custom-call | flops 12079595520 | bytes 9437184 | tf_op jit(solution)/shard_map/attention_backward/pallas_call | solution.py:360
  254.5 3.5 collective-permute-done.26
  267.8 12.3 %attention_backward.4 = (bf16[1024,2304]{1,0:T(8,128)(2,1)}, bf16[1024,768]{1,0:T(8,128)(2,1)}, bf16[1024,768]{1,0:T(8,128)(2,1)}, f32[8,768]{1,0:T(8,128)}) custom-call(s32[8]{0:T(128)} %get-tuple-element.426.length_ref.refs_0_, s32[8]{0:T(128)} %dynamic_slice.43.level_ref.refs_1_, ...), custom_call_target="tpu_custom_call", output_to_operand_aliasing={{0}: (10, {}), {1}: (11, {}), {2}: (12, {})} | custom-call | flops 6039797760 | bytes 4718592 | tf_op jit(solution)/shard_map/attention_backward/pallas_call | solution.py:360
  286.7 12.7 %attention_backward.5 = (bf16[1024,2304]{1,0:T(8,128)(2,1)}, bf16[1024,768]{1,0:T(8,128)(2,1)}, bf16[1024,768]{1,0:T(8,128)(2,1)}, f32[8,768]{1,0:T(8,128)}) custom-call(s32[8]{0:T(128)} %get-tuple-element.426.length_ref.refs_0_, s32[8]{0:T(128)} %dynamic_slice.43.level_ref.refs_1_, ...), custom_call_target="tpu_custom_call", output_to_operand_aliasing={{0}: (10, {}), {1}: (11, {}), {2}: (12, {})} | custom-call | flops 6039797760 | bytes 4718592 | tf_op jit(solution)/shard_map/attention_backward/pallas_call | solution.py:360
  299.4 6.9 %convolution_convert_fusion = bf16[2304,768]{1,0:T(8,128)(2,1)S(1)} fusion(bf16[1024,2304]{1,0:T(8,128)(2,1)} %get-tuple-element.241, bf16[1024,768]{1,0:T(8,128)(2,1)S(1)} %copy-done.52), kind=kOutput, calls=%fused_computation.42 | convolution fusion | flops 3625648128 | bytes 9830400 | tf_op jit(solution)/shard_map/dot_general | solution.py:76
  317.0 5.1 %fusion.13 = bf16[1536,768]{1,0:T(8,128)(2,1)S(1)} fusion(bf16[1024,768]{1,0:T(8,128)(2,1)} %get-tuple-element.629, s32[1024]{0:T(1024)} %copy-done.40), kind=kOutput, calls=%fused_computation.37 | convolution fusion | flops 2417491968 | bytes 3936256 | tf_op jit(solution)/shard_map/dot_general | solution.py:786
  323.8 5.1 %all-to-all-start.6 = ((bf16[32,48,768]{2,1,0:T(8,128)(2,1)}), bf16[32,48,768]{2,1,0:T(8,128)(2,1)}, u32[]{:S(2)}, u32[]{:S(2)}) async-start(bf16[32,48,768]{2,1,0:T(8,128)(2,1)} %select_convert_fusion), calls=%async_computation.6 | async-start | bytes 4718592 | tf_op jit(solution)/shard_map/all_to_all | solution.py:641
  328.9 3.4 fusion.15
  336.9 31.4 %collective-permute-done.34 = bf16[480,768]{1,0:T(8,128)(2,1)S(1)} collective-permute-done((bf16[480,768]{1,0:T(8,128)(2,1)S(1)}, bf16[480,768]{1,0:T(8,128)(2,1)S(1)}, u32[]{:S(2)}, u32[]{:S(2)}) %collective-permute-start.34) | collective-permute-done | bytes 737312 | tf_op jit(solution)/shard_map/ppermute | solution.py:83
  371.4 11.9 %collective-permute-done.35 = bf16[240,768]{1,0:T(8,128)(2,1)} collective-permute-done((bf16[240,768]{1,0:T(8,128)(2,1)}, bf16[240,768]{1,0:T(8,128)(2,1)}, u32[]{:S(2)}, u32[]{:S(2)}) %collective-permute-start.35) | collective-permute-done | bytes 368672 | tf_op jit(solution)/shard_map/ppermute | solution.py:83
  390.0 5.8 %collective-permute-done.37 = bf16[240,768]{1,0:T(8,128)(2,1)} collective-permute-done((bf16[240,768]{1,0:T(8,128)(2,1)}, bf16[240,768]{1,0:T(8,128)(2,1)}, u32[]{:S(2)}, u32[]{:S(2)}) %collective-permute-start.37) | collective-permute-done | bytes 368672 | tf_op jit(solution)/shard_map/ppermute | solution.py:83
  401.0 4.6 %collective-permute-start.39 = (bf16[120,768]{1,0:T(8,128)(2,1)}, bf16[120,768]{1,0:T(8,128)(2,1)S(1)}, u32[]{:S(2)}, u32[]{:S(2)}) collective-permute-start(bf16[120,768]{1,0:T(8,128)(2,1)} %get-tuple-element.439), channel_id=1, source_target_pairs={{0,2},{1,3},{2,0},{3,1},{4,6},{5,7},{6,4},{7,5},{8,10},{9,11},{10,... | collective-permute-start | bytes 552968 | tf_op jit(solution)/shard_map/ppermute | solution.py:143
  405.6 6.3 %fusion.11 = f32[956,768]{1,0:T(8,128)} fusion(bf16[1536,768]{1,0:T(8,128)(2,1)} %bitcast.14, s32[1536]{0:T(1024)S(1)} %copy-done.38), kind=kOutput, calls=%fused_computation.32 | convolution fusion | flops 2256955392 | bytes 5302272 | tf_op jit(solution)/shard_map/dot_general | solution.py:792
  414.2 3.2 multiply_reduce_fusion
  424.4 11.0 %all_to_all.65 = f32[32,1,256]{2,1,0:T(1,128)S(1)} all-to-all(f32[32,1,256]{2,1,0:T(1,128)S(1)} %broadcast_in_dim.216), channel_id=1, replica_groups=mesh['dp'=8,'mp'=4] {'dp','mp'}, dimensions={0} | all-to-all | bytes 65536 | tf_op jit(solution)/shard_map/all_to_all | solution.py:641
  440.7 3.0 fusion.52
  443.8 7.0 %fusion.56 = (bf16[956,768]{1,0:T(8,128)(2,1)}, f32[956,768]{1,0:T(8,128)}, f32[956,768]{1,0:T(8,128)}, f32[956,768]{1,0:T(8,128)}) fusion(f32[956,768]{1,0:T(8,128)S(1)} %copy-done.1, f32[956,768]{1,0:T(8,128)} %get-tuple-element.249, f32[]{:T(128)S(6)} %mul.340, f32[956,768]{1,0:T(8,128)} %param.39, f32[956,768]{1,0:T(8,128)} %param.40), kind=kLoop, calls=%fused_computation.177 | loop fusion | flops 12481536 | bytes 22026244 | tf_op jit(solution)/shard_map/convert_element_type | solution.py:867
  (284 shorter events, 122.8 us)
Async XLA Ops:
  1.7 26.4 %collective-permute-start = (bf16[120,768]{1,0:T(8,128)(2,1)S(1)}, bf16[120,768]{1,0:T(8,128)(2,1)S(1)}, u32[]{:S(2)}, u32[]{:S(2)}) collective-permute-start(bf16[120,768]{1,0:T(8,128)(2,1)S(1)} %convert_element_type.234), channel_id=1, source_target_pairs={{0,1},{1,0},{2,3},{3,2},{4,5},{5,4},{6,7},{7,6},{8,9},{9,8},{10,11... | collective-permute-start | bytes 552968 | tf_op jit(solution)/shard_map/ppermute | solution.py:143
  4.8 23.4 %collective-permute-start.1 = (bf16[120,768]{1,0:T(8,128)(2,1)S(1)}, bf16[120,768]{1,0:T(8,128)(2,1)S(1)}, u32[]{:S(2)}, u32[]{:S(2)}) collective-permute-start(bf16[120,768]{1,0:T(8,128)(2,1)S(1)} %convert_element_type.234), channel_id=1, source_target_pairs={{0,2},{1,3},{2,0},{3,1},{4,6},{5,7},{6,4},{7,5},{8,10},{9,11},{10,... | collective-permute-start | bytes 552968 | tf_op jit(solution)/shard_map/ppermute | solution.py:143
  7.3 20.8 %collective-permute-start.2 = (bf16[120,768]{1,0:T(8,128)(2,1)S(1)}, bf16[120,768]{1,0:T(8,128)(2,1)S(1)}, u32[]{:S(2)}, u32[]{:S(2)}) collective-permute-start(bf16[120,768]{1,0:T(8,128)(2,1)S(1)} %convert_element_type.234), channel_id=1, source_target_pairs={{0,3},{1,2},{2,1},{3,0},{4,7},{5,6},{6,5},{7,4},{8,11},{9,10},{10,... | collective-permute-start | bytes 552968 | tf_op jit(solution)/shard_map/ppermute | solution.py:143
  28.9 23.5 %collective-permute-start.4 = (bf16[96,1536]{1,0:T(8,128)(2,1)S(1)}, bf16[96,1536]{1,0:T(8,128)(2,1)S(1)}, u32[]{:S(2)}, u32[]{:S(2)}) collective-permute-start(bf16[96,1536]{1,0:T(8,128)(2,1)S(1)} %convert_element_type.235), channel_id=1, source_target_pairs={{0,2},{1,3},{2,0},{3,1},{4,6},{5,7},{6,4},{7,5},{8,10},{9,11},{10,... | collective-permute-start | bytes 884744 | tf_op jit(solution)/shard_map/ppermute | solution.py:143
  30.5 21.9 %collective-permute-start.5 = (bf16[96,1536]{1,0:T(8,128)(2,1)S(1)}, bf16[96,1536]{1,0:T(8,128)(2,1)S(1)}, u32[]{:S(2)}, u32[]{:S(2)}) collective-permute-start(bf16[96,1536]{1,0:T(8,128)(2,1)S(1)} %convert_element_type.235), channel_id=1, source_target_pairs={{0,3},{1,2},{2,1},{3,0},{4,7},{5,6},{6,5},{7,4},{8,11},{9,10},{10,... | collective-permute-start | bytes 884744 | tf_op jit(solution)/shard_map/ppermute | solution.py:143
  32.8 20.7 %collective-permute-start.6 = (bf16[480,768]{1,0:T(8,128)(2,1)S(1)}, bf16[480,768]{1,0:T(8,128)(2,1)S(1)}, u32[]{:S(2)}, u32[]{:S(2)}) collective-permute-start(bf16[480,768]{1,0:T(8,128)(2,1)S(1)} %pad_maximum_fusion.2.refs_0_), channel_id=1, source_target_pairs={{0,8},{4,12},{8,0},{12,4},{16,24},{20,28},{24,16},{28,20},{1,9},{5... | collective-permute-start | bytes 2211848 | tf_op jit(solution)/shard_map/ppermute | solution.py:83
  33.4 20.1 %collective-permute-start.7 = (bf16[480,768]{1,0:T(8,128)(2,1)S(1)}, bf16[480,768]{1,0:T(8,128)(2,1)S(1)}, u32[]{:S(2)}, u32[]{:S(2)}) collective-permute-start(bf16[480,768]{1,0:T(8,128)(2,1)S(1)} %pad_maximum_fusion.2.refs_0_), channel_id=1, source_target_pairs={{0,16},{4,20},{8,24},{12,28},{16,0},{20,4},{24,8},{28,12},{1,17},{... | collective-permute-start | bytes 2211848 | tf_op jit(solution)/shard_map/ppermute | solution.py:83
  55.2 68.1 %all-to-all-start.5 = ((bf16[32,48,768]{2,1,0:T(8,128)(2,1)}), bf16[32,48,768]{2,1,0:T(8,128)(2,1)S(1)}, u32[]{:S(2)}, u32[]{:S(2)}) async-start(bf16[32,48,768]{2,1,0:T(8,128)(2,1)} %bitcast.117), calls=%async_computation.5 | async-start | bytes 4718592 | tf_op jit(solution)/shard_map/all_to_all | solution.py:641
  62.6 29.3 %collective-permute-start.8 = (bf16[240,768]{1,0:T(8,128)(2,1)S(1)}, bf16[240,768]{1,0:T(8,128)(2,1)}, u32[]{:S(2)}, u32[]{:S(2)}) collective-permute-start(bf16[240,768]{1,0:T(8,128)(2,1)S(1)} %slice.208), channel_id=1, source_target_pairs={{0,16},{4,20},{8,24},{12,28},{16,0},{20,4},{24,8},{28,12},{1,17},{... | collective-permute-start | bytes 1105928 | tf_op jit(solution)/shard_map/ppermute | solution.py:83
  65.5 26.4 %collective-permute-start.9 = (bf16[240,768]{1,0:T(8,128)(2,1)S(1)}, bf16[240,768]{1,0:T(8,128)(2,1)}, u32[]{:S(2)}, u32[]{:S(2)}) collective-permute-start(bf16[240,768]{1,0:T(8,128)(2,1)S(1)} %slice.209), channel_id=1, source_target_pairs={{0,8},{4,12},{8,0},{12,4},{16,24},{20,28},{24,16},{28,20},{1,9},{5... | collective-permute-start | bytes 1105928 | tf_op jit(solution)/shard_map/ppermute | solution.py:83
  67.0 56.3 %collective-permute-start.15 = (bf16[384,1536]{1,0:T(8,128)(2,1)}, bf16[384,1536]{1,0:T(8,128)(2,1)}, u32[]{:S(2)}, u32[]{:S(2)}) collective-permute-start(bf16[384,1536]{1,0:T(8,128)(2,1)} %pad_maximum_fusion.1.refs_9_), channel_id=1, source_target_pairs={{0,8},{4,12},{8,0},{12,4},{16,24},{20,28},{24,16},{28,20},{1,9},{5... | collective-permute-start | bytes 3538952 | tf_op jit(solution)/shard_map/ppermute | solution.py:83
  67.5 55.7 %collective-permute-start.16 = (bf16[384,1536]{1,0:T(8,128)(2,1)}, bf16[384,1536]{1,0:T(8,128)(2,1)}, u32[]{:S(2)}, u32[]{:S(2)}) collective-permute-start(bf16[384,1536]{1,0:T(8,128)(2,1)} %pad_maximum_fusion.1.refs_9_), channel_id=1, source_target_pairs={{0,16},{4,20},{8,24},{12,28},{16,0},{20,4},{24,8},{28,12},{1,17},{... | collective-permute-start | bytes 3538952 | tf_op jit(solution)/shard_map/ppermute | solution.py:83
  125.2 15.2 %collective-permute-start.17 = (bf16[192,1536]{1,0:T(8,128)(2,1)}, bf16[192,1536]{1,0:T(8,128)(2,1)}, u32[]{:S(2)}, u32[]{:S(2)}) collective-permute-start(bf16[192,1536]{1,0:T(8,128)(2,1)} %slice.211), channel_id=1, source_target_pairs={{0,16},{4,20},{8,24},{12,28},{16,0},{20,4},{24,8},{28,12},{1,17},{... | collective-permute-start | bytes 1769480 | tf_op jit(solution)/shard_map/ppermute | solution.py:83
  127.8 14.8 %collective-permute-start.18 = (bf16[192,1536]{1,0:T(8,128)(2,1)S(1)}, bf16[192,1536]{1,0:T(8,128)(2,1)}, u32[]{:S(2)}, u32[]{:S(2)}) collective-permute-start(bf16[192,1536]{1,0:T(8,128)(2,1)S(1)} %slice.212), channel_id=1, source_target_pairs={{0,8},{4,12},{8,0},{12,4},{16,24},{20,28},{24,16},{28,20},{1,9},{5... | collective-permute-start | bytes 1769480 | tf_op jit(solution)/shard_map/ppermute | solution.py:83
  130.8 28.1 %collective-permute-start.20 = (bf16[384,1536]{1,0:T(8,128)(2,1)}, bf16[384,1536]{1,0:T(8,128)(2,1)}, u32[]{:S(2)}, u32[]{:S(2)}) collective-permute-start(bf16[384,1536]{1,0:T(8,128)(2,1)} %collective-permute-done.15.refs_10_), channel_id=1, source_target_pairs={{0,4},{4,0},{8,12},{12,8},{16,20},{20,16},{24,28},{28,24},{1,5},{5... | collective-permute-start | bytes 3538952 | tf_op jit(solution)/shard_map/ppermute | solution.py:83
  130.9 28.1 %collective-permute-start.23 = (bf16[384,1536]{1,0:T(8,128)(2,1)}, bf16[384,1536]{1,0:T(8,128)(2,1)}, u32[]{:S(2)}, u32[]{:S(2)}) collective-permute-start(bf16[384,1536]{1,0:T(8,128)(2,1)} %collective-permute-done.16.refs_13_), channel_id=1, source_target_pairs={{0,4},{4,0},{8,12},{12,8},{16,20},{20,16},{24,28},{28,24},{1,5},{5... | collective-permute-start | bytes 3538952 | tf_op jit(solution)/shard_map/ppermute | solution.py:83
  131.4 27.6 %collective-permute-start.19 = (bf16[384,1536]{1,0:T(8,128)(2,1)}, bf16[384,1536]{1,0:T(8,128)(2,1)}, u32[]{:S(2)}, u32[]{:S(2)}) collective-permute-start(bf16[384,1536]{1,0:T(8,128)(2,1)} %pad_maximum_fusion.1.refs_9_), channel_id=1, source_target_pairs={{0,4},{4,0},{8,12},{12,8},{16,20},{20,16},{24,28},{28,24},{1,5},{5... | collective-permute-start | bytes 3538952 | tf_op jit(solution)/shard_map/ppermute | solution.py:83
  140.4 18.5 %collective-permute-start.21 = (bf16[192,1536]{1,0:T(8,128)(2,1)}, bf16[192,1536]{1,0:T(8,128)(2,1)S(1)}, u32[]{:S(2)}, u32[]{:S(2)}) collective-permute-start(bf16[192,1536]{1,0:T(8,128)(2,1)} %collective-permute-done.17.refs_11_), channel_id=1, source_target_pairs={{0,4},{4,0},{8,12},{12,8},{16,20},{20,16},{24,28},{28,24},{1,5},{5... | collective-permute-start | bytes 1769480 | tf_op jit(solution)/shard_map/ppermute | solution.py:83
  142.5 16.4 %collective-permute-start.22 = (bf16[192,1536]{1,0:T(8,128)(2,1)}, bf16[192,1536]{1,0:T(8,128)(2,1)}, u32[]{:S(2)}, u32[]{:S(2)}) collective-permute-start(bf16[192,1536]{1,0:T(8,128)(2,1)} %collective-permute-done.18.refs_12_), channel_id=1, source_target_pairs={{0,4},{4,0},{8,12},{12,8},{16,20},{20,16},{24,28},{28,24},{1,5},{5... | collective-permute-start | bytes 1769480 | tf_op jit(solution)/shard_map/ppermute | solution.py:83
  229.4 28.5 %collective-permute-start.26 = (bf16[768,768]{1,0:T(8,128)(2,1)}, bf16[768,768]{1,0:T(8,128)(2,1)S(1)}, u32[]{:S(2)}, u32[]{:S(2)}) collective-permute-start(bf16[768,768]{1,0:T(8,128)(2,1)} %slice.219), channel_id=1, source_target_pairs={{0,8},{4,12},{8,0},{12,4},{16,24},{20,28},{24,16},{28,20},{1,9},{5... | collective-permute-start | bytes 3538952 | tf_op jit(solution)/shard_map/ppermute | solution.py:83
  231.1 28.4 %collective-permute-start.27 = (bf16[768,768]{1,0:T(8,128)(2,1)}, bf16[768,768]{1,0:T(8,128)(2,1)}, u32[]{:S(2)}, u32[]{:S(2)}) collective-permute-start(bf16[768,768]{1,0:T(8,128)(2,1)} %slice.221), channel_id=1, source_target_pairs={{0,16},{4,20},{8,24},{12,28},{16,0},{20,4},{24,8},{28,12},{1,17},{... | collective-permute-start | bytes 3538952 | tf_op jit(solution)/shard_map/ppermute | solution.py:83
  262.6 17.6 %collective-permute-start.29 = (bf16[384,768]{1,0:T(8,128)(2,1)}, bf16[384,768]{1,0:T(8,128)(2,1)S(1)}, u32[]{:S(2)}, u32[]{:S(2)}) collective-permute-start(bf16[384,768]{1,0:T(8,128)(2,1)} %add_convert_fusion.4), channel_id=1, source_target_pairs={{0,8},{4,12},{8,0},{12,4},{16,24},{20,28},{24,16},{28,20},{1,9},{5... | collective-permute-start | bytes 1769480 | tf_op jit(solution)/shard_map/ppermute | solution.py:83
  267.2 14.5 %collective-permute-start.28 = (bf16[384,768]{1,0:T(8,128)(2,1)}, bf16[384,768]{1,0:T(8,128)(2,1)S(1)}, u32[]{:S(2)}, u32[]{:S(2)}) collective-permute-start(bf16[384,768]{1,0:T(8,128)(2,1)} %add_convert_fusion.5), channel_id=1, source_target_pairs={{0,16},{4,20},{8,24},{12,28},{16,0},{20,4},{24,8},{28,12},{1,17},{... | collective-permute-start | bytes 1769480 | tf_op jit(solution)/shard_map/ppermute | solution.py:83
  282.1 26.2 %collective-permute-start.30 = (bf16[96,1536]{1,0:T(8,128)(2,1)S(1)}, bf16[96,1536]{1,0:T(8,128)(2,1)S(1)}, u32[]{:S(2)}, u32[]{:S(2)}) collective-permute-start(bf16[96,1536]{1,0:T(8,128)(2,1)S(1)} %pad_maximum_fusion.6), channel_id=1, source_target_pairs={{0,1},{1,0},{2,3},{3,2},{4,5},{5,4},{6,7},{7,6},{8,9},{9,8},{10,11... | collective-permute-start | bytes 884744 | tf_op jit(solution)/shard_map/ppermute | solution.py:143
  283.4 24.9 %collective-permute-start.31 = (bf16[96,1536]{1,0:T(8,128)(2,1)S(1)}, bf16[96,1536]{1,0:T(8,128)(2,1)S(1)}, u32[]{:S(2)}, u32[]{:S(2)}) collective-permute-start(bf16[96,1536]{1,0:T(8,128)(2,1)S(1)} %pad_maximum_fusion.7), channel_id=1, source_target_pairs={{0,2},{1,3},{2,0},{3,1},{4,6},{5,7},{6,4},{7,5},{8,10},{9,11},{10,... | collective-permute-start | bytes 884744 | tf_op jit(solution)/shard_map/ppermute | solution.py:143
  286.3 22.0 %collective-permute-start.32 = (bf16[96,1536]{1,0:T(8,128)(2,1)S(1)}, bf16[96,1536]{1,0:T(8,128)(2,1)S(1)}, u32[]{:S(2)}, u32[]{:S(2)}) collective-permute-start(bf16[96,1536]{1,0:T(8,128)(2,1)S(1)} %pad_maximum_fusion.8), channel_id=1, source_target_pairs={{0,3},{1,2},{2,1},{3,0},{4,7},{5,6},{6,5},{7,4},{8,11},{9,10},{10,... | collective-permute-start | bytes 884744 | tf_op jit(solution)/shard_map/ppermute | solution.py:143
  310.8 18.2 %collective-permute-start.33 = (bf16[4,480,768]{2,1,0:T(8,128)(2,1)S(1)}, bf16[4,480,768]{2,1,0:T(8,128)(2,1)}, u32[]{:S(2)}, u32[]{:S(2)}) collective-permute-start(bf16[4,480,768]{2,1,0:T(8,128)(2,1)S(1)} %dynamic-slice_bitcast_fusion), channel_id=1, source_target_pairs={{0,4},{4,0},{8,12},{12,8},{16,20},{20,16},{24,28},{28,24},{1,5},{5... | collective-permute-start | bytes 8847368 | tf_op jit(solution)/shard_map/ppermute | solution.py:83
  323.8 81.8 %all-to-all-start.6 = ((bf16[32,48,768]{2,1,0:T(8,128)(2,1)}), bf16[32,48,768]{2,1,0:T(8,128)(2,1)}, u32[]{:S(2)}, u32[]{:S(2)}) async-start(bf16[32,48,768]{2,1,0:T(8,128)(2,1)} %select_convert_fusion), calls=%async_computation.6 | async-start | bytes 4718592 | tf_op jit(solution)/shard_map/all_to_all | solution.py:641
  332.5 35.8 %collective-permute-start.34 = (bf16[480,768]{1,0:T(8,128)(2,1)S(1)}, bf16[480,768]{1,0:T(8,128)(2,1)S(1)}, u32[]{:S(2)}, u32[]{:S(2)}) collective-permute-start(bf16[480,768]{1,0:T(8,128)(2,1)S(1)} %pad_maximum_fusion.3), channel_id=1, source_target_pairs={{0,8},{4,12},{8,0},{12,4},{16,24},{20,28},{24,16},{28,20},{1,9},{5... | collective-permute-start | bytes 2211848 | tf_op jit(solution)/shard_map/ppermute | solution.py:83
  335.4 36.1 %collective-permute-start.36 = (bf16[480,768]{1,0:T(8,128)(2,1)}, bf16[480,768]{1,0:T(8,128)(2,1)}, u32[]{:S(2)}, u32[]{:S(2)}) collective-permute-start(bf16[480,768]{1,0:T(8,128)(2,1)} %pad_maximum_fusion.4), channel_id=1, source_target_pairs={{0,16},{4,20},{8,24},{12,28},{16,0},{20,4},{24,8},{28,12},{1,17},{... | collective-permute-start | bytes 2211848 | tf_op jit(solution)/shard_map/ppermute | solution.py:83
  399.7 17.7 %collective-permute-start.38 = (bf16[120,768]{1,0:T(8,128)(2,1)}, bf16[120,768]{1,0:T(8,128)(2,1)S(1)}, u32[]{:S(2)}, u32[]{:S(2)}) collective-permute-start(bf16[120,768]{1,0:T(8,128)(2,1)} %get-tuple-element.437), channel_id=1, source_target_pairs={{0,1},{1,0},{2,3},{3,2},{4,5},{5,4},{6,7},{7,6},{8,9},{9,8},{10,11... | collective-permute-start | bytes 552968 | tf_op jit(solution)/shard_map/ppermute | solution.py:143
  401.0 18.2 %collective-permute-start.39 = (bf16[120,768]{1,0:T(8,128)(2,1)}, bf16[120,768]{1,0:T(8,128)(2,1)S(1)}, u32[]{:S(2)}, u32[]{:S(2)}) collective-permute-start(bf16[120,768]{1,0:T(8,128)(2,1)} %get-tuple-element.439), channel_id=1, source_target_pairs={{0,2},{1,3},{2,0},{3,1},{4,6},{5,7},{6,4},{7,5},{8,10},{9,11},{10,... | collective-permute-start | bytes 552968 | tf_op jit(solution)/shard_map/ppermute | solution.py:143
  (70 other events, 806.0 us)

commit v3 on v2

--- a/solution.py
+++ b/solution.py
@@ -94,9 +94,12 @@
     return own, flip(own, 2), flip(own, 4)
 
 
-def gather_far(own, along_x, along_y):
-    half = own.shape[0] // 2
-    far_top, far_low = flip(along_x[:half], 4), flip(along_y[half:], 2)
+def far_blocks(along_x, along_y):
+    half = along_x.shape[0] // 2
+    return flip(along_x[:half], 4), flip(along_y[half:], 2)
+
+
+def all_blocks(own, along_x, along_y, far_top, far_low):
     mine = [own, along_x, far_top, far_low, along_y]
     return mine + [flip(block, 1) for block in mine]
 
@@ -160,7 +163,7 @@
     from_y = flip(low[2 * size :], 4)
     late_y = add_low(top[3 * size :], from_x[size:])
     late_x = add_low(low[size : 2 * size], from_y[:size])
-    return top[:size], low[:size], from_x[:size], from_y[size:], late_y, late_x
+    return together(top[:size], low[:size], from_x[:size], from_y[size:], late_y, late_x)
 
 
 def send_last(top, low, from_x, from_y, late_y, late_x):
@@ -206,9 +209,9 @@
 
 
 def attention_kernel(
-    length_ref, level_ref, embed_ref, qkv_ref, out_ref, gains_ref, project_ref, mixture_ref, first_ref, normed_ref
+    start, length_ref, level_ref, embed_ref, qkv_ref, out_ref, gains_ref, project_ref, mixture_ref, first_ref, normed_ref
 ):
-    step = pl.program_id(0)
+    step = pl.program_id(0) + start
     normed, _, _ = norm_forward(embed_ref[...].astype(jnp.float32), gains_ref[0:1], gains_ref[1:2])
     normed_low = normed.astype(jnp.bfloat16)
     normed_ref[...] = normed_low
@@ -243,33 +246,105 @@
     return pl.BlockSpec((BLOCK, width), lambda step: (step, 0))
 
 
-def attention_layer(own_lengths, own_levels, embedded, dense_full, norm_gains):
+def attention_layer(start, steps, scalars, embedded, dense_full, norm_gains, before):
     rows = embedded.shape[0]
     low = jnp.bfloat16
+    count = len(before)
+
+    def at_rows(width):
+        return pl.BlockSpec((BLOCK, width), lambda step: (step + start, 0))
+
+    def body(length_ref, level_ref, *refs):
+        attention_kernel(start, length_ref, level_ref, *refs[:4], *refs[4 + count :])
+
     return pl.pallas_call(
-        attention_kernel,
-        grid=(rows // BLOCK,),
+        body,
+        grid=(steps,),
         in_specs=[
             pl.BlockSpec(memory_space=pltpu.SMEM),
             pl.BlockSpec(memory_space=pltpu.SMEM),
-            by_rows(MODEL_WIDTH),
+            at_rows(MODEL_WIDTH),
             whole((3 * MODEL_WIDTH, MODEL_WIDTH)),
             pl.BlockSpec((MODEL_WIDTH, MODEL_WIDTH), lambda step: (3, 0)),
             whole((6, MODEL_WIDTH)),
-        ],
-        out_specs=[by_rows(3 * MODEL_WIDTH), by_rows(MODEL_WIDTH), by_rows(MODEL_WIDTH), by_rows(MODEL_WIDTH)],
+        ]
+        + [pl.BlockSpec(memory_space=pl.ANY)] * count,
+        out_specs=[at_rows(3 * MODEL_WIDTH), at_rows(MODEL_WIDTH), at_rows(MODEL_WIDTH), at_rows(MODEL_WIDTH)],
         out_shape=[
             jax.ShapeDtypeStruct((rows, 3 * MODEL_WIDTH), low),
             jax.ShapeDtypeStruct((rows, MODEL_WIDTH), low),
             jax.ShapeDtypeStruct((rows, MODEL_WIDTH), jnp.float32),
             jax.ShapeDtypeStruct((rows, MODEL_WIDTH), low),
         ],
+        input_output_aliases={6 + place: place for place in range(count)},
         compiler_params=pltpu.CompilerParams(vmem_limit_bytes=VMEM_BYTES),
         cost_estimate=pl.CostEstimate(
-            flops=rows * MODEL_WIDTH * MODEL_WIDTH * 10, bytes_accessed=rows * MODEL_WIDTH * 16, transcendentals=0
+            flops=steps * BLOCK * MODEL_WIDTH * MODEL_WIDTH * 20,
+            bytes_accessed=steps * BLOCK * MODEL_WIDTH * 16,
+            transcendentals=0,
         ),
         name="attention_layer",
-    )(own_lengths, own_levels, embedded, dense_full, dense_full, norm_gains)
+    )(*scalars, embedded, dense_full, dense_full, norm_gains, *before)
+
+
+def give_kernel(depth, spots_ref, grad_ref, rider_ref, sums_ref):
+    rows = sums_ref.shape[0]
+    row = pl.program_id(0) * rows + lax.broadcasted_iota(jnp.int32, (rows, 1), 0)
+    last = lax.broadcasted_iota(jnp.int32, (1, rider_ref.shape[0]), 1) * depth + depth - 1
+    own = (row == spots_ref[...]).astype(jnp.float32).astype(jnp.bfloat16)
+    ride = (row == last).astype(jnp.float32).astype(jnp.bfloat16)
+    sums_ref[...] = (dot_nn(own, grad_ref[...]) + dot_nn(ride, rider_ref[...])).astype(jnp.bfloat16)
+
+
+def give_rows(spots, grads, rider, depth):
+    total = rider.shape[0] * depth
+    size = 512 if total % 512 == 0 else total
+    return pl.pallas_call(
+        lambda *refs: give_kernel(depth, *refs),
+        grid=(total // size,),
+        in_specs=[whole((1, spots.shape[0])), whole(grads.shape), whole(rider.shape)],
+        out_specs=pl.BlockSpec((size, MODEL_WIDTH), lambda step: (step, 0)),
+        out_shape=jax.ShapeDtypeStruct((total, MODEL_WIDTH), jnp.bfloat16),
+        compiler_params=pltpu.CompilerParams(vmem_limit_bytes=VMEM_BYTES),
+        cost_estimate=pl.CostEstimate(
+            flops=2 * total * spots.shape[0] * MODEL_WIDTH, bytes_accessed=4 * total * MODEL_WIDTH, transcendentals=0
+        ),
+        name="give_rows",
+    )(spots[None, :], grads, rider)
+
+
+def collect_kernel(ids_ref, returned_ref, sums_ref, squares_ref):
+    step = pl.program_id(0)
+    rows = sums_ref.shape[0]
+    row = step * rows + lax.broadcasted_iota(jnp.int32, (rows, 1), 0)
+    hot = (row == ids_ref[...]).astype(jnp.float32).astype(jnp.bfloat16)
+    sums = dot_nn(hot, returned_ref[...])
+    sums_ref[...] = sums
+
+    @pl.when(step == 0)
+    def _():
+        squares_ref[...] = jnp.zeros_like(squares_ref)
+
+    squares_ref[0:1] += jnp.sum(sums * sums, axis=0, keepdims=True)
+
+
+def collect_rows(ids, returned, table_rows):
+    size = 240
+    return pl.pallas_call(
+        collect_kernel,
+        grid=(-(-table_rows // size),),
+        in_specs=[whole((1, ids.shape[0])), whole(returned.shape)],
+        out_specs=[pl.BlockSpec((size, MODEL_WIDTH), lambda step: (step, 0)), whole((8, MODEL_WIDTH))],
+        out_shape=[
+            jax.ShapeDtypeStruct((table_rows, MODEL_WIDTH), jnp.float32),
+            jax.ShapeDtypeStruct((8, MODEL_WIDTH), jnp.float32),
+        ],
+        compiler_params=pltpu.CompilerParams(vmem_limit_bytes=VMEM_BYTES),
+        cost_estimate=pl.CostEstimate(
+            flops=2 * table_rows * ids.shape[0] * MODEL_WIDTH, bytes_accessed=8 * table_rows * MODEL_WIDTH, transcendentals=0
+        ),
+        name="collect_rows",
+    )(ids[None, :], returned)
 
 
 def attention_back_kernel(
@@ -307,23 +382,25 @@
         length = length_ref[step * (BLOCK // L) + seq]
         heads = level_ref[step * (BLOCK // L) + seq] * (HEADS // LEVELS)
         usable.append((lax.broadcasted_iota(jnp.int32, (L, 1), 0) < length).astype(jnp.float32))
-        key_bias = jnp.where(lax.broadcasted_iota(jnp.int32, (1, L), 1) < length, 0.0, -1000000000.0)
+        key_bias = jnp.where(lax.broadcasted_iota(jnp.int32, (L, 1), 0) < length, 0.0, -1000000000.0)
         for pair in range(PAIRS):
             at = pair * PAIR
             queries = both_heads(project_ref[rows, at : at + PAIR], left_half)
             keys = project_ref[rows, MODEL_WIDTH + at : MODEL_WIDTH + at + PAIR]
             values = project_ref[rows, 2 * MODEL_WIDTH + at : 2 * MODEL_WIDTH + at + PAIR]
-            attend = pair_attend(queries, keys, key_bias)
+            scores = dot_nt(keys, queries) * scaling + key_bias
+            raised = jnp.exp(scores - jnp.max(scores, axis=0, keepdims=True))
+            attend = raised * (1.0 / jnp.sum(raised, axis=0, keepdims=True))
             head = 2 * pair + (lane >= PAIR // 2).astype(jnp.int32)
             mixture = grad_mixture_ref[rows, at : at + PAIR]
             mixture = both_heads(jnp.where(head < heads, mixture, jnp.zeros_like(mixture)), left_half)
-            grad_values = dot_tn(attend.astype(low), mixture)
-            grad_attend = dot_nt(mixture, values)
-            level = jnp.sum(grad_attend * attend, axis=-1, keepdims=True)
+            grad_values = dot_nn(attend.astype(low), mixture)
+            grad_attend = dot_nt(values, mixture)
+            level = jnp.sum(grad_attend * attend, axis=0, keepdims=True)
             grad_scores = (attend * (grad_attend - level)).astype(low)
-            grad_queries = dot_nn(grad_scores, keys) * scaling
+            grad_keys = dot_nn(grad_scores, queries) * scaling
+            grad_queries = dot_tn(grad_scores, keys) * scaling
             grad_queries = jnp.where(left_half, grad_queries[:L], grad_queries[L:])
-            grad_keys = dot_tn(grad_scores, queries) * scaling
             grad_project_ref[rows, at : at + PAIR] = grad_queries.astype(low)
             grad_project_ref[rows, MODEL_WIDTH + at : MODEL_WIDTH + at + PAIR] = grad_keys.astype(low)
             grad_project_ref[rows, 2 * MODEL_WIDTH + at : 2 * MODEL_WIDTH + at + PAIR] = grad_values.astype(low)
@@ -456,7 +533,8 @@
         gap = dot_nn(pooled_low, class_ref[...]) - logits_ref[...]
         grad_logits = split_low(2.0 * L * gap)
         rows = gap.shape[0]
-        grad_class_ref[...] = dot_tn(jnp.concatenate([pooled_low, pooled_low], axis=0), grad_logits)
+        grad_class = dot_tn(grad_logits, jnp.concatenate([pooled_low, pooled_low], axis=0))
+        grad_class_ref[...] = grad_class[: grad_class_ref.shape[0]]
         grad_pooled = dot_nt(grad_logits, class_ref[...])
         grad_inner = split_low((grad_pooled[:rows] + grad_pooled[rows:]) * (1.0 - pooled * pooled))
         grad_pool_ref[...] = dot_tn(jnp.concatenate([first_low, first_low], axis=0), grad_inner).astype(low)
@@ -522,7 +600,7 @@
             going(MODEL_WIDTH),
             coming(MODEL_WIDTH),
             whole((MODEL_WIDTH, MODEL_WIDTH)),
-            whole(class_wide.shape),
+            whole((8, MODEL_WIDTH)),
             whole((8, MODEL_WIDTH)),
         ],
         out_shape=[
@@ -532,7 +610,7 @@
             jax.ShapeDtypeStruct((rows, MODEL_WIDTH), low),
             jax.ShapeDtypeStruct((rows, MODEL_WIDTH), jnp.float32),
             jax.ShapeDtypeStruct((MODEL_WIDTH, MODEL_WIDTH), low),
-            jax.ShapeDtypeStruct(class_wide.shape, jnp.float32),
+            jax.ShapeDtypeStruct((8, MODEL_WIDTH), jnp.float32),
             jax.ShapeDtypeStruct((8, MODEL_WIDTH), jnp.float32),
         ],
         scratch_shapes=[
@@ -604,7 +682,6 @@
         neuron_index = (dp_index ^ codes) * chunk + (mp_index ^ steps) * neuron_piece + neuron_slot % neuron_piece
     else:
         neuron_index = neuron_slot
-    table_low = embed_table.astype(low)
 
     depth = -(-(own_rows * 3 // 2) // (n_dev * 16)) * 16
     capacity = depth - 1
@@ -647,44 +724,66 @@
     def own_hot(turn):
         return (positions(turn)[:, None] == jnp.arange(n_dev * depth)[None, :]).astype(low)
 
-    def answer(asked, *others):
-        rows = jnp.dot(asked_hot(asked), table_low, preferred_element_type=low)
-        rows, *others = together(rows.reshape(n_dev, depth, MODEL_WIDTH), *others)
-        return exchange(rows).reshape(-1, MODEL_WIDTH), *others
+    def answer(asked, table):
+        rows = jnp.dot(asked_hot(asked), table.astype(low), preferred_element_type=low)
+        return rows.reshape(n_dev, depth, MODEL_WIDTH)
 
     def place_rows(turn, rows):
-        return jnp.dot(own_hot(turn), rows, preferred_element_type=low)
-
-    dense_column, ffn_low = together(dense_column, feedforward.astype(low))
+        return jnp.dot(own_hot(turn), rows.reshape(-1, MODEL_WIDTH), preferred_element_type=low)
+
     asked_first = exchange(wanted(0))
+    ffn_low = feedforward.astype(low)
+    if by_bits:
+        dense_column, ffn_low = together(dense_column, ffn_low)
+        dense_near = gather_near(dense_column)
+        ffn_column = jnp.concatenate(gather_mp(ffn_low), axis=0)
+        rows_first, ffn_column, *dense_near = together(answer(asked_first, embed_table), ffn_column, *dense_near)
+    else:
+        rows_first = answer(asked_first, embed_table)
     turns = jnp.max(asked_first[:, capacity]) // capacity + 1
+    extra_rows = lax.while_loop(
+        lambda state: state[0] < turns,
+        lambda state: (
+            state[0] + 1,
+            state[1] + place_rows(state[0], exchange(answer(exchange(wanted(state[0])), embed_table))),
+        ),
+        (jnp.int32(1), jnp.zeros((own_rows, MODEL_WIDTH), low)),
+    )[1]
+    rows_first, extra_rows = together(rows_first, extra_rows)
+    rows_first = exchange(rows_first)
     if by_bits:
-        ffn_column = jnp.concatenate(gather_mp(ffn_low), axis=0)
-        rows_first, ffn_column, *dense_near = answer(asked_first, ffn_column, *gather_near(dense_column))
-        ffn_near = gather_near(ffn_column)
-        dense_full = assemble(dp_index, gather_far(*dense_near))
-        rows_first, dense_full, *ffn_near = together(rows_first, dense_full, *ffn_near)
-        ffn_pieces = gather_far(*ffn_near)
+        dense_full = assemble(dp_index, all_blocks(*dense_near, *far_blocks(*dense_near[1:])))
+        half = ffn_column.shape[0] // 2
+        top, rest = ffn_column[:half], ffn_column[half:]
+        x_top, y_rest = flip(top, 2), flip(rest, 4)
+        x_rest, y_top = flip(rest, 2), flip(top, 4)
+        rows_first, dense_full = together(rows_first, dense_full)
     else:
         dense_full = lax.all_gather(dense_column, "dp", axis=0, tiled=True)
         ffn_column = lax.all_gather(ffn_low, "mp", axis=0, tiled=True)
         ffn_pieces = [lax.all_gather(ffn_column, "dp", axis=0, tiled=True)]
-        rows_first, = answer(asked_first)
-    embedded_low = lax.while_loop(
-        lambda state: state[0] < turns,
-        lambda state: (
-            state[0] + 1,
-            state[1] + place_rows(state[0], answer(exchange(wanted(state[0])))[0]),
-        ),
-        (jnp.int32(1), place_rows(0, rows_first)),
-    )[1]
+    embedded_low = place_rows(0, rows_first) + extra_rows
 
     own_lengths = lax.dynamic_slice_in_dim(lengths, own_start, own_seqs)
     own_levels = lax.dynamic_slice_in_dim(widths, own_start, own_seqs)
     scalars = (own_lengths, own_levels)
-    project, head_mixture, first_sum, normed_low = attention_layer(
-        own_lengths, own_levels, embedded_low, dense_full, norm_gains
-    )
+    blocks = own_rows // BLOCK
+    if by_bits:
+        layer = attention_layer(0, blocks // 2, scalars, embedded_low, dense_full, norm_gains, ())
+        *layer, x_top, y_rest = together(*layer, x_top, y_rest)
+        far = flip(x_top, 4), flip(y_rest, 2)
+        layer = attention_layer(
+            blocks // 2, blocks - blocks // 2, scalars, embedded_low, dense_full, norm_gains, layer
+        )
+        near = [top, rest, x_top, x_rest, y_top, y_rest]
+        near = near + [flip(block, 1) for block in near]
+        flow = together(*layer, *near, *far)
+        layer, near, far = flow[:4], flow[4:16], flow[16:]
+        far = [*far, flip(far[0], 1), flip(far[1], 1)]
+        ffn_pieces = [*near[:4], *far[:2], *near[4:10], *far[2:], *near[10:]]
+    else:
+        layer = attention_layer(0, blocks, scalars, embedded_low, dense_full, norm_gains, ())
+    project, head_mixture, first_sum, normed_low = layer
     class_pad = -classifier.shape[1] % 128
     hidden_low, grad_before, grad_feed_low, middle_low, grad_middle, grad_pool_rows, grad_class, ffn_sums = ffn_layer(
         scalars,
@@ -697,7 +796,7 @@
         neuron_index[None, :],
         ffn_pieces,
     )
-    grad_class = grad_class[:, : classifier.shape[1]]
+    grad_class = grad_class[: classifier.shape[1]]
 
     def over_both(rows):
         rows = lax.psum_scatter(rows, "dp", scatter_dimension=0, tiled=True)
@@ -722,7 +821,8 @@
         parts = [lax.dynamic_index_in_dim(parts, place ^ code, 0, keepdims=False) for code in (0, 1, 3, 2)]
         top = jnp.concatenate([part[:half] for part in parts], axis=0)
         rest = jnp.concatenate([part[half:] for part in parts], axis=0)
-        parts = jnp.concatenate(send_last(*send_first(top, rest)), axis=0).reshape(mp_count, -1, rows.shape[1])
+        parts = send_last(*send_first(top, rest))
+        parts = jnp.concatenate(parts, axis=0).reshape(mp_count, -1, rows.shape[1])
         return sum_mp([lax.dynamic_index_in_dim(parts, mp_index ^ step, 0, keepdims=False) for step in range(mp_count)])
 
     arrays = [
@@ -733,24 +833,22 @@
         teacher_embed.reshape(own_rows, MODEL_WIDTH),
     ]
     weights = (dense_full, dense_full, norm_gains)
-    blocks = own_rows // BLOCK
     if by_bits:
         down_own, down_given = weight_sums(hidden_low, grad_feed_low)
         up_own, up_given = weight_sums(grad_before, middle_low)
         parts = (add_low(up_own, up_given), add_low(down_own, down_given))
         arrays[0], *parts = together(arrays[0], *parts)
         parts = send_first(*parts)
-        before = attention_backward(0, blocks - 2, scalars, arrays, weights, ())
+        before = attention_backward(0, blocks - 1, scalars, arrays, weights, ())
         arrays[0], *flow = together(arrays[0], *before, *parts)
         *before, sums_one = flow[:4]
         parts = send_last(*flow[4:])
-        before = attention_backward(blocks - 2, 1, scalars, arrays, weights, before)
-        arrays[0], *flow = together(arrays[0], *before, *parts)
-        *before, sums_two = flow[:4]
+        before = attention_backward(blocks - 1, 1, scalars, arrays, weights, before)
+        flow = together(*before, *parts)
+        *before, sums_last = flow[:4]
         parts = [part.reshape(mp_count, neuron_piece, MODEL_WIDTH) for part in flow[4:]]
         ffn_grad = sum_mp([jnp.concatenate([part[step] for part in parts], axis=1) for step in range(mp_count)])
-        *before, sums_last = attention_backward(blocks - 1, 1, scalars, arrays, weights, before)
-        sums = sums_one + sums_two + sums_last
+        sums = sums_one + sums_last
     else:
         ffn_grad = jnp.concatenate(
             [contract_first(grad_before, middle_low), contract_first(hidden_low, grad_feed_low)], axis=1
@@ -766,69 +864,44 @@
         ],
         axis=0,
     )
-    grad_embed_low, grad_dense, ffn_grad = together(grad_embed_low, grad_dense, ffn_grad)
     loss_own = jnp.sum(sums[4]) + jnp.sum(ffn_sums[2:4])
 
-    small = jnp.concatenate(
-        [
-            sums[:4].reshape(-1),
-            ffn_sums[:2].reshape(-1),
-            grad_class.reshape(-1),
-        ]
-    )
-    share = -(-small.shape[0] // n_dev)
-    small_parts = jnp.pad(small, (0, share * n_dev - small.shape[0])).reshape(n_dev, share)
-    upper = lax.reduce_precision(small_parts, 8, 7)
-    rider = jnp.concatenate([upper, small_parts - upper], axis=1).astype(low)
-    rider = jnp.pad(rider, ((0, 0), (0, MODEL_WIDTH - 2 * share)))
-
-    def give_back(turn):
-        sums = lax.dot_general(
-            own_hot(turn), grad_embed_low, (((0,), (0,)), ((), ())), preferred_element_type=jnp.float32
-        )
-        return sums.reshape(n_dev, depth, MODEL_WIDTH)
+    small = jnp.concatenate([sums[:4], ffn_sums[:2], grad_class], axis=0)
+    small_rows = small.shape[0]
+    upper = lax.reduce_precision(small, 8, 7)
+    rider = jnp.concatenate([upper, small - upper], axis=0).astype(low)
+    rider = jnp.pad(rider, ((0, n_dev - 2 * small_rows), (0, 0)))
+
+    def give_back(turn, rider):
+        return give_rows(positions(turn), grad_embed_low, rider, depth).reshape(n_dev, depth, MODEL_WIDTH)
 
     def collect(asked, returned):
-        return lax.dot_general(
-            asked_hot(asked),
-            returned.reshape(-1, MODEL_WIDTH),
-            (((0,), (0,)), ((), ())),
-            preferred_element_type=jnp.float32,
-        )
-
-    given = give_back(0)
-    given = jnp.where(jnp.arange(depth)[None, :, None] == capacity, rider.astype(jnp.float32)[:, None, :], given)
-    given = given.astype(low)
+        ids = jnp.where(jnp.arange(depth)[None, :] < capacity, asked, -1).reshape(-1)
+        return collect_rows(ids, returned.reshape(-1, MODEL_WIDTH), table_rows)
+
+    def collect_more(state):
+        turn, total, _ = state
+        total = total + collect(exchange(wanted(turn)), exchange(give_back(turn, jnp.zeros_like(rider))))[0]
+        return turn + 1, total, jnp.zeros((8, MODEL_WIDTH)).at[0].set(jnp.sum(total * total, axis=0))
+
+    given = give_back(0, rider)
+    given, grad_dense, ffn_grad = together(given, grad_dense, ffn_grad)
     returned = exchange(given)
     dense_grad = dense_scatter(grad_dense)
-    table_grad = collect(asked_first, returned)
-    table_grad = lax.while_loop(
-        lambda state: state[0] < turns,
-        lambda state: (
-            state[0] + 1,
-            state[1]
-            + collect(exchange(wanted(state[0])), exchange(give_back(state[0]).astype(low))),
-        ),
-        (jnp.int32(1), table_grad),
-    )[1]
-    riders = jnp.sum(returned[:, capacity, : 2 * share].astype(jnp.float32), axis=0)
-    small_share = riders[:share] + riders[share:]
-    square_sum = (
-        jnp.sum(table_grad * table_grad)
-        + jnp.sum(dense_grad * dense_grad)
-        + jnp.sum(ffn_grad * ffn_grad)
-        + jnp.sum(small_share * small_share)
-    )
+    _, table_grad, table_squares = lax.while_loop(
+        lambda state: state[0] < turns, collect_more, (jnp.int32(1), *collect(asked_first, returned))
+    )
+    small_row = jnp.sum(returned[:, capacity].astype(jnp.float32), axis=0)
+    square_sum = jnp.sum(table_squares) + jnp.sum(dense_grad * dense_grad) + jnp.sum(ffn_grad * ffn_grad)
     own_count = jnp.sum(own_lengths).astype(jnp.float32)
-    message = jnp.concatenate([small_share, jnp.stack([square_sum, own_count, loss_own])])
+    message = jnp.concatenate([small_row, jnp.stack([square_sum, own_count, loss_own])])
     message = jnp.pad(message, (0, -message.shape[0] % 128))
     told = exchange(jnp.broadcast_to(message[None], (n_dev, message.shape[0])))
-    scalars = jnp.sum(told[:, share : share + 3], axis=0)
-    total_square, token_count, loss_sum = scalars[0], scalars[1], scalars[2]
-    small_all = told[:, :share].reshape(-1)
-    gains_size = norm_gains.size
-    gains_grad = small_all[:gains_size].reshape(norm_gains.shape)
-    class_grad = small_all[gains_size : gains_size + classifier.size].reshape(classifier.shape)
+    scalars = jnp.sum(told[:, MODEL_WIDTH : MODEL_WIDTH + 128], axis=0)
+    token_count, loss_sum = scalars[1], scalars[2]
+    small = told[:small_rows, :MODEL_WIDTH] + told[small_rows : 2 * small_rows, :MODEL_WIDTH]
+    total_square = scalars[0] + jnp.sum(small * small)
+    gains_grad, class_grad = small[:6], small[6:].T
     inverse = 1.0 / token_count
     grad_norm = jnp.sqrt(total_square) * inverse
     scaling = inverse * (clip_bound / jnp.maximum(grad_norm, clip_bound))

time: 458 us -> 436 us (0.952); the launches traced: 455 us -> 427 us
  local copies, waits for them, and re-layouts: 32 us -> 23.4 us
  Pallas kernels: 119 us -> 111 us
  matrix products: 42 us -> 34.5 us
    ppermute x29 -> x34, waiting for transfers between devices: 105 us -> 75.9 us  [flip(): return lax.ppermute(block, 'dp', [(i, i ^ bit) for i in range(size)])]
    ppermute x12, waiting for transfers between devices: 16 us -> 35.6 us  [pass_mp(): lax.ppermute(block, 'mp', [(i, partner(i, step)) for i in range(lax.axis_...]
    pallas_call x1 -> x4, Pallas kernels: 16.1 us -> 31 us  [the longest x2 20.1 us: attention_layer(): pl.pallas_call(body, grid=(steps,), in_specs=[pl.BlockSpec(memory_space=p...]
    pallas_call x3 -> x2, Pallas kernels: 46.8 us -> 34.4 us  [attention_backward(): pl.pallas_call(body, grid=(steps,), in_specs=[pl.BlockSpec(memory_space=p...]
    pallas_call x1, Pallas kernels: 50.8 us -> 40.4 us  [ffn_layer(): pl.pallas_call(lambda *refs: ffn_kernel(sizes, *refs), grid=(2 * blocks +...]
    all_to_all x3, waiting for transfers between devices: 3.86 us -> 13.4 us  [exchange(): return lax.all_to_all(blocks, both, split_axis=0, concat_axis=0)]
    dot_general x4 -> x2, matrix products: 19.6 us -> 11.3 us  [the longest x1 5.69 us: place_rows(): jnp.dot(own_hot(turn), rows.reshape(-1, MODEL_WIDTH), preferred_element_t...]
    slice x10 -> x7, local copies, waits for them, and re-layouts: 8.2 us -> 2.79 us  [the longest x1 1.12 us: per_device(): top, rest = (ffn_column[:half], ffn_column[half:])]
  transfers between devices with their start and end apart: 44 -> 49, of which waited for: 16 -> 23; matrix products, arithmetic and copies ran while one was open for 19% -> 16% of each run, Pallas kernels for 15% -> 15%
where the time goes in v3:
time: 436 us; the launch traced here: 427 us
  waiting for transfers between devices  125 us (29%)
  Pallas kernels  111 us (25%)
  starting transfers between devices  56.2 us (13%)
  other arithmetic  54.1 us (12%)
  matrix products  34.5 us (8%)
  local copies, waits for them, and re-layouts  23.4 us (5%)
  blocking collectives  12.3 us (3%)
  between operations  10.8 us (2%)
    ppermute x34, waiting for transfers between devices, flip(): return lax.ppermute(block, 'dp', [(i, i ^ bit) for i in range(size)])  75.9 us
    pallas_call x1, Pallas kernels, ffn_layer(): pl.pallas_call(lambda *refs: ffn_kernel(sizes, *refs), grid=(2 * blocks +...  40.4 us
    ppermute x12, waiting for transfers between devices, pass_mp(): lax.ppermute(block, 'mp', [(i, partner(i, step)) for i in range(lax.axis_...  35.6 us
    pallas_call x2, Pallas kernels, attention_backward(): pl.pallas_call(body, grid=(steps,), in_specs=[pl.BlockSpec(memory_space=p...  34.4 us
    dot_general x6, matrix products, contract_first(): lax.dot_general(left, right, (((0,), (0,)), ((), ())), preferred_element_...  23.2 us
    ppermute x34, starting transfers between devices, flip(): return lax.ppermute(block, 'dp', [(i, i ^ bit) for i in range(size)])  21.7 us
    pallas_call x2, Pallas kernels, attention_layer(): pl.pallas_call(body, grid=(steps,), in_specs=[pl.BlockSpec(memory_space=p...  20.1 us
    ppermute x12, starting transfers between devices, pass_mp(): lax.ppermute(block, 'mp', [(i, partner(i, step)) for i in range(lax.axis_...  19.6 us
  transfers between devices with their start and end apart: 49, of which 23 were waited for; matrix products, arithmetic and copies ran while one was open for 16% of the time, Pallas kernels for 15%

profile of v3, /device:TPU:0, one launch (start us, length us, event | category | flops | bytes accessed | tf_op | source)
XLA Modules:
  0.0 427.4 jit_solution(18115284718446986902)
XLA Ops:
  1.7 4.1 collective-permute-start.1
  15.6 5.2 %all-to-all-start.4 = ((s32[32,1,48]{2,1,0:T(1,128)}), s32[32,1,48]{2,1,0:T(1,128)S(1)}, u32[]{:S(2)}, u32[]{:S(2)}) async-start(s32[32,1,48]{2,1,0:T(1,128)} %broadcast_select_fusion.6), calls=%async_computation.4 | async-start | bytes 32768 | tf_op jit(solution)/shard_map/all_to_all | solution.py:718
  22.5 3.1 convert_element_type.214
  37.6 5.6 %fusion.6 = bf16[1536,768]{1,0:T(8,128)(2,1)} fusion(bf16[956,768]{1,0:T(8,128)(2,1)} %convert_element_type.214, s32[1536]{0:T(1024)S(1)} %broadcast_select_fusion.7), kind=kOutput, calls=%fused_computation.29 | convolution fusion | flops 2256955392 | bytes 3833856 | tf_op jit(solution)/shard_map/dot_general | solution.py:728
  43.9 15.9 %collective-permute-done.4 = bf16[96,1536]{1,0:T(8,128)(2,1)S(1)} collective-permute-done((bf16[96,1536]{1,0:T(8,128)(2,1)S(1)}, bf16[96,1536]{1,0:T(8,128)(2,1)S(1)}, u32[]{:S(2)}, u32[]{:S(2)}) %collective-permute-start.4) | collective-permute-done | bytes 294944 | tf_op jit(solution)/shard_map/ppermute | solution.py:146
  63.5 4.5 %all-to-all-start.5 = ((bf16[32,48,768]{2,1,0:T(8,128)(2,1)}), bf16[32,48,768]{2,1,0:T(8,128)(2,1)}, u32[]{:S(2)}, u32[]{:S(2)}) async-start(bf16[32,48,768]{2,1,0:T(8,128)(2,1)} %bitcast.124), calls=%async_computation.5 | async-start | bytes 4718592 | tf_op jit(solution)/shard_map/all_to_all | solution.py:718
  72.1 24.7 %collective-permute-done.9.refs_3_ = bf16[240,768]{1,0:T(8,128)(2,1)S(1)} collective-permute-done((bf16[240,768]{1,0:T(8,128)(2,1)S(1)}, bf16[240,768]{1,0:T(8,128)(2,1)S(1)}, u32[]{:S(2)}, u32[]{:S(2)}) %collective-permute-start.9) | collective-permute-done | bytes 368672 | tf_op jit(solution)/shard_map/ppermute | solution.py:83
  104.7 5.4 %assemble.1.refs_1_.refs_2_.refs_4_.refs_5_.refs_6_ = bf16[3840,768]{1,0:T(8,128)(2,1)} custom-call(s32[1]{0:T(128)} %bitcast.10.place_ref, bf16[480,768]{1,0:T(8,128)(2,1)} %copy-done.7, bf16[480,768]{1,0:T(8,128)(2,1)} %copy-done.12, bf16[240,768]{1,0:T(8,128)(2,1)} %copy-done.32, bf16[240,768]{1,0:T(8,128)(2,1)} %copy-done.31, ...), custom_call_target="tpu_custom_call" | custom-call | bytes 11796480 | tf_op jit(solution)/shard_map/assemble/pallas_call | solution.py:128
  110.1 11.2 %all-to-all-done.5 = bf16[32,48,768]{2,1,0:T(8,128)(2,1)} async-done(((bf16[32,48,768]{2,1,0:T(8,128)(2,1)}), bf16[32,48,768]{2,1,0:T(8,128)(2,1)}, u32[]{:S(2)}, u32[]{:S(2)}) %all-to-all-start.5) | async-done | bytes 2359328 | tf_op jit(solution)/shard_map/all_to_all | solution.py:718
  124.3 5.7 %fusion.16.refs_0_.refs_3_ = bf16[1024,768]{1,0:T(8,128)(2,1)} fusion(bf16[1024,768]{1,0:T(8,128)(2,1)S(1)} %copy-done.18, bf16[1536,768]{1,0:T(8,128)(2,1)} %bitcast.11, s32[1024]{0:T(1024)S(1)} %copy-done.51), kind=kOutput, calls=%fused_computation.56 | convolution fusion | flops 2418278400 | bytes 5509120 | tf_op jit(solution)/shard_map/dot_general | solution.py:732
  130.0 10.0 %attention_layer.2 = (bf16[1024,2304]{1,0:T(8,128)(2,1)}, bf16[1024,768]{1,0:T(8,128)(2,1)}, f32[1024,768]{1,0:T(8,128)}, bf16[1024,768]{1,0:T(8,128)(2,1)}) custom-call(s32[8]{0:T(128)} %get-tuple-element.545.length_ref.refs_0_, s32[8]{0:T(128)} %dynamic_slice.44.level_ref.refs_1_, bf16[1024,768]{1,0:T(8,128)(2,1)} %fusion.16.refs_0_.refs_3_, ...), custom_call_target="tpu_custom_call" | custom-call | flops 6039797760 | bytes 6291456 | tf_op jit(solution)/shard_map/attention_layer/pallas_call | solution.py:260
  144.3 10.0 %attention_layer.3 = (bf16[1024,2304]{1,0:T(8,128)(2,1)}, bf16[1024,768]{1,0:T(8,128)(2,1)}, f32[1024,768]{1,0:T(8,128)}, bf16[1024,768]{1,0:T(8,128)(2,1)}) custom-call(s32[8]{0:T(128)} %get-tuple-element.545.length_ref.refs_0_, s32[8]{0:T(128)} %dynamic_slice.44.level_ref.refs_1_, ...), custom_call_target="tpu_custom_call", output_to_operand_aliasing={{0}: (6, {}), {1}: (7, {}), {2}: (8, {}), {3}: (9, {})} | custom-call | flops 6039797760 | bytes 6291456 | tf_op jit(solution)/shard_map/attention_layer/pallas_call | solution.py:260
  160.6 40.4 %ffn_layer.1 = (bf16[1024,3072]{1,0:T(8,128)(2,1)}, bf16[1024,3072]{1,0:T(8,128)(2,1)}, bf16[1024,768]{1,0:T(8,128)(2,1)}, bf16[1024,768]{1,0:T(8,128)(2,1)}, f3...) custom-call(s32[8]{0:T(128)} %get-tuple-element.545.length_ref.refs_0_, ...), custom_call_target="tpu_custom_call" | custom-call | flops 38654705664 | bytes 25165824 | tf_op jit(solution)/shard_map/ffn_layer/pallas_call | solution.py:581
  201.0 6.4 %convolution_convert_fusion.1 = bf16[1536,768]{1,0:T(8,128)(2,1)} fusion(bf16[1024,768]{1,0:T(8,128)(2,1)} %get-tuple-element.421, bf16[1024,3072]{1,0:T(8,128)(2,1)} %get-tuple-element.420), kind=kOutput, calls=%fused_computation.41 | convolution fusion | flops 2417098752 | bytes 7077888 | tf_op jit(solution)/shard_map/dot_general | solution.py:76
  207.6 5.2 %convolution_convert_fusion.3 = bf16[1536,768]{1,0:T(8,128)(2,1)S(1)} fusion(bf16[1024,768]{1,0:T(8,128)(2,1)} %get-tuple-element.419, bf16[1024,3072]{1,0:T(8,128)(2,1)} %get-tuple-element.418), kind=kOutput, calls=%fused_computation.43 | convolution fusion | flops 2417098752 | bytes 7077888 | tf_op jit(solution)/shard_map/dot_general | solution.py:76
  216.9 3.0 convolution_convert_fusion.2
  225.5 24.4 %attention_backward.2 = (bf16[1024,2304]{1,0:T(8,128)(2,1)}, bf16[1024,768]{1,0:T(8,128)(2,1)}, bf16[1024,768]{1,0:T(8,128)(2,1)S(1)}, f32[8,768]{1,0:T(8,128)}) custom-call(s32[8]{0:T(128)} %get-tuple-element.545.length_ref.refs_0_, s32[8]{0:T(128)} %dynamic_slice.44.level_ref.refs_1_, f32[1024,768]{1,0:T(8,128)} %get-tuple-element.436.refs_0_, ...), custom_call_target="tpu_custom_call" | custom-call | flops 18119393280 | bytes 14155776 | tf_op jit(solution)/shard_map/attention_backward/pallas_call | solution.py:437
  257.7 10.1 %attention_backward.3 = (bf16[1024,2304]{1,0:T(8,128)(2,1)}, bf16[1024,768]{1,0:T(8,128)(2,1)}, bf16[1024,768]{1,0:T(8,128)(2,1)S(1)}, f32[8,768]{1,0:T(8,128)}) custom-call(s32[8]{0:T(128)} %get-tuple-element.545.length_ref.refs_0_, s32[8]{0:T(128)} %dynamic_slice.44.level_ref.refs_1_, ...), custom_call_target="tpu_custom_call", output_to_operand_aliasing={{0}: (10, {}), {1}: (11, {}), {2}: (12, {})} | custom-call | flops 6039797760 | bytes 4718592 | tf_op jit(solution)/shard_map/attention_backward/pallas_call | solution.py:437
  280.8 4.2 convolution_convert_fusion
  286.2 5.3 %give_rows.5 = bf16[1536,768]{1,0:T(8,128)(2,1)} custom-call(s32[1,1024]{1,0:T(1,128)} %and_select_fusion.3.refs_0_, bf16[1024,768]{1,0:T(8,128)(2,1)S(1)} %get-tuple-element.761.refs_1_, bf16[32,768]{1,0:T(8,128)(2,1)} %fusion.27.refs_2_), custom_call_target="tpu_custom_call" | custom-call | flops 2415919104 | bytes 4718592 | tf_op jit(solution)/shard_map/give_rows/pallas_call | solution.py:302
  291.5 7.0 %collective-permute-done.36 = bf16[96,1536]{1,0:T(8,128)(2,1)S(1)} collective-permute-done((bf16[96,1536]{1,0:T(8,128)(2,1)}, bf16[96,1536]{1,0:T(8,128)(2,1)S(1)}, u32[]{:S(2)}, u32[]{:S(2)}) %collective-permute-start.36) | collective-permute-done | bytes 294944 | tf_op jit(solution)/shard_map/ppermute | solution.py:146
  302.4 5.3 %all-to-all-start.6 = ((bf16[32,48,768]{2,1,0:T(8,128)(2,1)}), bf16[32,48,768]{2,1,0:T(8,128)(2,1)}, u32[]{:S(2)}, u32[]{:S(2)}) async-start(bf16[32,48,768]{2,1,0:T(8,128)(2,1)} %bitcast.123), calls=%async_computation.6 | async-start | bytes 4718592 | tf_op jit(solution)/shard_map/all_to_all | solution.py:718
  308.1 3.4 fusion.7
  319.4 27.6 %collective-permute-done.39 = bf16[480,768]{1,0:T(8,128)(2,1)} collective-permute-done((bf16[480,768]{1,0:T(8,128)(2,1)}, bf16[480,768]{1,0:T(8,128)(2,1)}, u32[]{:S(2)}, u32[]{:S(2)}) %collective-permute-start.39) | collective-permute-done | bytes 737312 | tf_op jit(solution)/shard_map/ppermute | solution.py:83
  353.0 10.6 %collective-permute-done.41 = bf16[240,768]{1,0:T(8,128)(2,1)S(1)} collective-permute-done((bf16[240,768]{1,0:T(8,128)(2,1)S(1)}, bf16[240,768]{1,0:T(8,128)(2,1)S(1)}, u32[]{:S(2)}, u32[]{:S(2)}) %collective-permute-start.41) | collective-permute-done | bytes 368672 | tf_op jit(solution)/shard_map/ppermute | solution.py:83
  364.4 3.2 collective-permute-start.43
  372.8 5.6 %collective-permute-done.45 = bf16[120,768]{1,0:T(8,128)(2,1)S(1)} collective-permute-done((bf16[120,768]{1,0:T(8,128)(2,1)S(1)}, bf16[120,768]{1,0:T(8,128)(2,1)S(1)}, u32[]{:S(2)}, u32[]{:S(2)}) %collective-permute-start.45) | collective-permute-done | bytes 184352 | tf_op jit(solution)/shard_map/ppermute | solution.py:146
  378.4 6.3 %collective-permute-done.44 = bf16[120,768]{1,0:T(8,128)(2,1)S(1)} collective-permute-done((bf16[120,768]{1,0:T(8,128)(2,1)S(1)}, bf16[120,768]{1,0:T(8,128)(2,1)S(1)}, u32[]{:S(2)}, u32[]{:S(2)}) %collective-permute-start.44) | collective-permute-done | bytes 184352 | tf_op jit(solution)/shard_map/ppermute | solution.py:146
  386.2 5.6 %collect_rows.5 = (f32[956,768]{1,0:T(8,128)S(1)}, f32[8,768]{1,0:T(8,128)}) custom-call(s32[1,1536]{1,0:T(1,128)} %broadcast_select_fusion.8.ids_ref, bf16[1536,768]{1,0:T(8,128)(2,1)} %bitcast.16.returned_ref), custom_call_target="tpu_custom_call" | custom-call | flops 2255486976 | bytes 5873664 | tf_op jit(solution)/shard_map/collect_rows/pallas_call | solution.py:333
  396.4 12.3 %all_to_all.78 = f32[32,1,896]{2,1,0:T(1,128)S(1)} all-to-all(f32[32,1,896]{2,1,0:T(1,128)S(1)} %broadcast_in_dim.216), channel_id=1, replica_groups=mesh['dp'=8,'mp'=4] {'dp','mp'}, dimensions={0} | all-to-all | bytes 229376 | tf_op jit(solution)/shard_map/all_to_all | solution.py:718
  415.6 3.2 fusion.40
  420.1 6.0 %fusion.44 = (bf16[956,768]{1,0:T(8,128)(2,1)}, f32[956,768]{1,0:T(8,128)}, f32[956,768]{1,0:T(8,128)}, f32[956,768]{1,0:T(8,128)}) fusion(f32[956,768]{1,0:T(8,128)S(1)} %copy-done.1, f32[956,768]{1,0:T(8,128)S(1)} %get-tuple-element.880, f32[]{:T(128)S(6)} %mul.375, f32[956,768]{1,0:T(8,128)S(1)} %copy-done.6, f32[956,768]{1,0:T(8,128)} %param.42), kind=kLoop, calls=%fused_computation.169 | loop fusion | flops 12481536 | bytes 22026244 | tf_op jit(solution)/shard_map/convert_element_type | solution.py:940
  (320 shorter events, 116.1 us)
Async XLA Ops:
  1.7 30.2 %collective-permute-start.1 = (bf16[120,768]{1,0:T(8,128)(2,1)S(1)}, bf16[120,768]{1,0:T(8,128)(2,1)S(1)}, u32[]{:S(2)}, u32[]{:S(2)}) collective-permute-start(bf16[120,768]{1,0:T(8,128)(2,1)S(1)} %convert_element_type.215), channel_id=1, source_target_pairs={{0,2},{1,3},{2,0},{3,1},{4,6},{5,7},{6,4},{7,5},{8,10},{9,11},{10,... | collective-permute-start | bytes 552968 | tf_op jit(solution)/shard_map/ppermute | solution.py:146
  5.8 26.1 %collective-permute-start.2 = (bf16[120,768]{1,0:T(8,128)(2,1)S(1)}, bf16[120,768]{1,0:T(8,128)(2,1)S(1)}, u32[]{:S(2)}, u32[]{:S(2)}) collective-permute-start(bf16[120,768]{1,0:T(8,128)(2,1)S(1)} %convert_element_type.215), channel_id=1, source_target_pairs={{0,3},{1,2},{2,1},{3,0},{4,7},{5,6},{6,5},{7,4},{8,11},{9,10},{10,... | collective-permute-start | bytes 552968 | tf_op jit(solution)/shard_map/ppermute | solution.py:146
  7.1 24.7 %collective-permute-start = (bf16[120,768]{1,0:T(8,128)(2,1)S(1)}, bf16[120,768]{1,0:T(8,128)(2,1)S(1)}, u32[]{:S(2)}, u32[]{:S(2)}) collective-permute-start(bf16[120,768]{1,0:T(8,128)(2,1)S(1)} %convert_element_type.215), channel_id=1, source_target_pairs={{0,1},{1,0},{2,3},{3,2},{4,5},{5,4},{6,7},{7,6},{8,9},{9,8},{10,11... | collective-permute-start | bytes 552968 | tf_op jit(solution)/shard_map/ppermute | solution.py:146
  33.5 26.3 %collective-permute-start.4 = (bf16[96,1536]{1,0:T(8,128)(2,1)S(1)}, bf16[96,1536]{1,0:T(8,128)(2,1)S(1)}, u32[]{:S(2)}, u32[]{:S(2)}) collective-permute-start(bf16[96,1536]{1,0:T(8,128)(2,1)S(1)} %convert_element_type.216), channel_id=1, source_target_pairs={{0,2},{1,3},{2,0},{3,1},{4,6},{5,7},{6,4},{7,5},{8,10},{9,11},{10,... | collective-permute-start | bytes 884744 | tf_op jit(solution)/shard_map/ppermute | solution.py:146
  34.1 25.7 %collective-permute-start.3 = (bf16[96,1536]{1,0:T(8,128)(2,1)S(1)}, bf16[96,1536]{1,0:T(8,128)(2,1)S(1)}, u32[]{:S(2)}, u32[]{:S(2)}) collective-permute-start(bf16[96,1536]{1,0:T(8,128)(2,1)S(1)} %convert_element_type.216), channel_id=1, source_target_pairs={{0,1},{1,0},{2,3},{3,2},{4,5},{5,4},{6,7},{7,6},{8,9},{9,8},{10,11... | collective-permute-start | bytes 884744 | tf_op jit(solution)/shard_map/ppermute | solution.py:146
  36.5 23.4 %collective-permute-start.7 = (bf16[480,768]{1,0:T(8,128)(2,1)S(1)}, bf16[480,768]{1,0:T(8,128)(2,1)S(1)}, u32[]{:S(2)}, u32[]{:S(2)}) collective-permute-start(bf16[480,768]{1,0:T(8,128)(2,1)S(1)} %pad_maximum_fusion.2.refs_0_), channel_id=1, source_target_pairs={{0,16},{4,20},{8,24},{12,28},{16,0},{20,4},{24,8},{28,12},{1,17},{... | collective-permute-start | bytes 2211848 | tf_op jit(solution)/shard_map/ppermute | solution.py:83
  37.1 22.8 %collective-permute-start.6 = (bf16[480,768]{1,0:T(8,128)(2,1)S(1)}, bf16[480,768]{1,0:T(8,128)(2,1)S(1)}, u32[]{:S(2)}, u32[]{:S(2)}) collective-permute-start(bf16[480,768]{1,0:T(8,128)(2,1)S(1)} %pad_maximum_fusion.2.refs_0_), channel_id=1, source_target_pairs={{0,8},{4,12},{8,0},{12,4},{16,24},{20,28},{24,16},{28,20},{1,9},{5... | collective-permute-start | bytes 2211848 | tf_op jit(solution)/shard_map/ppermute | solution.py:83
  63.5 57.8 %all-to-all-start.5 = ((bf16[32,48,768]{2,1,0:T(8,128)(2,1)}), bf16[32,48,768]{2,1,0:T(8,128)(2,1)}, u32[]{:S(2)}, u32[]{:S(2)}) async-start(bf16[32,48,768]{2,1,0:T(8,128)(2,1)} %bitcast.124), calls=%async_computation.5 | async-start | bytes 4718592 | tf_op jit(solution)/shard_map/all_to_all | solution.py:718
  68.1 28.7 %collective-permute-start.9 = (bf16[240,768]{1,0:T(8,128)(2,1)S(1)}, bf16[240,768]{1,0:T(8,128)(2,1)S(1)}, u32[]{:S(2)}, u32[]{:S(2)}) collective-permute-start(bf16[240,768]{1,0:T(8,128)(2,1)S(1)} %slice.219), channel_id=1, source_target_pairs={{0,8},{4,12},{8,0},{12,4},{16,24},{20,28},{24,16},{28,20},{1,9},{5... | collective-permute-start | bytes 1105928 | tf_op jit(solution)/shard_map/ppermute | solution.py:83
  70.0 27.7 %collective-permute-start.8 = (bf16[240,768]{1,0:T(8,128)(2,1)S(1)}, bf16[240,768]{1,0:T(8,128)(2,1)S(1)}, u32[]{:S(2)}, u32[]{:S(2)}) collective-permute-start(bf16[240,768]{1,0:T(8,128)(2,1)S(1)} %slice.218), channel_id=1, source_target_pairs={{0,16},{4,20},{8,24},{12,28},{16,0},{20,4},{24,8},{28,12},{1,17},{... | collective-permute-start | bytes 1105928 | tf_op jit(solution)/shard_map/ppermute | solution.py:83
  71.6 31.6 %collective-permute-start.11 = (bf16[480,768]{1,0:T(8,128)(2,1)S(1)}, bf16[480,768]{1,0:T(8,128)(2,1)}, u32[]{:S(2)}, u32[]{:S(2)}) collective-permute-start(bf16[480,768]{1,0:T(8,128)(2,1)S(1)} %copy-done.13), channel_id=1, source_target_pairs={{0,4},{4,0},{8,12},{12,8},{16,20},{20,16},{24,28},{28,24},{1,5},{5... | collective-permute-start | bytes 2211848 | tf_op jit(solution)/shard_map/ppermute | solution.py:83
  71.6 32.1 %collective-permute-start.14 = (bf16[480,768]{1,0:T(8,128)(2,1)S(1)}, bf16[480,768]{1,0:T(8,128)(2,1)}, u32[]{:S(2)}, u32[]{:S(2)}) collective-permute-start(bf16[480,768]{1,0:T(8,128)(2,1)S(1)} %copy-done.11), channel_id=1, source_target_pairs={{0,4},{4,0},{8,12},{12,8},{16,20},{20,16},{24,28},{28,24},{1,5},{5... | collective-permute-start | bytes 2211848 | tf_op jit(solution)/shard_map/ppermute | solution.py:83
  72.1 31.1 %collective-permute-start.10 = (bf16[480,768]{1,0:T(8,128)(2,1)S(1)}, bf16[480,768]{1,0:T(8,128)(2,1)}, u32[]{:S(2)}, u32[]{:S(2)}) collective-permute-start(bf16[480,768]{1,0:T(8,128)(2,1)S(1)} %copy-done.8), channel_id=1, source_target_pairs={{0,4},{4,0},{8,12},{12,8},{16,20},{20,16},{24,28},{28,24},{1,5},{5... | collective-permute-start | bytes 2211848 | tf_op jit(solution)/shard_map/ppermute | solution.py:83
  98.9 22.4 %collective-permute-start.17 = (bf16[192,1536]{1,0:T(8,128)(2,1)}, bf16[192,1536]{1,0:T(8,128)(2,1)S(1)}, u32[]{:S(2)}, u32[]{:S(2)}) collective-permute-start(bf16[192,1536]{1,0:T(8,128)(2,1)} %get-tuple-element.404.refs_10_), channel_id=1, source_target_pairs={{0,8},{4,12},{8,0},{12,4},{16,24},{20,28},{24,16},{28,20},{1,9},{5... | collective-permute-start | bytes 1769480 | tf_op jit(solution)/shard_map/ppermute | solution.py:83
  100.3 21.5 %collective-permute-start.16 = (bf16[192,1536]{1,0:T(8,128)(2,1)}, bf16[192,1536]{1,0:T(8,128)(2,1)S(1)}, u32[]{:S(2)}, u32[]{:S(2)}) collective-permute-start(bf16[192,1536]{1,0:T(8,128)(2,1)} %get-tuple-element.404.refs_10_), channel_id=1, source_target_pairs={{0,16},{4,20},{8,24},{12,28},{16,0},{20,4},{24,8},{28,12},{1,17},{... | collective-permute-start | bytes 1769480 | tf_op jit(solution)/shard_map/ppermute | solution.py:83
  103.2 37.7 %collective-permute-start.20 = (bf16[192,1536]{1,0:T(8,128)(2,1)}, bf16[192,1536]{1,0:T(8,128)(2,1)}, u32[]{:S(2)}, u32[]{:S(2)}) collective-permute-start(bf16[192,1536]{1,0:T(8,128)(2,1)} %get-tuple-element.404.refs_10_), channel_id=1, source_target_pairs={{0,4},{4,0},{8,12},{12,8},{16,20},{20,16},{24,28},{28,24},{1,5},{5... | collective-permute-start | bytes 1769480 | tf_op jit(solution)/shard_map/ppermute | solution.py:83
  103.2 37.7 %collective-permute-start.19 = (bf16[192,1536]{1,0:T(8,128)(2,1)}, bf16[192,1536]{1,0:T(8,128)(2,1)}, u32[]{:S(2)}, u32[]{:S(2)}) collective-permute-start(bf16[192,1536]{1,0:T(8,128)(2,1)} %get-tuple-element.403.refs_9_), channel_id=1, source_target_pairs={{0,4},{4,0},{8,12},{12,8},{16,20},{20,16},{24,28},{28,24},{1,5},{5... | collective-permute-start | bytes 1769480 | tf_op jit(solution)/shard_map/ppermute | solution.py:83
  103.7 36.3 %collective-permute-start.18 = (bf16[192,1536]{1,0:T(8,128)(2,1)}, bf16[192,1536]{1,0:T(8,128)(2,1)}, u32[]{:S(2)}, u32[]{:S(2)}) collective-permute-start(bf16[192,1536]{1,0:T(8,128)(2,1)} %get-tuple-element.403.refs_9_), channel_id=1, source_target_pairs={{0,16},{4,20},{8,24},{12,28},{16,0},{20,4},{24,8},{28,12},{1,17},{... | collective-permute-start | bytes 1769480 | tf_op jit(solution)/shard_map/ppermute | solution.py:83
  121.3 19.0 %collective-permute-start.15 = (bf16[192,1536]{1,0:T(8,128)(2,1)S(1)}, bf16[192,1536]{1,0:T(8,128)(2,1)}, u32[]{:S(2)}, u32[]{:S(2)}) collective-permute-start(bf16[192,1536]{1,0:T(8,128)(2,1)S(1)} %copy-done.23), channel_id=1, source_target_pairs={{0,8},{4,12},{8,0},{12,4},{16,24},{20,28},{24,16},{28,20},{1,9},{5... | collective-permute-start | bytes 1769480 | tf_op jit(solution)/shard_map/ppermute | solution.py:83
  121.8 20.0 %collective-permute-start.22 = (bf16[192,1536]{1,0:T(8,128)(2,1)S(1)}, bf16[192,1536]{1,0:T(8,128)(2,1)S(1)}, u32[]{:S(2)}, u32[]{:S(2)}) collective-permute-start(bf16[192,1536]{1,0:T(8,128)(2,1)S(1)} %collective-permute-done.17.refs_12_), channel_id=1, source_target_pairs={{0,4},{4,0},{8,12},{12,8},{16,20},{20,16},{24,28},{28,24},{1,5},{5... | collective-permute-start | bytes 1769480 | tf_op jit(solution)/shard_map/ppermute | solution.py:83
  140.3 15.7 %collective-permute-start.25 = (bf16[192,1536]{1,0:T(8,128)(2,1)}, bf16[192,1536]{1,0:T(8,128)(2,1)S(1)}, u32[]{:S(2)}, u32[]{:S(2)}) collective-permute-start(bf16[192,1536]{1,0:T(8,128)(2,1)} %collective-permute-done.15.refs_11_), channel_id=1, source_target_pairs={{0,16},{4,20},{8,24},{12,28},{16,0},{20,4},{24,8},{28,12},{1,17},{... | collective-permute-start | bytes 1769480 | tf_op jit(solution)/shard_map/ppermute | solution.py:83
  140.8 15.2 %collective-permute-start.21 = (bf16[192,1536]{1,0:T(8,128)(2,1)}, bf16[192,1536]{1,0:T(8,128)(2,1)S(1)}, u32[]{:S(2)}, u32[]{:S(2)}) collective-permute-start(bf16[192,1536]{1,0:T(8,128)(2,1)} %collective-permute-done.15.refs_11_), channel_id=1, source_target_pairs={{0,4},{4,0},{8,12},{12,8},{16,20},{20,16},{24,28},{28,24},{1,5},{5... | collective-permute-start | bytes 1769480 | tf_op jit(solution)/shard_map/ppermute | solution.py:83
  140.9 15.8 %collective-permute-start.26 = (bf16[192,1536]{1,0:T(8,128)(2,1)S(1)}, bf16[192,1536]{1,0:T(8,128)(2,1)}, u32[]{:S(2)}, u32[]{:S(2)}) collective-permute-start(bf16[192,1536]{1,0:T(8,128)(2,1)S(1)} %collective-permute-done.16.refs_16_), channel_id=1, source_target_pairs={{0,8},{4,12},{8,0},{12,4},{16,24},{20,28},{24,16},{28,20},{1,9},{5... | collective-permute-start | bytes 1769480 | tf_op jit(solution)/shard_map/ppermute | solution.py:83
  223.6 28.3 %collective-permute-start.32 = (bf16[768,768]{1,0:T(8,128)(2,1)}, bf16[768,768]{1,0:T(8,128)(2,1)S(1)}, u32[]{:S(2)}, u32[]{:S(2)}) collective-permute-start(bf16[768,768]{1,0:T(8,128)(2,1)} %slice.230), channel_id=1, source_target_pairs={{0,16},{4,20},{8,24},{12,28},{16,0},{20,4},{24,8},{28,12},{1,17},{... | collective-permute-start | bytes 3538952 | tf_op jit(solution)/shard_map/ppermute | solution.py:83
  225.1 28.0 %collective-permute-start.31 = (bf16[768,768]{1,0:T(8,128)(2,1)}, bf16[768,768]{1,0:T(8,128)(2,1)}, u32[]{:S(2)}, u32[]{:S(2)}) collective-permute-start(bf16[768,768]{1,0:T(8,128)(2,1)} %slice.228), channel_id=1, source_target_pairs={{0,8},{4,12},{8,0},{12,4},{16,24},{20,28},{24,16},{28,20},{1,9},{5... | collective-permute-start | bytes 3538952 | tf_op jit(solution)/shard_map/ppermute | solution.py:83
  273.4 18.1 %collective-permute-start.35 = (bf16[96,1536]{1,0:T(8,128)(2,1)}, bf16[96,1536]{1,0:T(8,128)(2,1)S(1)}, u32[]{:S(2)}, u32[]{:S(2)}) collective-permute-start(bf16[96,1536]{1,0:T(8,128)(2,1)} %pad_maximum_fusion.6), channel_id=1, source_target_pairs={{0,1},{1,0},{2,3},{3,2},{4,5},{5,4},{6,7},{7,6},{8,9},{9,8},{10,11... | collective-permute-start | bytes 884744 | tf_op jit(solution)/shard_map/ppermute | solution.py:146
  275.8 22.8 %collective-permute-start.36 = (bf16[96,1536]{1,0:T(8,128)(2,1)}, bf16[96,1536]{1,0:T(8,128)(2,1)S(1)}, u32[]{:S(2)}, u32[]{:S(2)}) collective-permute-start(bf16[96,1536]{1,0:T(8,128)(2,1)} %pad_maximum_fusion.7), channel_id=1, source_target_pairs={{0,2},{1,3},{2,0},{3,1},{4,6},{5,7},{6,4},{7,5},{8,10},{9,11},{10,... | collective-permute-start | bytes 884744 | tf_op jit(solution)/shard_map/ppermute | solution.py:146
  277.8 20.7 %collective-permute-start.37 = (bf16[96,1536]{1,0:T(8,128)(2,1)}, bf16[96,1536]{1,0:T(8,128)(2,1)}, u32[]{:S(2)}, u32[]{:S(2)}) collective-permute-start(bf16[96,1536]{1,0:T(8,128)(2,1)} %pad_maximum_fusion.8), channel_id=1, source_target_pairs={{0,3},{1,2},{2,1},{3,0},{4,7},{5,6},{6,5},{7,4},{8,11},{9,10},{10,... | collective-permute-start | bytes 884744 | tf_op jit(solution)/shard_map/ppermute | solution.py:146
  302.4 83.8 %all-to-all-start.6 = ((bf16[32,48,768]{2,1,0:T(8,128)(2,1)}), bf16[32,48,768]{2,1,0:T(8,128)(2,1)}, u32[]{:S(2)}, u32[]{:S(2)}) async-start(bf16[32,48,768]{2,1,0:T(8,128)(2,1)} %bitcast.123), calls=%async_computation.6 | async-start | bytes 4718592 | tf_op jit(solution)/shard_map/all_to_all | solution.py:718
  313.5 33.5 %collective-permute-start.39 = (bf16[480,768]{1,0:T(8,128)(2,1)}, bf16[480,768]{1,0:T(8,128)(2,1)}, u32[]{:S(2)}, u32[]{:S(2)}) collective-permute-start(bf16[480,768]{1,0:T(8,128)(2,1)} %pad_maximum_fusion.3), channel_id=1, source_target_pairs={{0,8},{4,12},{8,0},{12,4},{16,24},{20,28},{24,16},{28,20},{1,9},{5... | collective-permute-start | bytes 2211848 | tf_op jit(solution)/shard_map/ppermute | solution.py:83
  315.7 32.8 %collective-permute-start.40 = (bf16[480,768]{1,0:T(8,128)(2,1)}, bf16[480,768]{1,0:T(8,128)(2,1)}, u32[]{:S(2)}, u32[]{:S(2)}) collective-permute-start(bf16[480,768]{1,0:T(8,128)(2,1)} %pad_maximum_fusion.4), channel_id=1, source_target_pairs={{0,16},{4,20},{8,24},{12,28},{16,0},{20,4},{24,8},{28,12},{1,17},{... | collective-permute-start | bytes 2211848 | tf_op jit(solution)/shard_map/ppermute | solution.py:83
  368.9 15.8 %collective-permute-start.44 = (bf16[120,768]{1,0:T(8,128)(2,1)S(1)}, bf16[120,768]{1,0:T(8,128)(2,1)S(1)}, u32[]{:S(2)}, u32[]{:S(2)}) collective-permute-start(bf16[120,768]{1,0:T(8,128)(2,1)S(1)} %get-tuple-element.560), channel_id=1, source_target_pairs={{0,2},{1,3},{2,0},{3,1},{4,6},{5,7},{6,4},{7,5},{8,10},{9,11},{10,... | collective-permute-start | bytes 552968 | tf_op jit(solution)/shard_map/ppermute | solution.py:146
  (88 other events, 776.0 us)
